TPU v7x, 32 devices: a whole 2x2x4 slice. The times are simulated.
32 devices in a mesh: req: 8 (over z, x), tp: 4 (over y, core).
Axes of the slice: x: 2, y: 2, z: 4, core: 2. Of those that a mesh axis runs over, the one named last changes fastest.
Arguments:
- tokens: bfloat16 [8192, 1280], P('req'), may hold values from -14 to 14
- segments: int32 [8192], P('req'), may hold values from 0 to 6, never falling along the last dimension, each value on 1 to 2048 neighbouring positions
- attend_gain: bfloat16 [1280], replicated, may hold values from 0.25 to 1.75
- attend_weight: bfloat16 [1280, 3, 1280], P(None, None, 'tp'), may hold values from -1 to 1
- output_weight: bfloat16 [1280, 1280], P('tp'), may hold values from -0.15625 to 0.15625
- mixer_gain: bfloat16 [1280], replicated, may hold values from 0.25 to 1.75
- expand_weight: bfloat16 [1280, 5120], P(None, 'tp'), may hold values from -0.15625 to 0.15625
- reduce_weight: bfloat16 [5120, 1280], P('tp'), may hold values from -0.078125 to 0.078125
- output_gain: bfloat16 [1280], replicated, may hold values from 0.25 to 1.75
- merge_weight: bfloat16 [5120, 1280], P(None, 'tp'), may hold values from -0.078125 to 0.078125
- merge_index: int32 [2048, 4], P('req'), may hold values from 0 to 8191, as said below
- owners: int32 [2048, 1], P('req'), may hold values from 0 to 7; in each aligned block of 256 rows (0 to 255, 256 to 511, ...) at most 64 rows name the same one
Outputs:
- owned: bfloat16 [8, 8, 64, 1280], P('req', None, None, 'tp')
Inputs may be any that keep to these rules, and one draw needn't show every extreme that they name: segments never fall along the tokens; every image has at most 2048 tokens. `merge_index`: merged rows 256 * j to 256 * (j + 1) - 1 name the tokens 1024 * j to 1024 * (j + 1) - 1, each exactly once. `owners`: within the rows of one index of req each owner is named at most 64 times.
All inputs are finite; a program needn't handle non-finite values.
Results may differ from a plain program's by a relative error of at most 0.014.
Values may be sent and summed in bfloat16 or wider, within the bound.
No kernel may reach another device: no remote copies, remote signals or barrier semaphores. Data moves between devices by JAX's collectives and lax.ppermute only.
A program may use at most 128 MiB of HBM per device.

v0:
```python
import functools
import math

import jax
import jax.numpy as jnp
from jax import lax
from jax.experimental import pallas as pl
from jax.experimental.pallas import tpu as pltpu
from jax.sharding import PartitionSpec as P

HD = 80
TILE = 512
MASKED = -1e30
START = -1e28
FACTOR = 1.0 / math.sqrt(HD)
SEGMENT_ROWS = 16
VROWS = 96
LANES = 256
AHEAD = 2
SMALL = 72.0


def swap(block, axis, flip):
    return lax.ppermute(block, axis, [(i, i ^ flip) for i in range(lax.axis_size(axis))])


def next_pair(i, first, size):
    other = i + 2 if i // 2 % 2 == first else i - 2
    return other if 0 <= other < size else i


def swap_pairs(block, first):
    size = lax.axis_size("req")
    return lax.ppermute(block, "req", [(i, next_pair(i, first, size)) for i in range(size)])


def alone(first):
    size = lax.axis_size("req")
    lonely = [i for i in range(size) if next_pair(i, first, size) == i]
    return sum([(lax.axis_index("req") == i).astype(jnp.int32) for i in lonely], jnp.int32(0))


def normalized(stream, gain):
    center = jnp.mean(stream, axis=-1, keepdims=True)
    moved = stream - center
    spread = jnp.mean(moved * moved, axis=-1, keepdims=True)
    return (moved * lax.rsqrt(spread + 1e-06) * gain).astype(jnp.bfloat16)


def dot(a, b, contract):
    return lax.dot_general(a, b, (contract, ((), ())), preferred_element_type=jnp.float32)


NN = ((1,), (0,))
NT = ((1,), (1,))


def row_of(gain_ref):
    return gain_ref[...].astype(jnp.float32).reshape(1, gain_ref.shape[0])


def vmem(mebibytes=60):
    return pltpu.CompilerParams(vmem_limit_bytes=mebibytes << 20)


def in_hbm(array):
    return pltpu.with_memory_space_constraint(array, pltpu.HBM)


def in_vmem(array):
    return pltpu.with_memory_space_constraint(array, pltpu.VMEM)


SCALARS = pl.BlockSpec(memory_space=pltpu.SMEM)
RESIDENT = pl.BlockSpec(memory_space=pltpu.VMEM)
ANYWHERE = pl.BlockSpec(memory_space=pl.ANY)


def load_mixer_kernel(place, *refs):
    wo_refs, we_refs, wr_refs, refs = refs[:4], refs[4:6], refs[6:8], refs[8:]
    wo, we, wr, sems = refs
    half = wo.shape[0] // 8
    copies = []
    for i in range(8):
        source = wo_refs[i // 2].at[place[0] ^ (i % 2)]
        copies.append((source, wo.at[pl.ds(i * half, half)]))
    copies += [(we_refs[i], we.at[i]) for i in range(2)]
    copies += [(wr_refs[i], wr.at[i]) for i in range(2)]
    copies = [pltpu.make_async_copy(*pair, sems.at[i]) for i, pair in enumerate(copies)]
    for copy in copies:
        copy.start()
    for copy in copies:
        copy.wait()


def load_mixer(place, wo, expand, reduce):
    half, width = wo[0].shape[1:]
    shapes = [(8 * half, width), (2,) + expand[0].shape, (2,) + reduce[0].shape]
    return pl.pallas_call(
        load_mixer_kernel,
        in_specs=[SCALARS] + [ANYWHERE] * 8,
        out_specs=[RESIDENT] * 3,
        out_shape=[pltpu.VMEM(shape, jnp.bfloat16) for shape in shapes],
        scratch_shapes=[pltpu.SemaphoreType.DMA((12,))],
        compiler_params=vmem(4),
        cost_estimate=pl.CostEstimate(flops=0, bytes_accessed=16_000_000, transcendentals=0),
        name="load_mixer",
    )(place, *[in_hbm(w) for w in (*wo, *expand, *reduce)])


def load_merge_kernel(own, other, both, sems):
    columns = own.shape[0]
    copies = [
        pltpu.make_async_copy(source, both.at[pl.ds(i * columns, columns)], sems.at[i])
        for i, source in enumerate((own, other))
    ]
    for copy in copies:
        copy.start()
    for copy in copies:
        copy.wait()


def load_merge(own, other):
    return pl.pallas_call(
        load_merge_kernel,
        in_specs=[ANYWHERE] * 2,
        out_specs=RESIDENT,
        out_shape=pltpu.VMEM((2 * own.shape[0], own.shape[1]), jnp.bfloat16),
        scratch_shapes=[pltpu.SemaphoreType.DMA((2,))],
        compiler_params=vmem(4),
        cost_estimate=pl.CostEstimate(flops=0, bytes_accessed=8_000_000, transcendentals=0),
        name="load_merge",
    )(in_hbm(own), in_hbm(other))


def project_kernel(parts, x_ref, segment_ref, gain_ref, *refs):
    w_refs, keep, send = refs[:parts], refs[parts], refs[parts + 1]
    first = lax.axis_index("req") % 2 == 0
    half = w_refs[0].shape[0] // 2
    rows = normalized(x_ref[...].astype(jnp.float32), row_of(gain_ref))
    for part in range(parts):
        out = dot(w_refs[part][...], rows, NT)
        low, high = out[:half], out[half:]
        at = slice(part * half, (part + 1) * half)
        keep[at, :] = jnp.where(first, low, high).astype(jnp.bfloat16)
        send[at, :] = jnp.where(first, high, low).astype(jnp.bfloat16)
    if parts > 1:
        number = segment_ref[...] + 1
        row = lax.broadcasted_iota(jnp.int32, (SEGMENT_ROWS, 1), 0)
        number = jnp.where(row == 0, number & 255, jnp.where(row == 1, number >> 8, 0))
        number = number.astype(jnp.float32).astype(jnp.bfloat16)
        keep[parts * half :, :] = number
        send[parts * half :, :] = number


def project(tokens, segments, gain, weight, parts, name):
    rows, width = tokens.shape
    half = weight.shape[0] // 6
    step = 256
    tall = len(parts) * half + (SEGMENT_ROWS if len(parts) > 1 else 0)
    return pl.pallas_call(
        functools.partial(project_kernel, len(parts)),
        grid=(rows // step,),
        in_specs=[
            pl.BlockSpec((step, width), lambda i: (i, 0)),
            pl.BlockSpec((1, step), lambda i: (0, i)),
            pl.BlockSpec(gain.shape, lambda i: (0,)),
        ]
        + [pl.BlockSpec((2 * half, width), lambda i, p=p: (p, 0)) for p in parts],
        out_specs=[pl.BlockSpec((tall, step), lambda i: (0, i))] * 2,
        out_shape=[jax.ShapeDtypeStruct((tall, rows), jnp.bfloat16)] * 2,
        compiler_params=vmem(),
        name=name,
    )(tokens, segments, gain, *[weight] * len(parts))


def numbers_of(ref, at):
    two = ref[:, at].astype(jnp.float32)
    return two[0:1] + 256.0 * two[1:2]


def largest_norm(first, second):
    squares = []
    for block in (first, second):
        block = block.astype(jnp.float32)
        squares.append(jnp.sum(block * block, axis=0, keepdims=True))
    return jnp.max(jnp.maximum(squares[0], squares[1]))


def attend_kernel(groups, blocks, flags, resumed, skip, last, place, *refs):
    q_refs, number_refs, refs = refs[:groups], refs[groups : 2 * groups], refs[2 * groups :]
    kv_refs, refs = refs[:blocks], refs[blocks:]
    if resumed:
        acc_in, peak_in, refs = refs[0], refs[1], refs[2:]
    if last:
        ctx_out, refs = refs[:groups], refs[groups:]
    else:
        acc_out, peak_out, refs = refs[0], refs[1], refs[2:]
    keys, values, columns, acc, peak, bounds, plain = refs
    tiles_of = kv_refs[0].shape[1] // TILE
    tiles = blocks * tiles_of
    tall = kv_refs[0].shape[0] - SEGMENT_ROWS
    steps_of = kv_refs[0].shape[1] // TILE
    j = pl.program_id(0)
    fresh = steps_of * groups - resumed

    @pl.when(j == 0)
    def _():
        for b in range(blocks):
            for t in range(tiles_of):
                n = b * tiles_of + t
                at = slice(t * TILE, (t + 1) * TILE)
                for h in range(2):
                    block = kv_refs[b][h * HD : (h + 1) * HD, at].astype(jnp.float32)
                    keys[n, h] = jnp.transpose(block).astype(jnp.bfloat16)
                    values[n, h, :HD] = kv_refs[b][(2 + h) * HD : (3 + h) * HD, at]
                    values[n, h, HD:] = jnp.ones((VROWS - HD, TILE), jnp.bfloat16)
                number = numbers_of(kv_refs[b].at[tall:], at)
                low, high = jnp.min(number), jnp.max(number)
                if b in flags:
                    low = jnp.where(place[flags[b]] == 1, -1.0, low)
                    high = jnp.where(place[flags[b]] == 1, -1.0, high)
                bounds[3 * n] = low
                bounds[3 * n + 1] = high
                bounds[3 * n + 2] = largest_norm(kv_refs[b][:HD, at], kv_refs[b][HD : 2 * HD, at])
                columns[n] = jnp.transpose(jnp.broadcast_to(number, (128, TILE)))

    def go_on():
        acc[...] = acc_in[0]
        peak[...] = peak_in[0]
        plain[0] = (jnp.max(jnp.abs(peak_in[0])) == 0.0).astype(jnp.int32)

    def start():
        acc[...] = jnp.zeros_like(acc)
        peak[...] = jnp.zeros_like(peak)
        plain[0] = 1

    if fresh:
        pl.when(j < fresh)(start)
    if resumed:
        pl.when(j >= fresh)(go_on)

    q_row = numbers_of(number_refs[0], slice(0, TILE))
    queries = q_refs[0][...]
    if groups > 1:
        q_row = jnp.where(j < steps_of, q_row, numbers_of(number_refs[1], slice(0, TILE)))
        queries = jnp.where(j < steps_of, queries, q_refs[1][...])
    q_low, q_high = jnp.min(q_row), jnp.max(q_row)
    q_norm = largest_norm(queries[:HD], queries[HD:])

    def scores_of(t, h, at, matches):
        scores = dot(keys[t, h], queries[h * HD : (h + 1) * HD, at], NN)
        return scores if matches is None else jnp.where(matches, scores, MASKED)

    def matches_of(t, at):
        column = columns[t]
        return jnp.concatenate([column] * (LANES // 128), axis=1) == q_row[:, at]

    units = [(slice(c, c + LANES), h) for c in range(0, TILE, LANES) for h in range(2)]

    def unshifted(t, masked):
        scores, probs, matches = {}, {}, None
        for i in range(len(units) + AHEAD + 1):
            if i < len(units):
                at, h = units[i]
                if masked and h == 0:
                    matches = matches_of(t, at)
                scores[i] = scores_of(t, h, at, matches)
            if 0 <= i - AHEAD < len(units):
                probs[i - AHEAD] = jnp.exp(scores.pop(i - AHEAD) * FACTOR).astype(jnp.bfloat16)
            if 0 <= i - AHEAD - 1 < len(units):
                at, h = units[i - AHEAD - 1]
                acc[h, :, at] += dot(values[t, h], probs.pop(i - AHEAD - 1), NN)

    def shifted_by_peak(t):
        for at, h in units:
            scores = scores_of(t, h, at, matches_of(t, at))
            old = jnp.where(acc[h, HD : HD + 1, at] > 0.0, peak[h : h + 1, at], START)
            new = jnp.maximum(old, jnp.max(scores, axis=0, keepdims=True))
            probs = jnp.exp((scores - new) * FACTOR).astype(jnp.bfloat16)
            shrink = jnp.exp((old - new) * FACTOR)
            peak[h : h + 1, at] = new
            acc[h, :, at] = acc[h, :, at] * shrink + dot(values[t, h], probs, NN)
        plain[0] = 0

    def visit(t, carry):
        k_low, k_high = bounds[3 * t], bounds[3 * t + 1]
        touches = (k_high >= q_low) & (k_low <= q_high)
        whole = (k_low == k_high) & (q_low == q_high)
        small = (plain[0] == 1) & (q_norm * bounds[3 * t + 2] <= SMALL * SMALL * HD)

        @pl.when(touches & small & whole)
        def _():
            unshifted(t, False)

        @pl.when(touches & small & jnp.logical_not(whole))
        def _():
            unshifted(t, True)

        @pl.when(touches & jnp.logical_not(small))
        def _():
            shifted_by_peak(t)

        return carry

    lax.fori_loop(jnp.where(j >= fresh, skip, 0), tiles, visit, 0)
    if last:

        def finish(out):
            for h in range(2):
                at = slice(h * HD, (h + 1) * HD)
                out[0, at, :] = (acc[h, :HD] / acc[h, HD : HD + 1]).astype(jnp.bfloat16)

        for g in range(groups):
            pl.when(j // steps_of == g)(functools.partial(finish, ctx_out[g]))
    else:
        acc_out[0] = acc[...]
        peak_out[0] = peak[...]


def attend(place, queries, numbers, key_values, name, flags={}, state=None, skip=0, last=False):
    half, rows = queries[0].shape
    groups, blocks = len(queries), len(key_values)
    steps_of = rows // TILE
    steps = groups * steps_of
    tiles = blocks * steps_of
    tall = numbers[0].shape[0] - SEGMENT_ROWS
    resumed = 0 if state is None else state[0].shape[0]
    whole = lambda a: pl.BlockSpec(a.shape, lambda j, s: (0,) * a.ndim)
    acc_shape, peak_shape = (2, VROWS, TILE), (2, TILE)
    q_spec = pl.BlockSpec((half, TILE), lambda j, s: (0, (j % steps_of) ^ s[1]))
    number_spec = pl.BlockSpec(
        (SEGMENT_ROWS, TILE), lambda j, s: (tall // SEGMENT_ROWS, (j % steps_of) ^ s[1])
    )
    in_specs = [q_spec] * groups + [number_spec] * groups + [whole(kv) for kv in key_values]
    operands = [*queries, *numbers, *key_values]
    if state is not None:
        behind = steps - resumed
        in_specs += [
            pl.BlockSpec((1,) + acc_shape, lambda j, s: (jnp.maximum(j - behind, 0), 0, 0, 0)),
            pl.BlockSpec((1,) + peak_shape, lambda j, s: (jnp.maximum(j - behind, 0), 0, 0)),
        ]
        operands += list(state)
    if last:
        out_specs = [
            pl.BlockSpec(
                (1, half, TILE), lambda j, s, g=g: (jnp.clip(j - g * steps_of, 0, steps_of - 1), 0, 0)
            )
            for g in range(groups)
        ]
        out_shape = [jax.ShapeDtypeStruct((steps_of, half, TILE), jnp.bfloat16)] * groups
    else:
        out_specs = [
            pl.BlockSpec((1,) + acc_shape, lambda j, s: (j, 0, 0, 0)),
            pl.BlockSpec((1,) + peak_shape, lambda j, s: (j, 0, 0)),
        ]
        out_shape = [
            jax.ShapeDtypeStruct((steps,) + acc_shape, jnp.float32),
            jax.ShapeDtypeStruct((steps,) + peak_shape, jnp.float32),
        ]
    return pl.pallas_call(
        functools.partial(attend_kernel, groups, blocks, flags, resumed, skip, last),
        grid_spec=pltpu.PrefetchScalarGridSpec(
            num_scalar_prefetch=1,
            grid=(steps,),
            in_specs=in_specs,
            out_specs=out_specs,
            scratch_shapes=[
                pltpu.VMEM((tiles, 2, TILE, HD), jnp.bfloat16),
                pltpu.VMEM((tiles, 2, VROWS, TILE), jnp.bfloat16),
                pltpu.VMEM((tiles, TILE, 128), jnp.float32),
                pltpu.VMEM(acc_shape, jnp.float32),
                pltpu.VMEM(peak_shape, jnp.float32),
                pltpu.SMEM((3 * tiles,), jnp.float32),
                pltpu.SMEM((1,), jnp.int32),
            ],
        ),
        out_shape=out_shape,
        compiler_params=vmem(),
        cost_estimate=pl.CostEstimate(flops=1_000_000, bytes_accessed=1_000_000, transcendentals=0),
        name=name,
    )(place, *operands)


def mixer_kernel(chunk, which, place, *refs):
    sources, refs = refs[:8], refs[8:]
    x_hbm, gain_ref, wo, we, wr, sent, kept, context, hidden, x, sem = refs
    rows = x.shape[0]
    half = sources[0].shape[1]
    width = we.shape[2]
    fetch = pltpu.make_async_copy(
        x_hbm.at[pl.ds(pl.multiple_of(place[2] + chunk * rows, rows), rows)], x, sem
    )
    fetch.start()
    lanes = slice(chunk * rows, (chunk + 1) * rows)
    for i in range(8):
        context[i * half : (i + 1) * half, :] = sources[i][which[i], :, lanes].astype(jnp.float32)
    inputs = jnp.transpose(context[...]).astype(jnp.bfloat16)
    fetch.wait()
    total = x[...].astype(jnp.float32) + dot(inputs, wo[...], NN)
    inputs = normalized(total, row_of(gain_ref))
    for i in range(2):
        inner = dot(inputs, we[i], NN)
        grown = 0.5 * inner * (1.0 + lax.erf(inner * (1.0 / math.sqrt(2.0))))
        hidden[:, i * width : (i + 1) * width] = grown.astype(jnp.bfloat16)
    out = dot(hidden[:, :width], wr[0], NN) + dot(hidden[:, width:], wr[1], NN)
    sent[...] = out.astype(jnp.bfloat16)
    kept[...] = total + out


def mixer(place, pieces, tokens, gain, weights, chunk, chunk_rows):
    width = tokens.shape[1]
    half = pieces[0][0].shape[1]
    hidden = weights[1].shape[2]
    return pl.pallas_call(
        functools.partial(mixer_kernel, chunk, [which for _, which in pieces]),
        in_specs=[SCALARS] + [RESIDENT] * 8 + [ANYWHERE] + [RESIDENT] * 4,
        out_specs=[RESIDENT] * 2,
        out_shape=[
            jax.ShapeDtypeStruct((chunk_rows, width), jnp.bfloat16),
            jax.ShapeDtypeStruct((chunk_rows, width), jnp.float32),
        ],
        scratch_shapes=[
            pltpu.VMEM((8 * half, chunk_rows), jnp.float32),
            pltpu.VMEM((chunk_rows, 2 * hidden), jnp.bfloat16),
            pltpu.VMEM((chunk_rows, width), jnp.bfloat16),
            pltpu.SemaphoreType.DMA,
        ],
        compiler_params=vmem(30),
        cost_estimate=pl.CostEstimate(
            flops=5_000_000_000, bytes_accessed=20_000_000, transcendentals=0
        ),
        name="mixer",
    )(place, *[source for source, _ in pieces], tokens, gain, *[in_vmem(w) for w in weights])


def one_hot_rows(index_ref, k, first, rows):
    column = jnp.transpose(jnp.broadcast_to(index_ref[k : k + 1, :], (128, index_ref.shape[1])))
    lanes = lax.broadcasted_iota(jnp.int32, (1, 128), 1)
    parts = [column == lanes + (first + 128 * n) for n in range(rows // 128)]
    return jnp.concatenate(parts, axis=1).astype(jnp.float32).astype(jnp.bfloat16)


def gather_kernel(place, index_ref, kept, received, gain_ref, merged):
    rows = kept.shape[0]
    final = normalized(kept[...] + received[...].astype(jnp.float32), row_of(gain_ref))
    for k in range(4):
        merged[k] = dot(one_hot_rows(index_ref, k, place[2], rows), final, NN).astype(jnp.bfloat16)


def gather(place, index, kept, received, gain):
    return pl.pallas_call(
        gather_kernel,
        in_specs=[SCALARS] + [RESIDENT] * 4,
        out_specs=RESIDENT,
        out_shape=pltpu.VMEM((4, index.shape[1], kept.shape[1]), jnp.bfloat16),
        compiler_params=vmem(20),
        cost_estimate=pl.CostEstimate(
            flops=1_000_000_000, bytes_accessed=5_000_000, transcendentals=0
        ),
        name="gather",
    )(place, index, kept, received, gain)


def merge_kernel(place, index_ref, kept, received, gain_ref, earlier, weights, own, other, parts):
    rows, width = kept.shape
    columns = own.shape[1]
    final = normalized(kept[...] + received[...].astype(jnp.float32), row_of(gain_ref))
    for k in range(4):
        part = dot(one_hot_rows(index_ref, k, place[3], rows), final, NN)
        part = part + earlier[k].astype(jnp.float32)
        parts[:, k * width : (k + 1) * width] = part.astype(jnp.bfloat16)
    total = dot(parts[...], weights[...], NT)
    own[...] = total[:, :columns]
    other[...] = total[:, columns:]


def merge(place, index, kept, received, gain, earlier, weights):
    merged_rows = index.shape[1]
    columns = weights.shape[0] // 2
    return pl.pallas_call(
        merge_kernel,
        in_specs=[SCALARS] + [RESIDENT] * 6,
        out_specs=[RESIDENT] * 2,
        out_shape=[jax.ShapeDtypeStruct((merged_rows, columns), jnp.float32)] * 2,
        scratch_shapes=[pltpu.VMEM((merged_rows, weights.shape[1]), jnp.bfloat16)],
        compiler_params=vmem(20),
        cost_estimate=pl.CostEstimate(
            flops=3_000_000_000, bytes_accessed=12_000_000, transcendentals=0
        ),
        name="merge",
    )(place, index, kept, received, gain, in_vmem(earlier), in_vmem(weights))


def place_kernel(position, own, received, out):
    feature = (own[...] + received[...]).astype(jnp.bfloat16)
    slots = lax.broadcasted_iota(jnp.int32, (out.shape[0], 1), 0)
    chosen = (slots == position[...]).astype(jnp.float32).astype(jnp.bfloat16)
    out[...] = dot(chosen, feature, NN).astype(jnp.bfloat16)


def body(
    tokens,
    segments,
    attend_gain,
    attend_weight,
    output_weight,
    mixer_gain,
    expand_weight,
    reduce_weight,
    output_gain,
    merge_weight,
    merge_index,
    owners,
):
    rows, width = tokens.shape
    head_width = attend_weight.shape[2]
    half = head_width // 2
    peers = lax.axis_size("req")
    req = lax.axis_index("req")
    par = req % 2
    core = lax.axis_index("tp") % 2

    chunk_rows = 256
    per_core = rows // 2
    place = jnp.stack([par, core, core * per_core, core * per_core + chunk_rows, alone(0), alone(1)])
    tie = lax.optimization_barrier
    with jax.named_scope("weights"):
        wo_own = output_weight.reshape(2, half, width)
        wo_across = swap(wo_own, "tp", 2)
        expand_other = swap(expand_weight, "tp", 1)

    with jax.named_scope("project"):
        weight = jnp.transpose(attend_weight, (1, 2, 0)).reshape(6 * half, width)
        numbers = segments[None, :]
        kv_own, kv_send = project(tokens, numbers, attend_gain, weight, (1, 2), "project_keys")
        kv_own, kv_send, expand_other, late_reduce = tie(
            (kv_own, kv_send, expand_other, reduce_weight)
        )

    with jax.named_scope("exchange_keys"):
        kv_peer = swap(kv_send, "req", 1)
        kv_even = swap_pairs(kv_own, 0)
        kv_odd = swap_pairs(kv_own, 1)
        reduce_other = swap(late_reduce, "tp", 1)
        q_own, q_send = project(tokens, numbers, attend_gain, weight, (0,), "project_queries")
        state = attend(place, [q_own], [kv_own], [kv_own], "attend_own")
        q_send, kv_peer, state, wo_across, reduce_other = tie(
            (q_send, kv_peer, state, wo_across, reduce_other)
        )
        q_peer = swap(q_send, "req", 1)
        kv_even_peer = swap_pairs(kv_peer, 0)
        kv_odd_peer = swap_pairs(kv_peer, 1)

    with jax.named_scope("slots"):
        capacity = 2 * merge_index.shape[0] // peers
        target = owners[:, 0]
        choose = (target[:, None] == jnp.arange(peers, dtype=jnp.int32)[None, :]).astype(jnp.int32)
        slot = jnp.sum((jnp.cumsum(choose, axis=0) - 1) * choose, axis=1)
        position = (target * capacity + slot)[None, :]
        index = jnp.transpose(merge_index) - req * rows

    with jax.named_scope("more_weights"):
        q_peer, kv_even, kv_odd, late_wo, wo_across, position, index = tie(
            (q_peer, kv_even, kv_odd, wo_own, wo_across, position, index)
        )
        wo_core = swap(late_wo, "tp", 1)
        wo_both = swap(wo_across, "tp", 1)

    with jax.named_scope("attention"):
        queries, numbers = [q_peer, q_own], [kv_peer, kv_own]
        near = [kv_own, kv_peer, kv_even, kv_odd]
        skip = rows // TILE
        state = attend(place, queries, numbers, near, "attend_near", {2: 4, 3: 5}, state, skip)
        state, kv_even_peer, kv_odd_peer, wo_core, wo_both = tie(
            (state, kv_even_peer, kv_odd_peer, wo_core, wo_both)
        )
        far = [kv_even_peer, kv_odd_peer]
        for_peer, context = attend(
            place, queries, numbers, far, "attend_far", {0: 4, 1: 5}, state, last=True
        )

    with jax.named_scope("exchange_context"):
        late_wo, context, for_peer = tie((wo_own, context, for_peer))
        from_peer = swap(for_peer, "req", 1)
        weights = load_mixer(
            place,
            [late_wo, wo_core, wo_across, wo_both],
            [expand_weight, expand_other],
            [reduce_weight, reduce_other],
        )
        from_peer, weights = tie((from_peer, weights))
        sides = []
        for source in (context, from_peer):
            across = swap(source, "tp", 2)
            sides.append(
                [(source, 0), (swap(source, "tp", 1), 1), (across, 0), (swap(across, "tp", 1), 1)]
            )
        pieces = [sides[h][t] for t in range(4) for h in range(2)]

    with jax.named_scope("mixer"):
        sent, kept, received = [], [], []
        for chunk in range(2):
            s, k = mixer(place, pieces, tokens, mixer_gain, weights, chunk, chunk_rows)
            sent.append(s)
            kept.append(k)
            received.append(swap(s, "tp", 2))
            if chunk == 0:
                merge_own, _ = tie((jnp.transpose(merge_weight), s))
                merge_other = swap(merge_own, "tp", 1)

    with jax.named_scope("merge"):
        merge_other, position, index, _ = tie((merge_other, position, index, sent[1]))
        weights = load_merge(merge_own, merge_other)
        earlier = gather(place, index, kept[0], received[0], output_gain)
        weights, earlier, last, position = tie((weights, earlier, received[1], position))
        own, other = merge(place, index, kept[1], last, output_gain, earlier, weights)
        other = swap(other, "tp", 1)

    with jax.named_scope("place"):
        columns = own.shape[1]
        outgoing = pl.pallas_call(
            place_kernel,
            in_specs=[RESIDENT] * 3,
            out_specs=RESIDENT,
            out_shape=jax.ShapeDtypeStruct((peers * capacity, columns), jnp.bfloat16),
            compiler_params=vmem(10),
            name="place",
        )(position, in_vmem(own), in_vmem(other))
        outgoing = outgoing.reshape(peers, capacity, columns)
        arrived = lax.all_to_all(outgoing, "req", split_axis=0, concat_axis=0, tiled=True)
    return arrived.reshape(1, peers, capacity, columns)


def solution(mesh):
    placed = (
        P("req", None),
        P("req"),
        P(),
        P(None, None, "tp"),
        P("tp", None),
        P(),
        P(None, "tp"),
        P("tp", None),
        P(),
        P(None, "tp"),
        P("req", None),
        P("req", None),
    )
    return jax.shard_map(
        body, mesh=mesh, in_specs=placed, out_specs=P("req", None, None, "tp"), check_vma=False
    )
```

profile of v0, /device:TPU:0, one launch (start us, length us, event | category | flops | bytes accessed | tf_op | source)
XLA Modules:
  0.0 175.1 jit_solution(16334582676510765115)
XLA Ops:
  0.0 0.5 collective-permute-start
  0.5 6.7 %project_keys.1 = (bf16[336,1024]{1,0:T(8,128)(2,1)}, bf16[336,1024]{1,0:T(8,128)(2,1)}) custom-call(bf16[1024,1280]{1,0:T(8,128)(2,1)} %refs_8_.3, s32[1,1024]{1,0:T(1,128)} %bitcast.36, bf16[1280]{0:T(1024)(128)(2,1)} %gain_ref.5, bf16[960,1280]{1,0:T(8,128)(2,1)} %bitcast.27, bf16[960,1280]{1,0:T(8,128)(2,1)} %bitcast.28), custom_call_target="tpu_custom_call" | custom-call | tf_op jit(solution)/shard_map/project/project_keys/pallas_call | solution.py:161
  7.1 0.0 collective-permute-done.refs_5_
  7.1 0.1 collective-permute-start.3
  7.3 1.5 copy-done.7
  8.8 2.5 %collective-permute-start.2 = (bf16[2,160,1280]{2,1,0:T(8,128)(2,1)S(1)}, bf16[2,160,1280]{2,1,0:T(8,128)(2,1)}, u32[]{:S(2)}, u32[]{:S(2)}) collective-permute-start(bf16[2,160,1280]{2,1,0:T(8,128)(2,1)S(1)} %bitcast.34), channel_id=1, source_target_pairs={{0,2},{1,3},{2,0},{3,1},{4,6},{5,7},{6,4},{7,5},{8,10},{9,11},{10,... | collective-permute-start | bytes 2457608 | tf_op jit(solution)/shard_map/weights/ppermute | solution.py:24
  11.4 1.5 collective-permute-start.1
  12.8 1.6 collective-permute-start.5
  14.4 1.7 collective-permute-start.6
  16.2 5.6 %project_queries.1 = (bf16[160,1024]{1,0:T(8,128)(2,1)}, bf16[160,1024]{1,0:T(8,128)(2,1)}) custom-call(bf16[1024,1280]{1,0:T(8,128)(2,1)} %refs_8_.3, s32[1,1024]{1,0:T(1,128)} %bitcast.37, bf16[1280]{0:T(1024)(128)(2,1)} %gain_ref.5, bf16[960,1280]{1,0:T(8,128)(2,1)} %bitcast.29), custom_call_target="tpu_custom_call" | custom-call | tf_op jit(solution)/shard_map/exchange_keys/project_queries/pallas_call | solution.py:161
  21.8 0.6 reduce-window.6
  22.3 0.2 slice_reduce_fusion
  22.6 0.6 stack.23.place
  23.2 0.1 fusion
  23.3 10.6 %attend_own.1 = (f32[2,2,96,512]{3,2,1,0:T(8,128)}, f32[2,2,512]{2,1,0:T(2,128)}) custom-call(s32[6]{0:T(128)} %stack.23.place, bf16[160,1024]{1,0:T(8,128)(2,1)} %get-tuple-element.66.refs_0_.refs_1_, bf16[336,1024]{1,0:T(8,128)(2,1)} %get-tuple-element.67.refs_1_.refs_2_.refs_3_.refs_4_, bf16[336,1024]{1,0:T(8,128)(2,1)} %get-tuple-element.67.refs_1_.refs_2_.refs_3_.refs_4_), custom_call_target="tpu_custom_call" | custom-call | flops 1000000 | bytes 1000000 | tf_op jit(solution)/shard_map/exchange_keys/attend_own/pallas_call | solution.py:361
  33.9 0.0 collective-permute-done.2.refs_2_
  34.0 0.0 collective-permute-done.1.refs_2_.refs_5_
  34.0 0.6 collective-permute-start.4
  34.6 0.0 collective-permute-done.6.refs_7_
  34.6 0.8 copy-done.12
  35.5 0.9 copy-done.13
  36.3 7.2 %collective-permute-done.4.refs_0_ = bf16[160,1024]{1,0:T(8,128)(2,1)S(1)} collective-permute-done((bf16[160,1024]{1,0:T(8,128)(2,1)}, bf16[160,1024]{1,0:T(8,128)(2,1)S(1)}, u32[]{:S(2)}, u32[]{:S(2)}) %collective-permute-start.4) | collective-permute-done | bytes 327712 | tf_op jit(solution)/shard_map/exchange_keys/ppermute | solution.py:24
  43.5 0.0 collective-permute-start.10
  43.5 0.5 collective-permute-start.9
  44.0 3.1 %collective-permute-start.7 = (bf16[336,1024]{1,0:T(8,128)(2,1)S(1)}, bf16[336,1024]{1,0:T(8,128)(2,1)S(1)}, u32[]{:S(2)}, u32[]{:S(2)}) collective-permute-start(bf16[336,1024]{1,0:T(8,128)(2,1)S(1)} %collective-permute-done.1.refs_2_.refs_5_), channel_id=1, source_target_pairs={{0,8},{4,12},{8,0},{12,4},{16,24},{20,28},{24,16},{28,20},{1,9},{5... | collective-permute-start | bytes 2064392 | tf_op jit(solution)/shard_map/exchange_keys/ppermute | solution.py:34
  47.1 1.5 collective-permute-start.8
  48.7 31.7 %attend_near.1 = (f32[4,2,96,512]{3,2,1,0:T(8,128)}, f32[4,2,512]{2,1,0:T(2,128)}) custom-call(s32[6]{0:T(128)} %stack.23.place, bf16[160,1024]{1,0:T(8,128)(2,1)} %copy-done.8, bf16[160,1024]{1,0:T(8,128)(2,1)} %get-tuple-element.66.refs_0_.refs_1_, bf16[336,1024]{1,0:T(8,128)(2,1)} %copy-done.5, ...), custom_call_target="tpu_custom_call" | custom-call | flops 1000000 | bytes 1000000 | tf_op jit(solution)/shard_map/attention/attend_near/pallas_call | solution.py:361
  80.4 0.0 collective-permute-done.8.refs_5_
  80.4 0.0 collective-permute-done.10.refs_3_
  80.4 0.8 copy-done.11
  81.2 8.3 %attend_far.1 = (bf16[2,160,512]{2,1,0:T(8,128)(2,1)}, bf16[2,160,512]{2,1,0:T(8,128)(2,1)}) custom-call(s32[6]{0:T(128)} %stack.23.place, bf16[160,1024]{1,0:T(8,128)(2,1)} %copy-done.8, bf16[160,1024]{1,0:T(8,128)(2,1)} %get-tuple-element.66.refs_0_.refs_1_, bf16[336,1024]{1,0:T(8,128)(2,1)} %copy-done.5, ...), custom_call_target="tpu_custom_call" | custom-call | flops 1000000 | bytes 1000000 | tf_op jit(solution)/shard_map/attention/attend_far/pallas_call | solution.py:361
  89.6 0.0 copy-start
  89.6 0.0 copy-start.4
  89.6 0.6 collective-permute-start.11
  90.2 0.5 collective-permute-start.14
  90.8 6.4 %load_mixer.1 = (bf16[1280,1280]{1,0:T(8,128)(2,1)S(1)}, bf16[2,1280,1280]{2,1,0:T(8,128)(2,1)S(1)}, bf16[2,1280,1280]{2,1,0:T(8,128)(2,1)S(1)}) custom-call(s32[6]{0:T(128)S(1)} %copy-done.2, bf16[2,160,1280]{2,1,0:T(8,128)(2,1)} %bitcast.33, bf16[2,160,1280]{2,1,0:T(8,128)(2,1)} %collective-permute-done.9.refs_1_, ...), custom_call_target="tpu_custom_call" | custom-call | bytes 16000000 | tf_op jit(solution)/shard_map/exchange_context/load_mixer/pallas_call | solution.py:99
  97.2 2.1 %collective-permute-done.11.refs_1_ = bf16[2,160,512]{2,1,0:T(8,128)(2,1)S(1)} collective-permute-done((bf16[2,160,512]{2,1,0:T(8,128)(2,1)}, bf16[2,160,512]{2,1,0:T(8,128)(2,1)S(1)}, u32[]{:S(2)}, u32[]{:S(2)}) %collective-permute-start.11) | collective-permute-done | bytes 327712 | tf_op jit(solution)/shard_map/exchange_context/ppermute | solution.py:24
  99.3 0.5 collective-permute-start.15
  99.8 0.5 collective-permute-start.13
  100.3 0.0 collective-permute-done.14.refs_4_
  100.3 0.0 collective-permute-start.16
  100.3 7.5 %collective-permute-done.15.refs_5_ = bf16[2,160,512]{2,1,0:T(8,128)(2,1)S(1)} collective-permute-done((bf16[2,160,512]{2,1,0:T(8,128)(2,1)S(1)}, bf16[2,160,512]{2,1,0:T(8,128)(2,1)S(1)}, u32[]{:S(2)}, u32[]{:S(2)}) %collective-permute-start.15) | collective-permute-done | bytes 327712 | tf_op jit(solution)/shard_map/exchange_context/ppermute | solution.py:24
  107.7 0.0 collective-permute-start.17
  107.7 0.0 collective-permute-done.12.refs_2_
  107.7 0.0 collective-permute-done.13.refs_3_
  107.8 0.0 collective-permute-done.16.refs_6_
  107.8 1.6 collective-permute-done.17.refs_7_
  109.4 6.8 %mixer.2 = (bf16[256,1280]{1,0:T(8,128)(2,1)S(1)}, f32[256,1280]{1,0:T(8,128)S(1)}) custom-call(s32[6]{0:T(128)S(1)} %copy-done.2, bf16[2,160,512]{2,1,0:T(8,128)(2,1)S(1)} %copy-done.1, bf16[2,160,512]{2,1,0:T(8,128)(2,1)S(1)} %collective-permute-done.11.refs_1_, bf16[2,160,512]{2,1,0:T(8,128)(2,1)S(1)} %collective-permute-done.12.refs_2_, ...), custom_call_target="tpu_custom_call" | custom-call | flops 5000000000 | bytes 20000000 | tf_op jit(solution)/shard_map/mixer/mixer/pallas_call | solution.py:415
  116.2 0.2 collective-permute-start.18
  116.4 0.5 collective-permute-start.19
  116.9 6.6 %mixer.3 = (bf16[256,1280]{1,0:T(8,128)(2,1)S(1)}, f32[256,1280]{1,0:T(8,128)S(1)}) custom-call(s32[6]{0:T(128)S(1)} %copy-done.2, bf16[2,160,512]{2,1,0:T(8,128)(2,1)S(1)} %copy-done.1, bf16[2,160,512]{2,1,0:T(8,128)(2,1)S(1)} %collective-permute-done.11.refs_1_, bf16[2,160,512]{2,1,0:T(8,128)(2,1)S(1)} %collective-permute-done.12.refs_2_, ...), custom_call_target="tpu_custom_call" | custom-call | flops 5000000000 | bytes 20000000 | tf_op jit(solution)/shard_map/mixer/mixer/pallas_call | solution.py:415
  123.6 0.0 copy-start.3
  123.6 1.6 collective-permute-start.20
  125.2 0.0 collective-permute-done.18.other
  125.2 2.9 %load_merge.1.weights = bf16[640,5120]{1,0:T(8,128)(2,1)S(1)} custom-call(bf16[320,5120]{1,0:T(8,128)(2,1)} %bitcast.30, bf16[320,5120]{1,0:T(8,128)(2,1)} %collective-permute-done.18.other), custom_call_target="tpu_custom_call" | custom-call | bytes 8000000 | tf_op jit(solution)/shard_map/merge/load_merge/pallas_call | solution.py:124
  128.1 5.9 %collective-permute-done.19.received = bf16[256,1280]{1,0:T(8,128)(2,1)S(1)} collective-permute-done((bf16[256,1280]{1,0:T(8,128)(2,1)S(1)}, bf16[256,1280]{1,0:T(8,128)(2,1)S(1)}, u32[]{:S(2)}, u32[]{:S(2)}) %collective-permute-start.19) | collective-permute-done | bytes 655392 | tf_op jit(solution)/shard_map/mixer/ppermute | solution.py:24
  134.0 1.8 %gather.1.earlier = bf16[4,256,1280]{2,1,0:T(8,128)(2,1)S(1)} custom-call(s32[6]{0:T(128)S(1)} %copy-done.2, s32[4,256]{1,0:T(4,128)S(1)} %subtract_bitcast_fusion.index_ref, f32[256,1280]{1,0:T(8,128)S(1)} %get-tuple-element.110.kept, bf16[256,1280]{1,0:T(8,128)(2,1)S(1)} %collective-permute-done.19.received, bf16[1280]{0:T(1024)(128)(2,1)S(1)} %copy-done.3), custom_call_target="tpu_custom_call" | custom-call | flops 1000000000 | bytes 5000000 | tf_op jit(solution)/shard_map/merge/gather/pallas_call | solution.py:452
  135.8 11.7 %collective-permute-done.20.received = bf16[256,1280]{1,0:T(8,128)(2,1)S(1)} collective-permute-done((bf16[256,1280]{1,0:T(8,128)(2,1)S(1)}, bf16[256,1280]{1,0:T(8,128)(2,1)S(1)}, u32[]{:S(2)}, u32[]{:S(2)}) %collective-permute-start.20) | collective-permute-done | bytes 655392 | tf_op jit(solution)/shard_map/mixer/ppermute | solution.py:24
  147.5 4.0 %merge.1 = (f32[256,320]{1,0:T(8,128)S(1)}, f32[256,320]{1,0:T(8,128)S(1)}) custom-call(s32[6]{0:T(128)S(1)} %copy-done.2, s32[4,256]{1,0:T(4,128)S(1)} %subtract_bitcast_fusion.index_ref, f32[256,1280]{1,0:T(8,128)S(1)} %get-tuple-element.113.kept, bf16[256,1280]{1,0:T(8,128)(2,1)S(1)} %collective-permute-done.20.received, bf16[1280]{0:T(1024)(128)(2,1)S(1)} %copy-done.3, ...), custom_call_target="tpu_custom_call" | custom-call | flops 3000000000 | bytes 12000000 | tf_op jit(solution)/shard_map/merge/merge/pallas_call | solution.py:481
  151.5 0.1 collective-permute-start.21
  151.6 1.7 collective-permute-done.21.received
  153.3 0.3 place.1
  153.6 20.7 %all_to_all.5 = bf16[8,64,320]{2,1,0:T(8,128)(2,1)S(1)} all-to-all(bf16[8,64,320]{2,1,0:T(8,128)(2,1)S(1)} %bitcast.26), channel_id=1, replica_groups=mesh['req'=8,'tp'=4] {'req'}, dimensions={0} | all-to-all | bytes 655360 | tf_op jit(solution)/shard_map/place/all_to_all | solution.py:631
  174.3 0.7 copy.14
  (35 shorter events, 0.1 us)
Async XLA Ops:
  0.0 7.1 %collective-permute-start = (bf16[1280,1280]{1,0:T(8,128)(2,1)}, bf16[1280,1280]{1,0:T(8,128)(2,1)S(1)}, u32[]{:S(2)}, u32[]{:S(2)}) collective-permute-start(bf16[1280,1280]{1,0:T(8,128)(2,1)} %refs_4_.1), channel_id=1, source_target_pairs={{0,1},{1,0},{2,3},{3,2},{4,5},{5,4},{6,7},{7,6},{8,9},{9,8},{10,11... | collective-permute-start | bytes 9830408 | tf_op jit(solution)/shard_map/weights/ppermute | solution.py:24
  0.5 8.4 %copy-start.9 = (bf16[320,1280]{1,0:T(8,128)(2,1)S(1)}, bf16[320,1280]{1,0:T(8,128)(2,1)}, u32[]{:S(2)}) copy-start(bf16[320,1280]{1,0:T(8,128)(2,1)} %param.16) | copy-start | bytes 2457604
  0.5 15.7 %copy-start.14 = (s32[256,1]{0,1:T(1,128)S(1)}, s32[256,1]{0,1:T(1,128)}, u32[]{:S(2)}) copy-start(s32[256,1]{0,1:T(1,128)} %param.23) | copy-start | bytes 3076
  7.1 1.7 copy-start.7
  7.1 26.8 %collective-permute-start.3 = (bf16[1280,1280]{1,0:T(8,128)(2,1)}, bf16[1280,1280]{1,0:T(8,128)(2,1)}, u32[]{:S(2)}, u32[]{:S(2)}) collective-permute-start(bf16[1280,1280]{1,0:T(8,128)(2,1)} %refs_6_.1), channel_id=1, source_target_pairs={{0,1},{1,0},{2,3},{3,2},{4,5},{5,4},{6,7},{7,6},{8,9},{9,8},{10,11... | collective-permute-start | bytes 9830408 | tf_op jit(solution)/shard_map/exchange_keys/ppermute | solution.py:24
  8.8 25.1 %collective-permute-start.2 = (bf16[2,160,1280]{2,1,0:T(8,128)(2,1)S(1)}, bf16[2,160,1280]{2,1,0:T(8,128)(2,1)}, u32[]{:S(2)}, u32[]{:S(2)}) collective-permute-start(bf16[2,160,1280]{2,1,0:T(8,128)(2,1)S(1)} %bitcast.34), channel_id=1, source_target_pairs={{0,2},{1,3},{2,0},{3,1},{4,6},{5,7},{6,4},{7,5},{8,10},{9,11},{10,... | collective-permute-start | bytes 2457608 | tf_op jit(solution)/shard_map/weights/ppermute | solution.py:24
  11.4 22.6 %collective-permute-start.1 = (bf16[336,1024]{1,0:T(8,128)(2,1)}, bf16[336,1024]{1,0:T(8,128)(2,1)S(1)}, u32[]{:S(2)}, u32[]{:S(2)}) collective-permute-start(bf16[336,1024]{1,0:T(8,128)(2,1)} %get-tuple-element.65), channel_id=1, source_target_pairs={{0,4},{4,0},{8,12},{12,8},{16,20},{20,16},{24,28},{28,24},{1,5},{5... | collective-permute-start | bytes 2064392 | tf_op jit(solution)/shard_map/exchange_keys/ppermute | solution.py:24
  12.8 21.7 %collective-permute-start.5 = (bf16[336,1024]{1,0:T(8,128)(2,1)}, bf16[336,1024]{1,0:T(8,128)(2,1)S(1)}, u32[]{:S(2)}, u32[]{:S(2)}) collective-permute-start(bf16[336,1024]{1,0:T(8,128)(2,1)} %get-tuple-element.67.refs_1_.refs_2_.refs_3_.refs_4_), channel_id=1, source_target_pairs={{0,8},{4,12},{8,0},{12,4},{16,24},{20,28},{24,16},{28,20},{1,9},{5... | collective-permute-start | bytes 2064392 | tf_op jit(solution)/shard_map/exchange_keys/ppermute | solution.py:34
  14.4 20.2 %collective-permute-start.6 = (bf16[336,1024]{1,0:T(8,128)(2,1)}, bf16[336,1024]{1,0:T(8,128)(2,1)S(1)}, u32[]{:S(2)}, u32[]{:S(2)}) collective-permute-start(bf16[336,1024]{1,0:T(8,128)(2,1)} %get-tuple-element.67.refs_1_.refs_2_.refs_3_.refs_4_), channel_id=1, source_target_pairs={{0,0},{4,4},{8,16},{12,20},{16,8},{20,12},{24,24},{28,28},{1,1},{5... | collective-permute-start | bytes 2064392 | tf_op jit(solution)/shard_map/exchange_keys/ppermute | solution.py:34
  16.2 18.4 %copy-start.15 = (s32[256,4]{0,1:T(4,128)S(1)}, s32[256,4]{0,1:T(4,128)}, u32[]{:S(2)}) copy-start(s32[256,4]{0,1:T(4,128)} %param.22) | copy-start | bytes 12292
  34.0 14.7 %copy-start.5 = (bf16[336,1024]{1,0:T(8,128)(2,1)}, bf16[336,1024]{1,0:T(8,128)(2,1)S(1)}, u32[]{:S(2)}) copy-start(bf16[336,1024]{1,0:T(8,128)(2,1)S(1)} %collective-permute-done.1.refs_2_.refs_5_) | copy-start | bytes 2064388
  34.0 9.5 %collective-permute-start.4 = (bf16[160,1024]{1,0:T(8,128)(2,1)}, bf16[160,1024]{1,0:T(8,128)(2,1)S(1)}, u32[]{:S(2)}, u32[]{:S(2)}) collective-permute-start(bf16[160,1024]{1,0:T(8,128)(2,1)} %get-tuple-element.71), channel_id=1, source_target_pairs={{0,4},{4,0},{8,12},{12,8},{16,20},{20,16},{24,28},{28,24},{1,5},{5... | collective-permute-start | bytes 983048 | tf_op jit(solution)/shard_map/exchange_keys/ppermute | solution.py:24
  34.6 0.9 copy-start.12
  35.5 0.9 copy-start.13
  43.5 5.1 %copy-start.8 = (bf16[160,1024]{1,0:T(8,128)(2,1)}, bf16[160,1024]{1,0:T(8,128)(2,1)S(1)}, u32[]{:S(2)}) copy-start(bf16[160,1024]{1,0:T(8,128)(2,1)S(1)} %collective-permute-done.4.refs_0_) | copy-start | bytes 983044
  43.5 36.9 %collective-permute-start.10 = (bf16[2,160,1280]{2,1,0:T(8,128)(2,1)}, bf16[2,160,1280]{2,1,0:T(8,128)(2,1)S(1)}, u32[]{:S(2)}, u32[]{:S(2)}) collective-permute-start(bf16[2,160,1280]{2,1,0:T(8,128)(2,1)} %collective-permute-done.2.refs_2_), channel_id=1, source_target_pairs={{0,1},{1,0},{2,3},{3,2},{4,5},{5,4},{6,7},{7,6},{8,9},{9,8},{10,11... | collective-permute-start | bytes 2457608 | tf_op jit(solution)/shard_map/more_weights/ppermute | solution.py:24
  43.5 36.9 %collective-permute-start.9 = (bf16[2,160,1280]{2,1,0:T(8,128)(2,1)S(1)}, bf16[2,160,1280]{2,1,0:T(8,128)(2,1)}, u32[]{:S(2)}, u32[]{:S(2)}) collective-permute-start(bf16[2,160,1280]{2,1,0:T(8,128)(2,1)S(1)} %bitcast.35), channel_id=1, source_target_pairs={{0,1},{1,0},{2,3},{3,2},{4,5},{5,4},{6,7},{7,6},{8,9},{9,8},{10,11... | collective-permute-start | bytes 2457608 | tf_op jit(solution)/shard_map/more_weights/ppermute | solution.py:24
  44.0 36.3 %collective-permute-start.7 = (bf16[336,1024]{1,0:T(8,128)(2,1)S(1)}, bf16[336,1024]{1,0:T(8,128)(2,1)S(1)}, u32[]{:S(2)}, u32[]{:S(2)}) collective-permute-start(bf16[336,1024]{1,0:T(8,128)(2,1)S(1)} %collective-permute-done.1.refs_2_.refs_5_), channel_id=1, source_target_pairs={{0,8},{4,12},{8,0},{12,4},{16,24},{20,28},{24,16},{28,20},{1,9},{5... | collective-permute-start | bytes 2064392 | tf_op jit(solution)/shard_map/exchange_keys/ppermute | solution.py:34
  47.1 33.3 %collective-permute-start.8 = (bf16[336,1024]{1,0:T(8,128)(2,1)S(1)}, bf16[336,1024]{1,0:T(8,128)(2,1)}, u32[]{:S(2)}, u32[]{:S(2)}) collective-permute-start(bf16[336,1024]{1,0:T(8,128)(2,1)S(1)} %collective-permute-done.1.refs_2_.refs_5_), channel_id=1, source_target_pairs={{0,0},{4,4},{8,16},{12,20},{16,8},{20,12},{24,24},{28,28},{1,1},{5... | collective-permute-start | bytes 2064392 | tf_op jit(solution)/shard_map/exchange_keys/ppermute | solution.py:34
  80.4 10.4 %copy-start.2 = (s32[6]{0:T(128)S(1)}, s32[6]{0:T(128)}, u32[]{:S(2)}) copy-start(s32[6]{0:T(128)} %stack.23.place) | copy-start | bytes 76
  80.4 0.9 copy-start.11
  80.4 10.3 %copy-start.10 = (bf16[2,160,1280]{2,1,0:T(8,128)(2,1)}, bf16[2,160,1280]{2,1,0:T(8,128)(2,1)S(1)}, u32[]{:S(2)}) copy-start(bf16[2,160,1280]{2,1,0:T(8,128)(2,1)S(1)} %collective-permute-done.10.refs_3_) | copy-start | bytes 2457604
  89.6 10.2 %copy-start.1 = (bf16[2,160,512]{2,1,0:T(8,128)(2,1)S(1)}, bf16[2,160,512]{2,1,0:T(8,128)(2,1)}, u32[]{:S(2)}) copy-start(bf16[2,160,512]{2,1,0:T(8,128)(2,1)} %get-tuple-element.89.refs_0_) | copy-start | bytes 983044
  89.6 19.8 %copy-start = (bf16[1024,1280]{1,0:T(8,128)(2,1)S(1)}, bf16[1024,1280]{1,0:T(8,128)(2,1)}, u32[]{:S(2)}) copy-start(bf16[1024,1280]{1,0:T(8,128)(2,1)} %refs_8_.3) | copy-start | bytes 7864324
  89.6 19.8 %copy-start.4 = (bf16[1280]{0:T(1024)(128)(2,1)S(1)}, bf16[1280]{0:T(1024)(128)(2,1)}, u32[]{:S(2)}) copy-start(bf16[1280]{0:T(1024)(128)(2,1)} %refs_9_.3) | copy-start | bytes 7684
  89.6 9.6 %collective-permute-start.11 = (bf16[2,160,512]{2,1,0:T(8,128)(2,1)}, bf16[2,160,512]{2,1,0:T(8,128)(2,1)S(1)}, u32[]{:S(2)}, u32[]{:S(2)}) collective-permute-start(bf16[2,160,512]{2,1,0:T(8,128)(2,1)} %get-tuple-element.90), channel_id=1, source_target_pairs={{0,4},{4,0},{8,12},{12,8},{16,20},{20,16},{24,28},{28,24},{1,5},{5... | collective-permute-start | bytes 983048 | tf_op jit(solution)/shard_map/exchange_context/ppermute | solution.py:24
  90.2 10.0 %collective-permute-start.14 = (bf16[2,160,512]{2,1,0:T(8,128)(2,1)}, bf16[2,160,512]{2,1,0:T(8,128)(2,1)S(1)}, u32[]{:S(2)}, u32[]{:S(2)}) collective-permute-start(bf16[2,160,512]{2,1,0:T(8,128)(2,1)} %get-tuple-element.89.refs_0_), channel_id=1, source_target_pairs={{0,2},{1,3},{2,0},{3,1},{4,6},{5,7},{6,4},{7,5},{8,10},{9,11},{10,... | collective-permute-start | bytes 983048 | tf_op jit(solution)/shard_map/exchange_context/ppermute | solution.py:24
  99.3 17.0 %copy-start.6 = (bf16[5120,320]{0,1:T(8,128)(2,1)S(1)}, bf16[5120,320]{0,1:T(8,128)(2,1)}, u32[]{:S(2)}) copy-start(bf16[5120,320]{0,1:T(8,128)(2,1)} %param.21) | copy-start | bytes 9830404
  99.3 8.5 %collective-permute-start.15 = (bf16[2,160,512]{2,1,0:T(8,128)(2,1)S(1)}, bf16[2,160,512]{2,1,0:T(8,128)(2,1)S(1)}, u32[]{:S(2)}, u32[]{:S(2)}) collective-permute-start(bf16[2,160,512]{2,1,0:T(8,128)(2,1)S(1)} %collective-permute-done.11.refs_1_), channel_id=1, source_target_pairs={{0,2},{1,3},{2,0},{3,1},{4,6},{5,7},{6,4},{7,5},{8,10},{9,11},{10,... | collective-permute-start | bytes 983048 | tf_op jit(solution)/shard_map/exchange_context/ppermute | solution.py:24
  99.8 8.0 %collective-permute-start.12 = (bf16[2,160,512]{2,1,0:T(8,128)(2,1)S(1)}, bf16[2,160,512]{2,1,0:T(8,128)(2,1)S(1)}, u32[]{:S(2)}, u32[]{:S(2)}) collective-permute-start(bf16[2,160,512]{2,1,0:T(8,128)(2,1)S(1)} %copy-done.1), channel_id=1, source_target_pairs={{0,1},{1,0},{2,3},{3,2},{4,5},{5,4},{6,7},{7,6},{8,9},{9,8},{10,11... | collective-permute-start | bytes 983048 | tf_op jit(solution)/shard_map/exchange_context/ppermute | solution.py:24
  99.8 8.0 %collective-permute-start.13 = (bf16[2,160,512]{2,1,0:T(8,128)(2,1)S(1)}, bf16[2,160,512]{2,1,0:T(8,128)(2,1)S(1)}, u32[]{:S(2)}, u32[]{:S(2)}) collective-permute-start(bf16[2,160,512]{2,1,0:T(8,128)(2,1)S(1)} %collective-permute-done.11.refs_1_), channel_id=1, source_target_pairs={{0,1},{1,0},{2,3},{3,2},{4,5},{5,4},{6,7},{7,6},{8,9},{9,8},{10,11... | collective-permute-start | bytes 983048 | tf_op jit(solution)/shard_map/exchange_context/ppermute | solution.py:24
  100.3 7.5 %collective-permute-start.16 = (bf16[2,160,512]{2,1,0:T(8,128)(2,1)S(1)}, bf16[2,160,512]{2,1,0:T(8,128)(2,1)S(1)}, u32[]{:S(2)}, u32[]{:S(2)}) collective-permute-start(bf16[2,160,512]{2,1,0:T(8,128)(2,1)S(1)} %collective-permute-done.14.refs_4_), channel_id=1, source_target_pairs={{0,1},{1,0},{2,3},{3,2},{4,5},{5,4},{6,7},{7,6},{8,9},{9,8},{10,11... | collective-permute-start | bytes 983048 | tf_op jit(solution)/shard_map/exchange_context/ppermute | solution.py:24
  107.7 1.6 collective-permute-start.17
  116.2 8.9 %collective-permute-start.18 = (bf16[320,5120]{1,0:T(8,128)(2,1)S(1)}, bf16[320,5120]{1,0:T(8,128)(2,1)}, u32[]{:S(2)}, u32[]{:S(2)}) collective-permute-start(bf16[320,5120]{1,0:T(8,128)(2,1)S(1)} %bitcast.31), channel_id=1, source_target_pairs={{0,1},{1,0},{2,3},{3,2},{4,5},{5,4},{6,7},{7,6},{8,9},{9,8},{10,11... | collective-permute-start | bytes 9830408 | tf_op jit(solution)/shard_map/mixer/ppermute | solution.py:24
  116.4 17.6 %collective-permute-start.19 = (bf16[256,1280]{1,0:T(8,128)(2,1)S(1)}, bf16[256,1280]{1,0:T(8,128)(2,1)S(1)}, u32[]{:S(2)}, u32[]{:S(2)}) collective-permute-start(bf16[256,1280]{1,0:T(8,128)(2,1)S(1)} %get-tuple-element.103), channel_id=1, source_target_pairs={{0,2},{1,3},{2,0},{3,1},{4,6},{5,7},{6,4},{7,5},{8,10},{9,11},{10,... | collective-permute-start | bytes 1966088 | tf_op jit(solution)/shard_map/mixer/ppermute | solution.py:24
  123.6 10.4 %copy-start.3 = (bf16[1280]{0:T(1024)(128)(2,1)S(1)}, bf16[1280]{0:T(1024)(128)(2,1)}, u32[]{:S(2)}) copy-start(bf16[1280]{0:T(1024)(128)(2,1)} %gain_ref.7) | copy-start | bytes 7684
  123.6 23.9 %collective-permute-start.20 = (bf16[256,1280]{1,0:T(8,128)(2,1)S(1)}, bf16[256,1280]{1,0:T(8,128)(2,1)S(1)}, u32[]{:S(2)}, u32[]{:S(2)}) collective-permute-start(bf16[256,1280]{1,0:T(8,128)(2,1)S(1)} %get-tuple-element.107), channel_id=1, source_target_pairs={{0,2},{1,3},{2,0},{3,1},{4,6},{5,7},{6,4},{7,5},{8,10},{9,11},{10,... | collective-permute-start | bytes 1966088 | tf_op jit(solution)/shard_map/mixer/ppermute | solution.py:24
  151.5 1.8 %collective-permute-start.21 = (f32[256,320]{1,0:T(8,128)S(1)}, f32[256,320]{1,0:T(8,128)S(1)}, u32[]{:S(2)}, u32[]{:S(2)}) collective-permute-start(f32[256,320]{1,0:T(8,128)S(1)} %get-tuple-element.118), channel_id=1, source_target_pairs={{0,1},{1,0},{2,3},{3,2},{4,5},{5,4},{6,7},{7,6},{8,9},{9,8},{10,11... | collective-permute-start | bytes 983048 | tf_op jit(solution)/shard_map/merge/ppermute | solution.py:24
where the time goes:
time: 172 us; the launch traced here: 175 us
  Pallas kernels  91.8 us (53%)
  waiting for transfers between devices  37.7 us (22%)
  blocking collectives  20.7 us (12%)
  starting transfers between devices  18.2 us (11%)
  local copies, waits for them, and re-layouts  5.71 us (3%)
    pallas_call x3, Pallas kernels, attend(): pl.pallas_call(functools.partial(attend_kernel, groups, blocks, flags, re...  50.7 us
    ppermute x18, waiting for transfers between devices, swap(): lax.ppermute(block, axis, [(i, i ^ flip) for i in range(lax.axis_size(axi...  37.7 us
    all_to_all x1, blocking collectives, body(): lax.all_to_all(outgoing, 'req', split_axis=0, concat_axis=0, tiled=True)  20.7 us
    pallas_call x2, Pallas kernels, mixer(): pl.pallas_call(functools.partial(mixer_kernel, chunk, [which for _, which...  13.4 us
    pallas_call x2, Pallas kernels, project(): pl.pallas_call(functools.partial(project_kernel, len(parts)), grid=(rows...  12.3 us
    ppermute x18, starting transfers between devices, swap(): lax.ppermute(block, axis, [(i, i ^ flip) for i in range(lax.axis_size(axi...  10.2 us
    ppermute x4, starting transfers between devices, swap_pairs(): lax.ppermute(block, 'req', [(i, next_pair(i, first, size)) for i in range...  7.92 us
    pallas_call x1, Pallas kernels, load_mixer(): pl.pallas_call(load_mixer_kernel, in_specs=[SCALARS] + [ANYWHERE] * 8, ou...  6.4 us
  transfers between devices with their start and end apart: 22, of which 7 were waited for; matrix products, arithmetic and copies ran while one was open for 1% of the time, Pallas kernels for 41%

commit v1 on v0

--- a/solution.py
+++ b/solution.py
@@ -30,8 +30,13 @@
 
 
 def swap_pairs(block, first):
-    size = lax.axis_size("req")
-    return lax.ppermute(block, "req", [(i, next_pair(i, first, size)) for i in range(size)])
+    size, width = lax.axis_size("req"), lax.axis_size("tp")
+    route = []
+    for i in range(size):
+        other = next_pair(i, first, size)
+        for t in range(width):
+            route.append((i * width + t, other * width + (t if other != i else t ^ 1)))
+    return lax.ppermute(block, ("req", "tp"), route)
 
 
 def alone(first):
@@ -168,7 +173,7 @@
         ]
         + [pl.BlockSpec((2 * half, width), lambda i, p=p: (p, 0)) for p in parts],
         out_specs=[pl.BlockSpec((tall, step), lambda i: (0, i))] * 2,
-        out_shape=[jax.ShapeDtypeStruct((tall, rows), jnp.bfloat16)] * 2,
+        out_shape=[pltpu.HBM((tall, rows), jnp.bfloat16)] * 2,
         compiler_params=vmem(),
         name=name,
     )(tokens, segments, gain, *[weight] * len(parts))
@@ -527,30 +532,30 @@
     tie = lax.optimization_barrier
     with jax.named_scope("weights"):
         wo_own = output_weight.reshape(2, half, width)
-        wo_across = swap(wo_own, "tp", 2)
+        wo_core = swap(wo_own, "tp", 1)
         expand_other = swap(expand_weight, "tp", 1)
 
     with jax.named_scope("project"):
         weight = jnp.transpose(attend_weight, (1, 2, 0)).reshape(6 * half, width)
         numbers = segments[None, :]
         kv_own, kv_send = project(tokens, numbers, attend_gain, weight, (1, 2), "project_keys")
-        kv_own, kv_send, expand_other, late_reduce = tie(
-            (kv_own, kv_send, expand_other, reduce_weight)
-        )
+        kv_own, kv_send, expand_other, wo_core = tie((kv_own, kv_send, expand_other, wo_core))
 
     with jax.named_scope("exchange_keys"):
         kv_peer = swap(kv_send, "req", 1)
         kv_even = swap_pairs(kv_own, 0)
         kv_odd = swap_pairs(kv_own, 1)
-        reduce_other = swap(late_reduce, "tp", 1)
+        wo_across = swap(wo_own, "tp", 2)
         q_own, q_send = project(tokens, numbers, attend_gain, weight, (0,), "project_queries")
+        q_peer = swap(q_send, "req", 1)
         state = attend(place, [q_own], [kv_own], [kv_own], "attend_own")
-        q_send, kv_peer, state, wo_across, reduce_other = tie(
-            (q_send, kv_peer, state, wo_across, reduce_other)
+        kv_odd, kv_even, kv_peer, state, wo_across, late_reduce, late_wo = tie(
+            (kv_odd, kv_even, kv_peer, state, wo_across, reduce_weight, wo_core)
         )
-        q_peer = swap(q_send, "req", 1)
         kv_even_peer = swap_pairs(kv_peer, 0)
         kv_odd_peer = swap_pairs(kv_peer, 1)
+        reduce_other = swap(late_reduce, "tp", 1)
+        wo_both = swap(late_wo, "tp", 2)
 
     with jax.named_scope("slots"):
         capacity = 2 * merge_index.shape[0] // peers
@@ -560,20 +565,14 @@
         position = (target * capacity + slot)[None, :]
         index = jnp.transpose(merge_index) - req * rows
 
-    with jax.named_scope("more_weights"):
-        q_peer, kv_even, kv_odd, late_wo, wo_across, position, index = tie(
-            (q_peer, kv_even, kv_odd, wo_own, wo_across, position, index)
-        )
-        wo_core = swap(late_wo, "tp", 1)
-        wo_both = swap(wo_across, "tp", 1)
+        q_peer, position, index = tie((q_peer, position, index))
 
     with jax.named_scope("attention"):
         queries, numbers = [q_peer, q_own], [kv_peer, kv_own]
         near = [kv_own, kv_peer, kv_even, kv_odd]
-        skip = rows // TILE
-        state = attend(place, queries, numbers, near, "attend_near", {2: 4, 3: 5}, state, skip)
-        state, kv_even_peer, kv_odd_peer, wo_core, wo_both = tie(
-            (state, kv_even_peer, kv_odd_peer, wo_core, wo_both)
+        state = attend(place, queries, numbers, near, "attend_near", {2: 4, 3: 5}, state, rows // TILE)
+        state, kv_even_peer, kv_odd_peer, reduce_other, wo_both = tie(
+            (state, kv_even_peer, kv_odd_peer, reduce_other, wo_both)
         )
         far = [kv_even_peer, kv_odd_peer]
         for_peer, context = attend(

time: 172 us -> 169 us (0.983); the launches traced: 175 us -> 168 us
  starting transfers between devices: 18.2 us -> 12.5 us
    ppermute x4, starting transfers between devices: 7.92 us -> 2.1 us  [swap_pairs(): return lax.ppermute(block, ('req', 'tp'), route)]
    unnamed x33 -> x29, local copies, waits for them, and re-layouts: 4.89 us -> 3.95 us
  transfers between devices with their start and end apart: 22 -> 22, of which waited for: 7 -> 7; matrix products, arithmetic and copies ran while one was open for 1% -> 1% of each run, Pallas kernels for 41% -> 43%
where the time goes in v1:
time: 169 us; the launch traced here: 168 us
  Pallas kernels  91.6 us (54%)
  waiting for transfers between devices  38.4 us (23%)
  blocking collectives  19.2 us (11%)
  starting transfers between devices  12.5 us (7%)
  local copies, waits for them, and re-layouts  4.84 us (3%)
    pallas_call x3, Pallas kernels, attend(): pl.pallas_call(functools.partial(attend_kernel, groups, blocks, flags, re...  50.9 us
    ppermute x18, waiting for transfers between devices, swap(): lax.ppermute(block, axis, [(i, i ^ flip) for i in range(lax.axis_size(axi...  38.4 us
    all_to_all x1, blocking collectives, body(): lax.all_to_all(outgoing, 'req', split_axis=0, concat_axis=0, tiled=True)  19.2 us
    pallas_call x2, Pallas kernels, mixer(): pl.pallas_call(functools.partial(mixer_kernel, chunk, [which for _, which...  13.1 us
    pallas_call x2, Pallas kernels, project(): pl.pallas_call(functools.partial(project_kernel, len(parts)), grid=(rows...  12.2 us
    ppermute x18, starting transfers between devices, swap(): lax.ppermute(block, axis, [(i, i ^ flip) for i in range(lax.axis_size(axi...  10.4 us
    pallas_call x1, Pallas kernels, load_mixer(): pl.pallas_call(load_mixer_kernel, in_specs=[SCALARS] + [ANYWHERE] * 8, ou...  6.4 us
    pallas_call x1, Pallas kernels, merge(): pl.pallas_call(merge_kernel, in_specs=[SCALARS] + [RESIDENT] * 6, out_spe...  3.95 us
  transfers between devices with their start and end apart: 22, of which 7 were waited for; matrix products, arithmetic and copies ran while one was open for 1% of the time, Pallas kernels for 43%

profile of v1, /device:TPU:0, one launch (start us, length us, event | category | flops | bytes accessed | tf_op | source)
XLA Modules:
  0.0 167.6 jit_solution(9016667803369659236)
XLA Ops:
  0.0 0.5 collective-permute-start.1
  0.5 0.1 collective-permute-start.2
  0.5 3.0 %collective-permute-start.6 = (bf16[2,160,1280]{2,1,0:T(8,128)(2,1)}, bf16[2,160,1280]{2,1,0:T(8,128)(2,1)}, u32[]{:S(2)}, u32[]{:S(2)}) collective-permute-start(bf16[2,160,1280]{2,1,0:T(8,128)(2,1)} %bitcast.34), channel_id=1, source_target_pairs={{0,2},{1,3},{2,0},{3,1},{4,6},{5,7},{6,4},{7,5},{8,10},{9,11},{10,... | collective-permute-start | bytes 2457608 | tf_op jit(solution)/shard_map/exchange_keys/ppermute | solution.py:24
  3.5 6.6 %project_keys.1 = (bf16[336,1024]{1,0:T(8,128)(2,1)}, bf16[336,1024]{1,0:T(8,128)(2,1)}) custom-call(bf16[1024,1280]{1,0:T(8,128)(2,1)} %refs_8_.3, s32[1,1024]{1,0:T(1,128)} %bitcast.36, bf16[1280]{0:T(1024)(128)(2,1)} %gain_ref.5, bf16[960,1280]{1,0:T(8,128)(2,1)} %bitcast.27, bf16[960,1280]{1,0:T(8,128)(2,1)} %bitcast.28), custom_call_target="tpu_custom_call" | custom-call | tf_op jit(solution)/shard_map/project/project_keys/pallas_call | solution.py:166
  10.1 0.0 collective-permute-done.2.refs_1_
  10.1 0.0 collective-permute-done.1.refs_5_
  10.1 0.1 collective-permute-start.3
  10.2 1.6 copy-done.7
  11.8 1.6 collective-permute-start.4
  13.4 1.5 collective-permute-start.5
  14.9 5.6 %project_queries.1 = (bf16[160,1024]{1,0:T(8,128)(2,1)}, bf16[160,1024]{1,0:T(8,128)(2,1)}) custom-call(bf16[1024,1280]{1,0:T(8,128)(2,1)} %refs_8_.3, s32[1,1024]{1,0:T(1,128)} %bitcast.37, bf16[1280]{0:T(1024)(128)(2,1)} %gain_ref.5, bf16[960,1280]{1,0:T(8,128)(2,1)} %bitcast.29), custom_call_target="tpu_custom_call" | custom-call | tf_op jit(solution)/shard_map/exchange_keys/project_queries/pallas_call | solution.py:166
  20.5 0.7 stack.23.place
  21.2 10.6 %attend_own.1 = (f32[2,2,96,512]{3,2,1,0:T(8,128)}, f32[2,2,512]{2,1,0:T(2,128)}) custom-call(s32[6]{0:T(128)} %stack.23.place, bf16[160,1024]{1,0:T(8,128)(2,1)} %get-tuple-element.62.refs_0_.refs_1_, bf16[336,1024]{1,0:T(8,128)(2,1)} %get-tuple-element.65.refs_1_.refs_2_.refs_3_.refs_4_, bf16[336,1024]{1,0:T(8,128)(2,1)} %get-tuple-element.65.refs_1_.refs_2_.refs_3_.refs_4_), custom_call_target="tpu_custom_call" | custom-call | flops 1000000 | bytes 1000000 | tf_op jit(solution)/shard_map/exchange_keys/attend_own/pallas_call | solution.py:366
  31.8 0.0 collective-permute-done.6.refs_2_
  31.8 0.0 collective-permute-done.3.refs_7_
  31.8 0.0 collective-permute-done.4.refs_6_
  31.8 0.0 collective-permute-done.5.refs_2_.refs_5_
  31.9 0.1 collective-permute-start.9
  31.9 0.6 collective-permute-start
  32.5 0.5 collective-permute-start.7
  33.0 0.2 collective-permute-start.10
  33.2 0.6 reduce-window.6
  33.8 0.2 slice_reduce_fusion
  34.1 0.1 fusion
  34.2 8.1 %collective-permute-done.refs_0_ = bf16[160,1024]{1,0:T(8,128)(2,1)S(1)} collective-permute-done((bf16[160,1024]{1,0:T(8,128)(2,1)}, bf16[160,1024]{1,0:T(8,128)(2,1)S(1)}, u32[]{:S(2)}, u32[]{:S(2)}) %collective-permute-start) | collective-permute-done | bytes 327712 | tf_op jit(solution)/shard_map/exchange_keys/ppermute | solution.py:24
  42.3 0.7 copy-done.8
  43.0 31.7 %attend_near.1 = (f32[4,2,96,512]{3,2,1,0:T(8,128)}, f32[4,2,512]{2,1,0:T(2,128)}) custom-call(s32[6]{0:T(128)} %stack.23.place, bf16[160,1024]{1,0:T(8,128)(2,1)} %copy-done.8, bf16[160,1024]{1,0:T(8,128)(2,1)} %get-tuple-element.62.refs_0_.refs_1_, bf16[336,1024]{1,0:T(8,128)(2,1)} %copy-done.5, ...), custom_call_target="tpu_custom_call" | custom-call | flops 1000000 | bytes 1000000 | tf_op jit(solution)/shard_map/attention/attend_near/pallas_call | solution.py:366
  74.7 0.0 collective-permute-done.7.refs_4_
  74.8 0.0 collective-permute-done.8.refs_5_
  74.8 0.0 collective-permute-done.9.refs_7_
  74.8 0.8 copy-done.11
  75.6 8.5 %attend_far.1 = (bf16[2,160,512]{2,1,0:T(8,128)(2,1)}, bf16[2,160,512]{2,1,0:T(8,128)(2,1)}) custom-call(s32[6]{0:T(128)} %stack.23.place, bf16[160,1024]{1,0:T(8,128)(2,1)} %copy-done.8, bf16[160,1024]{1,0:T(8,128)(2,1)} %get-tuple-element.62.refs_0_.refs_1_, bf16[336,1024]{1,0:T(8,128)(2,1)} %copy-done.5, ...), custom_call_target="tpu_custom_call" | custom-call | flops 1000000 | bytes 1000000 | tf_op jit(solution)/shard_map/attention/attend_far/pallas_call | solution.py:366
  84.2 0.0 copy-start
  84.2 0.0 copy-start.4
  84.2 0.6 collective-permute-start.11
  84.8 0.5 collective-permute-start.14
  85.3 6.4 %load_mixer.1 = (bf16[1280,1280]{1,0:T(8,128)(2,1)S(1)}, bf16[2,1280,1280]{2,1,0:T(8,128)(2,1)S(1)}, bf16[2,1280,1280]{2,1,0:T(8,128)(2,1)S(1)}) custom-call(s32[6]{0:T(128)S(1)} %copy-done.2, bf16[2,160,1280]{2,1,0:T(8,128)(2,1)} %bitcast.35, bf16[2,160,1280]{2,1,0:T(8,128)(2,1)} %copy-done.9, bf16[2,160,1280]{2,1,0:T(8,128)(2,1)} %collective-permute-done.6.refs_2_, ...), custom_call_target="tpu_custom_call" | custom-call | bytes 16000000 | tf_op jit(solution)/shard_map/exchange_context/load_mixer/pallas_call | solution.py:104
  91.7 2.0 %collective-permute-done.11.refs_1_ = bf16[2,160,512]{2,1,0:T(8,128)(2,1)S(1)} collective-permute-done((bf16[2,160,512]{2,1,0:T(8,128)(2,1)}, bf16[2,160,512]{2,1,0:T(8,128)(2,1)S(1)}, u32[]{:S(2)}, u32[]{:S(2)}) %collective-permute-start.11) | collective-permute-done | bytes 327712 | tf_op jit(solution)/shard_map/exchange_context/ppermute | solution.py:24
  93.8 0.5 collective-permute-start.15
  94.3 0.5 collective-permute-start.13
  94.8 0.0 collective-permute-done.14.refs_4_
  94.8 0.0 collective-permute-start.16
  94.8 7.4 %collective-permute-done.15.refs_5_ = bf16[2,160,512]{2,1,0:T(8,128)(2,1)S(1)} collective-permute-done((bf16[2,160,512]{2,1,0:T(8,128)(2,1)S(1)}, bf16[2,160,512]{2,1,0:T(8,128)(2,1)S(1)}, u32[]{:S(2)}, u32[]{:S(2)}) %collective-permute-start.15) | collective-permute-done | bytes 327712 | tf_op jit(solution)/shard_map/exchange_context/ppermute | solution.py:24
  102.2 0.0 collective-permute-start.17
  102.2 0.0 collective-permute-done.12.refs_2_
  102.2 0.0 collective-permute-done.13.refs_3_
  102.2 1.6 collective-permute-done.17.refs_7_
  103.8 6.4 %mixer.2 = (bf16[256,1280]{1,0:T(8,128)(2,1)S(1)}, f32[256,1280]{1,0:T(8,128)S(1)}) custom-call(s32[6]{0:T(128)S(1)} %copy-done.2, bf16[2,160,512]{2,1,0:T(8,128)(2,1)S(1)} %copy-done.1, bf16[2,160,512]{2,1,0:T(8,128)(2,1)S(1)} %collective-permute-done.11.refs_1_, bf16[2,160,512]{2,1,0:T(8,128)(2,1)S(1)} %collective-permute-done.12.refs_2_, ...), custom_call_target="tpu_custom_call" | custom-call | flops 5000000000 | bytes 20000000 | tf_op jit(solution)/shard_map/mixer/mixer/pallas_call | solution.py:420
  110.3 0.2 collective-permute-start.18
  110.5 0.5 collective-permute-start.19
  111.0 6.7 %mixer.3 = (bf16[256,1280]{1,0:T(8,128)(2,1)S(1)}, f32[256,1280]{1,0:T(8,128)S(1)}) custom-call(s32[6]{0:T(128)S(1)} %copy-done.2, bf16[2,160,512]{2,1,0:T(8,128)(2,1)S(1)} %copy-done.1, bf16[2,160,512]{2,1,0:T(8,128)(2,1)S(1)} %collective-permute-done.11.refs_1_, bf16[2,160,512]{2,1,0:T(8,128)(2,1)S(1)} %collective-permute-done.12.refs_2_, ...), custom_call_target="tpu_custom_call" | custom-call | flops 5000000000 | bytes 20000000 | tf_op jit(solution)/shard_map/mixer/mixer/pallas_call | solution.py:420
  117.7 0.0 copy-start.3
  117.7 1.6 collective-permute-start.20
  119.3 0.0 collective-permute-done.18.other
  119.3 2.9 %load_merge.1.weights = bf16[640,5120]{1,0:T(8,128)(2,1)S(1)} custom-call(bf16[320,5120]{1,0:T(8,128)(2,1)} %bitcast.30, bf16[320,5120]{1,0:T(8,128)(2,1)} %collective-permute-done.18.other), custom_call_target="tpu_custom_call" | custom-call | bytes 8000000 | tf_op jit(solution)/shard_map/merge/load_merge/pallas_call | solution.py:129
  122.2 5.8 %collective-permute-done.19.received = bf16[256,1280]{1,0:T(8,128)(2,1)S(1)} collective-permute-done((bf16[256,1280]{1,0:T(8,128)(2,1)S(1)}, bf16[256,1280]{1,0:T(8,128)(2,1)S(1)}, u32[]{:S(2)}, u32[]{:S(2)}) %collective-permute-start.19) | collective-permute-done | bytes 655392 | tf_op jit(solution)/shard_map/mixer/ppermute | solution.py:24
  128.0 1.7 %gather.1.earlier = bf16[4,256,1280]{2,1,0:T(8,128)(2,1)S(1)} custom-call(s32[6]{0:T(128)S(1)} %copy-done.2, s32[4,256]{1,0:T(4,128)S(1)} %subtract_bitcast_fusion.index_ref, f32[256,1280]{1,0:T(8,128)S(1)} %get-tuple-element.106.kept, bf16[256,1280]{1,0:T(8,128)(2,1)S(1)} %collective-permute-done.19.received, bf16[1280]{0:T(1024)(128)(2,1)S(1)} %copy-done.3), custom_call_target="tpu_custom_call" | custom-call | flops 1000000000 | bytes 5000000 | tf_op jit(solution)/shard_map/merge/gather/pallas_call | solution.py:457
  129.8 11.7 %collective-permute-done.20.received = bf16[256,1280]{1,0:T(8,128)(2,1)S(1)} collective-permute-done((bf16[256,1280]{1,0:T(8,128)(2,1)S(1)}, bf16[256,1280]{1,0:T(8,128)(2,1)S(1)}, u32[]{:S(2)}, u32[]{:S(2)}) %collective-permute-start.20) | collective-permute-done | bytes 655392 | tf_op jit(solution)/shard_map/mixer/ppermute | solution.py:24
  141.5 4.0 %merge.1 = (f32[256,320]{1,0:T(8,128)S(1)}, f32[256,320]{1,0:T(8,128)S(1)}) custom-call(s32[6]{0:T(128)S(1)} %copy-done.2, s32[4,256]{1,0:T(4,128)S(1)} %subtract_bitcast_fusion.index_ref, f32[256,1280]{1,0:T(8,128)S(1)} %get-tuple-element.109.kept, bf16[256,1280]{1,0:T(8,128)(2,1)S(1)} %collective-permute-done.20.received, bf16[1280]{0:T(1024)(128)(2,1)S(1)} %copy-done.3, ...), custom_call_target="tpu_custom_call" | custom-call | flops 3000000000 | bytes 12000000 | tf_op jit(solution)/shard_map/merge/merge/pallas_call | solution.py:486
  145.5 0.1 collective-permute-start.21
  145.6 1.7 %collective-permute-done.21.received = f32[256,320]{1,0:T(8,128)S(1)} collective-permute-done((f32[256,320]{1,0:T(8,128)S(1)}, f32[256,320]{1,0:T(8,128)S(1)}, u32[]{:S(2)}, u32[]{:S(2)}) %collective-permute-start.21) | collective-permute-done | bytes 327712 | tf_op jit(solution)/shard_map/merge/ppermute | solution.py:24
  147.3 0.3 place.1
  147.6 19.2 %all_to_all.5 = bf16[8,64,320]{2,1,0:T(8,128)(2,1)S(1)} all-to-all(bf16[8,64,320]{2,1,0:T(8,128)(2,1)S(1)} %bitcast.26), channel_id=1, replica_groups=mesh['req'=8,'tp'=4] {'req'}, dimensions={0} | all-to-all | bytes 655360 | tf_op jit(solution)/shard_map/place/all_to_all | solution.py:630
  166.8 0.7 copy.14
  (31 shorter events, 0.1 us)
Async XLA Ops:
  0.0 10.1 %collective-permute-start.1 = (bf16[1280,1280]{1,0:T(8,128)(2,1)}, bf16[1280,1280]{1,0:T(8,128)(2,1)S(1)}, u32[]{:S(2)}, u32[]{:S(2)}) collective-permute-start(bf16[1280,1280]{1,0:T(8,128)(2,1)} %refs_4_.1), channel_id=1, source_target_pairs={{0,1},{1,0},{2,3},{3,2},{4,5},{5,4},{6,7},{7,6},{8,9},{9,8},{10,11... | collective-permute-start | bytes 9830408 | tf_op jit(solution)/shard_map/weights/ppermute | solution.py:24
  0.5 9.6 %collective-permute-start.2 = (bf16[2,160,1280]{2,1,0:T(8,128)(2,1)}, bf16[2,160,1280]{2,1,0:T(8,128)(2,1)S(1)}, u32[]{:S(2)}, u32[]{:S(2)}) collective-permute-start(bf16[2,160,1280]{2,1,0:T(8,128)(2,1)} %bitcast.33), channel_id=1, source_target_pairs={{0,1},{1,0},{2,3},{3,2},{4,5},{5,4},{6,7},{7,6},{8,9},{9,8},{10,11... | collective-permute-start | bytes 2457608 | tf_op jit(solution)/shard_map/weights/ppermute | solution.py:24
  0.5 31.3 %collective-permute-start.6 = (bf16[2,160,1280]{2,1,0:T(8,128)(2,1)}, bf16[2,160,1280]{2,1,0:T(8,128)(2,1)}, u32[]{:S(2)}, u32[]{:S(2)}) collective-permute-start(bf16[2,160,1280]{2,1,0:T(8,128)(2,1)} %bitcast.34), channel_id=1, source_target_pairs={{0,2},{1,3},{2,0},{3,1},{4,6},{5,7},{6,4},{7,5},{8,10},{9,11},{10,... | collective-permute-start | bytes 2457608 | tf_op jit(solution)/shard_map/exchange_keys/ppermute | solution.py:24
  10.1 75.2 %copy-start.9 = (bf16[2,160,1280]{2,1,0:T(8,128)(2,1)}, bf16[2,160,1280]{2,1,0:T(8,128)(2,1)S(1)}, u32[]{:S(2)}) copy-start(bf16[2,160,1280]{2,1,0:T(8,128)(2,1)S(1)} %collective-permute-done.2.refs_1_) | copy-start | bytes 2457604
  10.1 1.7 %copy-start.7 = (bf16[1280,1280]{1,0:T(8,128)(2,1)}, bf16[1280,1280]{1,0:T(8,128)(2,1)S(1)}, u32[]{:S(2)}) copy-start(bf16[1280,1280]{1,0:T(8,128)(2,1)S(1)} %collective-permute-done.1.refs_5_) | copy-start | bytes 9830404
  10.1 21.7 %collective-permute-start.3 = (bf16[336,1024]{1,0:T(8,128)(2,1)}, bf16[336,1024]{1,0:T(8,128)(2,1)}, u32[]{:S(2)}, u32[]{:S(2)}) collective-permute-start(bf16[336,1024]{1,0:T(8,128)(2,1)} %get-tuple-element.65.refs_1_.refs_2_.refs_3_.refs_4_), channel_id=1, source_target_pairs={{0,1},{1,0},{2,3},{3,2},{4,5},{5,4},{6,7},{7,6},{8,16},{9,17},{10,... | collective-permute-start | bytes 2064392 | tf_op jit(solution)/shard_map/exchange_keys/ppermute | solution.py:39
  11.8 20.0 %collective-permute-start.4 = (bf16[336,1024]{1,0:T(8,128)(2,1)}, bf16[336,1024]{1,0:T(8,128)(2,1)}, u32[]{:S(2)}, u32[]{:S(2)}) collective-permute-start(bf16[336,1024]{1,0:T(8,128)(2,1)} %get-tuple-element.65.refs_1_.refs_2_.refs_3_.refs_4_), channel_id=1, source_target_pairs={{0,8},{1,9},{2,10},{3,11},{4,12},{5,13},{6,14},{7,15},{8,0},{9,1},... | collective-permute-start | bytes 2064392 | tf_op jit(solution)/shard_map/exchange_keys/ppermute | solution.py:39
  13.4 18.5 %collective-permute-start.5 = (bf16[336,1024]{1,0:T(8,128)(2,1)}, bf16[336,1024]{1,0:T(8,128)(2,1)S(1)}, u32[]{:S(2)}, u32[]{:S(2)}) collective-permute-start(bf16[336,1024]{1,0:T(8,128)(2,1)} %get-tuple-element.66), channel_id=1, source_target_pairs={{0,4},{4,0},{8,12},{12,8},{16,20},{20,16},{24,28},{28,24},{1,5},{5... | collective-permute-start | bytes 2064392 | tf_op jit(solution)/shard_map/exchange_keys/ppermute | solution.py:24
  14.9 18.4 %copy-start.12 = (s32[256,1]{0,1:T(1,128)S(1)}, s32[256,1]{0,1:T(1,128)}, u32[]{:S(2)}) copy-start(s32[256,1]{0,1:T(1,128)} %param.23) | copy-start | bytes 3076
  14.9 19.3 %copy-start.13 = (s32[256,4]{0,1:T(4,128)S(1)}, s32[256,4]{0,1:T(4,128)}, u32[]{:S(2)}) copy-start(s32[256,4]{0,1:T(4,128)} %param.22) | copy-start | bytes 12292
  31.8 10.4 %copy-start.5 = (bf16[336,1024]{1,0:T(8,128)(2,1)}, bf16[336,1024]{1,0:T(8,128)(2,1)S(1)}, u32[]{:S(2)}) copy-start(bf16[336,1024]{1,0:T(8,128)(2,1)S(1)} %collective-permute-done.5.refs_2_.refs_5_) | copy-start | bytes 2064388
  31.9 42.9 %collective-permute-start.9 = (bf16[1280,1280]{1,0:T(8,128)(2,1)}, bf16[1280,1280]{1,0:T(8,128)(2,1)}, u32[]{:S(2)}, u32[]{:S(2)}) collective-permute-start(bf16[1280,1280]{1,0:T(8,128)(2,1)} %refs_6_.1), channel_id=1, source_target_pairs={{0,1},{1,0},{2,3},{3,2},{4,5},{5,4},{6,7},{7,6},{8,9},{9,8},{10,11... | collective-permute-start | bytes 9830408 | tf_op jit(solution)/shard_map/exchange_keys/ppermute | solution.py:24
  31.9 10.3 %collective-permute-start = (bf16[160,1024]{1,0:T(8,128)(2,1)}, bf16[160,1024]{1,0:T(8,128)(2,1)S(1)}, u32[]{:S(2)}, u32[]{:S(2)}) collective-permute-start(bf16[160,1024]{1,0:T(8,128)(2,1)} %get-tuple-element.60), channel_id=1, source_target_pairs={{0,4},{4,0},{8,12},{12,8},{16,20},{20,16},{24,28},{28,24},{1,5},{5... | collective-permute-start | bytes 983048 | tf_op jit(solution)/shard_map/exchange_keys/ppermute | solution.py:24
  32.5 42.2 %collective-permute-start.7 = (bf16[336,1024]{1,0:T(8,128)(2,1)S(1)}, bf16[336,1024]{1,0:T(8,128)(2,1)S(1)}, u32[]{:S(2)}, u32[]{:S(2)}) collective-permute-start(bf16[336,1024]{1,0:T(8,128)(2,1)S(1)} %collective-permute-done.5.refs_2_.refs_5_), channel_id=1, source_target_pairs={{0,8},{1,9},{2,10},{3,11},{4,12},{5,13},{6,14},{7,15},{8,0},{9,1},... | collective-permute-start | bytes 2064392 | tf_op jit(solution)/shard_map/exchange_keys/ppermute | solution.py:39
  33.0 41.8 %collective-permute-start.8 = (bf16[336,1024]{1,0:T(8,128)(2,1)S(1)}, bf16[336,1024]{1,0:T(8,128)(2,1)}, u32[]{:S(2)}, u32[]{:S(2)}) collective-permute-start(bf16[336,1024]{1,0:T(8,128)(2,1)S(1)} %collective-permute-done.5.refs_2_.refs_5_), channel_id=1, source_target_pairs={{0,1},{1,0},{2,3},{3,2},{4,5},{5,4},{6,7},{7,6},{8,16},{9,17},{10,... | collective-permute-start | bytes 2064392 | tf_op jit(solution)/shard_map/exchange_keys/ppermute | solution.py:39
  33.0 41.8 %collective-permute-start.10 = (bf16[2,160,1280]{2,1,0:T(8,128)(2,1)S(1)}, bf16[2,160,1280]{2,1,0:T(8,128)(2,1)S(1)}, u32[]{:S(2)}, u32[]{:S(2)}) collective-permute-start(bf16[2,160,1280]{2,1,0:T(8,128)(2,1)S(1)} %collective-permute-done.2.refs_1_), channel_id=1, source_target_pairs={{0,2},{1,3},{2,0},{3,1},{4,6},{5,7},{6,4},{7,5},{8,10},{9,11},{10,... | collective-permute-start | bytes 2457608 | tf_op jit(solution)/shard_map/exchange_keys/ppermute | solution.py:24
  42.3 0.7 copy-start.8
  74.7 10.6 %copy-start.2 = (s32[6]{0:T(128)S(1)}, s32[6]{0:T(128)}, u32[]{:S(2)}) copy-start(s32[6]{0:T(128)} %stack.23.place) | copy-start | bytes 76
  74.7 0.9 copy-start.11
  74.8 10.5 %copy-start.10 = (bf16[2,160,1280]{2,1,0:T(8,128)(2,1)}, bf16[2,160,1280]{2,1,0:T(8,128)(2,1)S(1)}, u32[]{:S(2)}) copy-start(bf16[2,160,1280]{2,1,0:T(8,128)(2,1)S(1)} %collective-permute-done.10.refs_3_) | copy-start | bytes 2457604
  84.1 10.1 %copy-start.1 = (bf16[2,160,512]{2,1,0:T(8,128)(2,1)S(1)}, bf16[2,160,512]{2,1,0:T(8,128)(2,1)}, u32[]{:S(2)}) copy-start(bf16[2,160,512]{2,1,0:T(8,128)(2,1)} %get-tuple-element.85.refs_0_) | copy-start | bytes 983044
  84.2 19.6 %copy-start = (bf16[1024,1280]{1,0:T(8,128)(2,1)S(1)}, bf16[1024,1280]{1,0:T(8,128)(2,1)}, u32[]{:S(2)}) copy-start(bf16[1024,1280]{1,0:T(8,128)(2,1)} %refs_8_.3) | copy-start | bytes 7864324
  84.2 19.6 %copy-start.4 = (bf16[1280]{0:T(1024)(128)(2,1)S(1)}, bf16[1280]{0:T(1024)(128)(2,1)}, u32[]{:S(2)}) copy-start(bf16[1280]{0:T(1024)(128)(2,1)} %refs_9_.3) | copy-start | bytes 7684
  84.2 9.6 %collective-permute-start.11 = (bf16[2,160,512]{2,1,0:T(8,128)(2,1)}, bf16[2,160,512]{2,1,0:T(8,128)(2,1)S(1)}, u32[]{:S(2)}, u32[]{:S(2)}) collective-permute-start(bf16[2,160,512]{2,1,0:T(8,128)(2,1)} %get-tuple-element.86), channel_id=1, source_target_pairs={{0,4},{4,0},{8,12},{12,8},{16,20},{20,16},{24,28},{28,24},{1,5},{5... | collective-permute-start | bytes 983048 | tf_op jit(solution)/shard_map/exchange_context/ppermute | solution.py:24
  84.8 10.0 %collective-permute-start.14 = (bf16[2,160,512]{2,1,0:T(8,128)(2,1)}, bf16[2,160,512]{2,1,0:T(8,128)(2,1)S(1)}, u32[]{:S(2)}, u32[]{:S(2)}) collective-permute-start(bf16[2,160,512]{2,1,0:T(8,128)(2,1)} %get-tuple-element.85.refs_0_), channel_id=1, source_target_pairs={{0,2},{1,3},{2,0},{3,1},{4,6},{5,7},{6,4},{7,5},{8,10},{9,11},{10,... | collective-permute-start | bytes 983048 | tf_op jit(solution)/shard_map/exchange_context/ppermute | solution.py:24
  93.8 16.5 %copy-start.6 = (bf16[5120,320]{0,1:T(8,128)(2,1)S(1)}, bf16[5120,320]{0,1:T(8,128)(2,1)}, u32[]{:S(2)}) copy-start(bf16[5120,320]{0,1:T(8,128)(2,1)} %param.21) | copy-start | bytes 9830404
  93.8 8.4 %collective-permute-start.15 = (bf16[2,160,512]{2,1,0:T(8,128)(2,1)S(1)}, bf16[2,160,512]{2,1,0:T(8,128)(2,1)S(1)}, u32[]{:S(2)}, u32[]{:S(2)}) collective-permute-start(bf16[2,160,512]{2,1,0:T(8,128)(2,1)S(1)} %collective-permute-done.11.refs_1_), channel_id=1, source_target_pairs={{0,2},{1,3},{2,0},{3,1},{4,6},{5,7},{6,4},{7,5},{8,10},{9,11},{10,... | collective-permute-start | bytes 983048 | tf_op jit(solution)/shard_map/exchange_context/ppermute | solution.py:24
  94.3 7.9 %collective-permute-start.12 = (bf16[2,160,512]{2,1,0:T(8,128)(2,1)S(1)}, bf16[2,160,512]{2,1,0:T(8,128)(2,1)S(1)}, u32[]{:S(2)}, u32[]{:S(2)}) collective-permute-start(bf16[2,160,512]{2,1,0:T(8,128)(2,1)S(1)} %copy-done.1), channel_id=1, source_target_pairs={{0,1},{1,0},{2,3},{3,2},{4,5},{5,4},{6,7},{7,6},{8,9},{9,8},{10,11... | collective-permute-start | bytes 983048 | tf_op jit(solution)/shard_map/exchange_context/ppermute | solution.py:24
  94.3 7.9 %collective-permute-start.13 = (bf16[2,160,512]{2,1,0:T(8,128)(2,1)S(1)}, bf16[2,160,512]{2,1,0:T(8,128)(2,1)S(1)}, u32[]{:S(2)}, u32[]{:S(2)}) collective-permute-start(bf16[2,160,512]{2,1,0:T(8,128)(2,1)S(1)} %collective-permute-done.11.refs_1_), channel_id=1, source_target_pairs={{0,1},{1,0},{2,3},{3,2},{4,5},{5,4},{6,7},{7,6},{8,9},{9,8},{10,11... | collective-permute-start | bytes 983048 | tf_op jit(solution)/shard_map/exchange_context/ppermute | solution.py:24
  94.8 7.4 %collective-permute-start.16 = (bf16[2,160,512]{2,1,0:T(8,128)(2,1)S(1)}, bf16[2,160,512]{2,1,0:T(8,128)(2,1)S(1)}, u32[]{:S(2)}, u32[]{:S(2)}) collective-permute-start(bf16[2,160,512]{2,1,0:T(8,128)(2,1)S(1)} %collective-permute-done.14.refs_4_), channel_id=1, source_target_pairs={{0,1},{1,0},{2,3},{3,2},{4,5},{5,4},{6,7},{7,6},{8,9},{9,8},{10,11... | collective-permute-start | bytes 983048 | tf_op jit(solution)/shard_map/exchange_context/ppermute | solution.py:24
  102.2 1.6 collective-permute-start.17
  110.3 9.0 %collective-permute-start.18 = (bf16[320,5120]{1,0:T(8,128)(2,1)S(1)}, bf16[320,5120]{1,0:T(8,128)(2,1)}, u32[]{:S(2)}, u32[]{:S(2)}) collective-permute-start(bf16[320,5120]{1,0:T(8,128)(2,1)S(1)} %bitcast.31), channel_id=1, source_target_pairs={{0,1},{1,0},{2,3},{3,2},{4,5},{5,4},{6,7},{7,6},{8,9},{9,8},{10,11... | collective-permute-start | bytes 9830408 | tf_op jit(solution)/shard_map/mixer/ppermute | solution.py:24
  110.5 17.6 %collective-permute-start.19 = (bf16[256,1280]{1,0:T(8,128)(2,1)S(1)}, bf16[256,1280]{1,0:T(8,128)(2,1)S(1)}, u32[]{:S(2)}, u32[]{:S(2)}) collective-permute-start(bf16[256,1280]{1,0:T(8,128)(2,1)S(1)} %get-tuple-element.99), channel_id=1, source_target_pairs={{0,2},{1,3},{2,0},{3,1},{4,6},{5,7},{6,4},{7,5},{8,10},{9,11},{10,... | collective-permute-start | bytes 1966088 | tf_op jit(solution)/shard_map/mixer/ppermute | solution.py:24
  117.7 10.4 %copy-start.3 = (bf16[1280]{0:T(1024)(128)(2,1)S(1)}, bf16[1280]{0:T(1024)(128)(2,1)}, u32[]{:S(2)}) copy-start(bf16[1280]{0:T(1024)(128)(2,1)} %gain_ref.7) | copy-start | bytes 7684
  117.7 23.8 %collective-permute-start.20 = (bf16[256,1280]{1,0:T(8,128)(2,1)S(1)}, bf16[256,1280]{1,0:T(8,128)(2,1)S(1)}, u32[]{:S(2)}, u32[]{:S(2)}) collective-permute-start(bf16[256,1280]{1,0:T(8,128)(2,1)S(1)} %get-tuple-element.103), channel_id=1, source_target_pairs={{0,2},{1,3},{2,0},{3,1},{4,6},{5,7},{6,4},{7,5},{8,10},{9,11},{10,... | collective-permute-start | bytes 1966088 | tf_op jit(solution)/shard_map/mixer/ppermute | solution.py:24
  145.5 1.8 %collective-permute-start.21 = (f32[256,320]{1,0:T(8,128)S(1)}, f32[256,320]{1,0:T(8,128)S(1)}, u32[]{:S(2)}, u32[]{:S(2)}) collective-permute-start(f32[256,320]{1,0:T(8,128)S(1)} %get-tuple-element.114), channel_id=1, source_target_pairs={{0,1},{1,0},{2,3},{3,2},{4,5},{5,4},{6,7},{7,6},{8,9},{9,8},{10,11... | collective-permute-start | bytes 983048 | tf_op jit(solution)/shard_map/merge/ppermute | solution.py:24

commit v2 on v1

--- a/solution.py
+++ b/solution.py
@@ -387,17 +387,17 @@
     )(place, *operands)
 
 
-def mixer_kernel(chunk, which, place, *refs):
+def mixer_kernel(first, which, place, *refs):
     sources, refs = refs[:8], refs[8:]
     x_hbm, gain_ref, wo, we, wr, sent, kept, context, hidden, x, sem = refs
     rows = x.shape[0]
     half = sources[0].shape[1]
     width = we.shape[2]
     fetch = pltpu.make_async_copy(
-        x_hbm.at[pl.ds(pl.multiple_of(place[2] + chunk * rows, rows), rows)], x, sem
+        x_hbm.at[pl.ds(pl.multiple_of(place[2] + first, 128), rows)], x, sem
     )
     fetch.start()
-    lanes = slice(chunk * rows, (chunk + 1) * rows)
+    lanes = slice(first, first + rows)
     for i in range(8):
         context[i * half : (i + 1) * half, :] = sources[i][which[i], :, lanes].astype(jnp.float32)
     inputs = jnp.transpose(context[...]).astype(jnp.bfloat16)
@@ -413,12 +413,12 @@
     kept[...] = total + out
 
 
-def mixer(place, pieces, tokens, gain, weights, chunk, chunk_rows):
+def mixer(place, pieces, tokens, gain, weights, first, chunk_rows):
     width = tokens.shape[1]
     half = pieces[0][0].shape[1]
     hidden = weights[1].shape[2]
     return pl.pallas_call(
-        functools.partial(mixer_kernel, chunk, [which for _, which in pieces]),
+        functools.partial(mixer_kernel, first, [which for _, which in pieces]),
         in_specs=[SCALARS] + [RESIDENT] * 8 + [ANYWHERE] + [RESIDENT] * 4,
         out_specs=[RESIDENT] * 2,
         out_shape=[
@@ -446,17 +446,21 @@
     return jnp.concatenate(parts, axis=1).astype(jnp.float32).astype(jnp.bfloat16)
 
 
-def gather_kernel(place, index_ref, kept, received, gain_ref, merged):
+def gather_kernel(first, place, index_ref, kept, received, gain_ref, *refs):
+    merged = refs[-1]
     rows = kept.shape[0]
     final = normalized(kept[...] + received[...].astype(jnp.float32), row_of(gain_ref))
     for k in range(4):
-        merged[k] = dot(one_hot_rows(index_ref, k, place[2], rows), final, NN).astype(jnp.bfloat16)
-
-
-def gather(place, index, kept, received, gain):
+        part = dot(one_hot_rows(index_ref, k, place[2] + first, rows), final, NN)
+        if len(refs) > 1:
+            part = part + refs[0][k].astype(jnp.float32)
+        merged[k] = part.astype(jnp.bfloat16)
+
+
+def gather(place, index, kept, received, gain, first, earlier):
     return pl.pallas_call(
-        gather_kernel,
-        in_specs=[SCALARS] + [RESIDENT] * 4,
+        functools.partial(gather_kernel, first),
+        in_specs=[SCALARS] + [RESIDENT] * (4 + len(earlier)),
         out_specs=RESIDENT,
         out_shape=pltpu.VMEM((4, index.shape[1], kept.shape[1]), jnp.bfloat16),
         compiler_params=vmem(20),
@@ -464,15 +468,17 @@
             flops=1_000_000_000, bytes_accessed=5_000_000, transcendentals=0
         ),
         name="gather",
-    )(place, index, kept, received, gain)
-
-
-def merge_kernel(place, index_ref, kept, received, gain_ref, earlier, weights, own, other, parts):
+    )(place, index, kept, received, gain, *[in_vmem(a) for a in earlier])
+
+
+def merge_kernel(
+    first, place, index_ref, kept, received, gain_ref, earlier, weights, own, other, parts
+):
     rows, width = kept.shape
     columns = own.shape[1]
     final = normalized(kept[...] + received[...].astype(jnp.float32), row_of(gain_ref))
     for k in range(4):
-        part = dot(one_hot_rows(index_ref, k, place[3], rows), final, NN)
+        part = dot(one_hot_rows(index_ref, k, place[2] + first, rows), final, NN)
         part = part + earlier[k].astype(jnp.float32)
         parts[:, k * width : (k + 1) * width] = part.astype(jnp.bfloat16)
     total = dot(parts[...], weights[...], NT)
@@ -480,11 +486,11 @@
     other[...] = total[:, columns:]
 
 
-def merge(place, index, kept, received, gain, earlier, weights):
+def merge(place, index, kept, received, gain, first, earlier, weights):
     merged_rows = index.shape[1]
     columns = weights.shape[0] // 2
     return pl.pallas_call(
-        merge_kernel,
+        functools.partial(merge_kernel, first),
         in_specs=[SCALARS] + [RESIDENT] * 6,
         out_specs=[RESIDENT] * 2,
         out_shape=[jax.ShapeDtypeStruct((merged_rows, columns), jnp.float32)] * 2,
@@ -526,9 +532,9 @@
     par = req % 2
     core = lax.axis_index("tp") % 2
 
-    chunk_rows = 256
     per_core = rows // 2
-    place = jnp.stack([par, core, core * per_core, core * per_core + chunk_rows, alone(0), alone(1)])
+    chunks = [(0, 128), (128, per_core - 256), (per_core - 128, 128)]
+    place = jnp.stack([par, core, core * per_core, req, alone(0), alone(1)])
     tie = lax.optimization_barrier
     with jax.named_scope("weights"):
         wo_own = output_weight.reshape(2, half, width)
@@ -599,21 +605,28 @@
 
     with jax.named_scope("mixer"):
         sent, kept, received = [], [], []
-        for chunk in range(2):
-            s, k = mixer(place, pieces, tokens, mixer_gain, weights, chunk, chunk_rows)
+        for first, size in chunks:
+            s, k = mixer(place, pieces, tokens, mixer_gain, weights, first, size)
             sent.append(s)
             kept.append(k)
             received.append(swap(s, "tp", 2))
-            if chunk == 0:
+            if first == 0:
                 merge_own, _ = tie((jnp.transpose(merge_weight), s))
                 merge_other = swap(merge_own, "tp", 1)
 
     with jax.named_scope("merge"):
-        merge_other, position, index, _ = tie((merge_other, position, index, sent[1]))
+        merge_other, position, index, _ = tie((merge_other, position, index, sent[-1]))
         weights = load_merge(merge_own, merge_other)
-        earlier = gather(place, index, kept[0], received[0], output_gain)
-        weights, earlier, last, position = tie((weights, earlier, received[1], position))
-        own, other = merge(place, index, kept[1], last, output_gain, earlier, weights)
+        earlier = []
+        for c, (first, _) in enumerate(chunks[:-1]):
+            earlier = [
+                gather(place, index, kept[c], received[c], output_gain, first, earlier)
+            ]
+        weights, earlier, last, position = tie((weights, earlier[0], received[-1], position))
+        first = chunks[-1][0]
+        own, other = merge(
+            place, index, kept[-1], last, output_gain, first, earlier, weights
+        )
         other = swap(other, "tp", 1)
 
     with jax.named_scope("place"):

time: 169 us -> 162 us (0.959); the launches traced: 168 us -> 164 us
  waiting for transfers between devices: 38.4 us -> 30.3 us
  Pallas kernels: 91.6 us -> 95.8 us
  blocking collectives: 19.2 us -> 15 us
  starting transfers between devices: 12.5 us -> 15.9 us
    ppermute x18 -> x19, waiting for transfers between devices: 38.4 us -> 30.3 us  [swap(): lax.ppermute(block, axis, [(i, i ^ flip) for i in range(lax.axis_size(axi...]
    all_to_all x1, blocking collectives: 19.2 us -> 15 us  [body(): lax.all_to_all(outgoing, 'req', split_axis=0, concat_axis=0, tiled=True)]
    ppermute x4, starting transfers between devices: 2.1 us -> 4.74 us  [swap_pairs(): return lax.ppermute(block, ('req', 'tp'), route)]
    pallas_call x4 -> x6, Pallas kernels: 18.8 us -> 21.4 us  [the longest x3 14.2 us: mixer(): pl.pallas_call(functools.partial(mixer_kernel, first, [which for _, which...]
    pallas_call x3, Pallas kernels: 50.9 us -> 52.7 us  [attend(): pl.pallas_call(functools.partial(attend_kernel, groups, blocks, flags, re...]
    ppermute x18 -> x19, starting transfers between devices: 10.4 us -> 11.2 us  [swap(): lax.ppermute(block, axis, [(i, i ^ flip) for i in range(lax.axis_size(axi...]
    unnamed x29 -> x33, local copies, waits for them, and re-layouts: 3.95 us -> 4.57 us
  transfers between devices with their start and end apart: 22 -> 23, of which waited for: 7 -> 7; matrix products, arithmetic and copies ran while one was open for 1% -> 1% of each run, Pallas kernels for 43% -> 50%
where the time goes in v2:
time: 162 us; the launch traced here: 164 us
  Pallas kernels  95.8 us (59%)
  waiting for transfers between devices  30.3 us (19%)
  starting transfers between devices  15.9 us (10%)
  blocking collectives  15 us (9%)
  local copies, waits for them, and re-layouts  5.46 us (3%)
    pallas_call x3, Pallas kernels, attend(): pl.pallas_call(functools.partial(attend_kernel, groups, blocks, flags, re...  52.7 us
    ppermute x19, waiting for transfers between devices, swap(): lax.ppermute(block, axis, [(i, i ^ flip) for i in range(lax.axis_size(axi...  30.3 us
    all_to_all x1, blocking collectives, body(): lax.all_to_all(outgoing, 'req', split_axis=0, concat_axis=0, tiled=True)  15 us
    pallas_call x3, Pallas kernels, mixer(): pl.pallas_call(functools.partial(mixer_kernel, first, [which for _, which...  14.2 us
    pallas_call x2, Pallas kernels, project(): pl.pallas_call(functools.partial(project_kernel, len(parts)), grid=(rows...  12.2 us
    ppermute x19, starting transfers between devices, swap(): lax.ppermute(block, axis, [(i, i ^ flip) for i in range(lax.axis_size(axi...  11.2 us
    pallas_call x1, Pallas kernels, load_mixer(): pl.pallas_call(load_mixer_kernel, in_specs=[SCALARS] + [ANYWHERE] * 8, ou...  6.4 us
    ppermute x4, starting transfers between devices, swap_pairs(): return lax.ppermute(block, ('req', 'tp'), route)  4.74 us
  transfers between devices with their start and end apart: 23, of which 7 were waited for; matrix products, arithmetic and copies ran while one was open for 1% of the time, Pallas kernels for 50%

profile of v2, /device:TPU:0, one launch (start us, length us, event | category | flops | bytes accessed | tf_op | source)
XLA Modules:
  0.0 163.6 jit_solution(2639138544866324257)
XLA Ops:
  0.0 0.5 collective-permute-start.1
  0.5 0.1 collective-permute-start.2
  0.5 3.0 %collective-permute-start.6 = (bf16[2,160,1280]{2,1,0:T(8,128)(2,1)}, bf16[2,160,1280]{2,1,0:T(8,128)(2,1)}, u32[]{:S(2)}, u32[]{:S(2)}) collective-permute-start(bf16[2,160,1280]{2,1,0:T(8,128)(2,1)} %bitcast.34), channel_id=1, source_target_pairs={{0,2},{1,3},{2,0},{3,1},{4,6},{5,7},{6,4},{7,5},{8,10},{9,11},{10,... | collective-permute-start | bytes 2457608 | tf_op jit(solution)/shard_map/exchange_keys/ppermute | solution.py:24
  3.5 6.6 %project_keys.1 = (bf16[336,1024]{1,0:T(8,128)(2,1)}, bf16[336,1024]{1,0:T(8,128)(2,1)}) custom-call(bf16[1024,1280]{1,0:T(8,128)(2,1)} %refs_8_.5, s32[1,1024]{1,0:T(1,128)} %bitcast.36, bf16[1280]{0:T(1024)(128)(2,1)} %gain_ref.6, bf16[960,1280]{1,0:T(8,128)(2,1)} %bitcast.27, bf16[960,1280]{1,0:T(8,128)(2,1)} %bitcast.28), custom_call_target="tpu_custom_call" | custom-call | tf_op jit(solution)/shard_map/project/project_keys/pallas_call | solution.py:166
  10.1 1.7 %copy-done.7 = bf16[1280,1280]{1,0:T(8,128)(2,1)} copy-done((bf16[1280,1280]{1,0:T(8,128)(2,1)}, bf16[1280,1280]{1,0:T(8,128)(2,1)S(1)}, u32[]{:S(2)}) %copy-start.7) | copy-done | bytes 3276824
  11.8 1.5 collective-permute-start.5
  13.3 1.6 collective-permute-start.4
  14.9 0.0 collective-permute-start.3
  14.9 5.6 %project_queries.1 = (bf16[160,1024]{1,0:T(8,128)(2,1)}, bf16[160,1024]{1,0:T(8,128)(2,1)}) custom-call(bf16[1024,1280]{1,0:T(8,128)(2,1)} %refs_8_.5, s32[1,1024]{1,0:T(1,128)} %bitcast.37, bf16[1280]{0:T(1024)(128)(2,1)} %gain_ref.6, bf16[960,1280]{1,0:T(8,128)(2,1)} %bitcast.29), custom_call_target="tpu_custom_call" | custom-call | tf_op jit(solution)/shard_map/exchange_keys/project_queries/pallas_call | solution.py:166
  20.5 0.7 stack.23.place
  21.2 10.6 %attend_own.1 = (f32[2,2,96,512]{3,2,1,0:T(8,128)}, f32[2,2,512]{2,1,0:T(2,128)}) custom-call(s32[6]{0:T(128)} %stack.23.place, bf16[160,1024]{1,0:T(8,128)(2,1)} %get-tuple-element.64.refs_0_.refs_1_, bf16[336,1024]{1,0:T(8,128)(2,1)} %get-tuple-element.67.refs_1_.refs_2_.refs_3_.refs_4_, bf16[336,1024]{1,0:T(8,128)(2,1)} %get-tuple-element.67.refs_1_.refs_2_.refs_3_.refs_4_), custom_call_target="tpu_custom_call" | custom-call | flops 1000000 | bytes 1000000 | tf_op jit(solution)/shard_map/exchange_keys/attend_own/pallas_call | solution.py:366
  31.8 0.0 collective-permute-done.6.refs_2_
  31.8 0.0 collective-permute-done.4.refs_6_
  31.8 0.0 collective-permute-done.3.refs_7_
  31.9 0.6 collective-permute-start.9
  32.4 0.3 copy-done.12
  32.8 0.2 copy-done.13
  32.9 0.5 collective-permute-start
  33.5 0.2 collective-permute-start.8
  33.7 2.9 %collective-permute-start.7 = (bf16[336,1024]{1,0:T(8,128)(2,1)S(1)}, bf16[336,1024]{1,0:T(8,128)(2,1)}, u32[]{:S(2)}, u32[]{:S(2)}) collective-permute-start(bf16[336,1024]{1,0:T(8,128)(2,1)S(1)} %collective-permute-done.5.refs_2_.refs_5_), channel_id=1, source_target_pairs={{0,8},{1,9},{2,10},{3,11},{4,12},{5,13},{6,14},{7,15},{8,0},{9,1},... | collective-permute-start | bytes 2064392 | tf_op jit(solution)/shard_map/exchange_keys/ppermute | solution.py:39
  36.6 0.5 collective-permute-start.10
  37.1 0.6 reduce-window.6
  37.7 0.2 slice_reduce_fusion
  38.0 0.1 fusion
  38.1 5.2 %collective-permute-done.refs_0_ = bf16[160,1024]{1,0:T(8,128)(2,1)S(1)} collective-permute-done((bf16[160,1024]{1,0:T(8,128)(2,1)}, bf16[160,1024]{1,0:T(8,128)(2,1)S(1)}, u32[]{:S(2)}, u32[]{:S(2)}) %collective-permute-start) | collective-permute-done | bytes 327712 | tf_op jit(solution)/shard_map/exchange_keys/ppermute | solution.py:24
  43.3 0.7 copy-done.8
  44.0 35.2 %attend_near.1 = (f32[4,2,96,512]{3,2,1,0:T(8,128)}, f32[4,2,512]{2,1,0:T(2,128)}) custom-call(s32[6]{0:T(128)} %stack.23.place, bf16[160,1024]{1,0:T(8,128)(2,1)} %copy-done.8, bf16[160,1024]{1,0:T(8,128)(2,1)} %get-tuple-element.64.refs_0_.refs_1_, bf16[336,1024]{1,0:T(8,128)(2,1)} %copy-done.5, ...), custom_call_target="tpu_custom_call" | custom-call | flops 1000000 | bytes 1000000 | tf_op jit(solution)/shard_map/attention/attend_near/pallas_call | solution.py:366
  79.2 0.0 collective-permute-done.8.refs_5_
  79.3 0.0 collective-permute-done.10.refs_3_
  79.3 0.0 collective-permute-done.9.refs_7_
  79.3 0.8 copy-done.11
  80.1 6.8 %attend_far.1 = (bf16[2,160,512]{2,1,0:T(8,128)(2,1)}, bf16[2,160,512]{2,1,0:T(8,128)(2,1)}) custom-call(s32[6]{0:T(128)} %stack.23.place, bf16[160,1024]{1,0:T(8,128)(2,1)} %copy-done.8, bf16[160,1024]{1,0:T(8,128)(2,1)} %get-tuple-element.64.refs_0_.refs_1_, bf16[336,1024]{1,0:T(8,128)(2,1)} %copy-done.5, ...), custom_call_target="tpu_custom_call" | custom-call | flops 1000000 | bytes 1000000 | tf_op jit(solution)/shard_map/attention/attend_far/pallas_call | solution.py:366
  86.9 0.0 copy-start
  87.0 0.0 copy-start.3
  87.0 0.1 collective-permute-start.11
  87.0 0.6 collective-permute-start.14
  87.6 6.4 %load_mixer.1 = (bf16[1280,1280]{1,0:T(8,128)(2,1)S(1)}, bf16[2,1280,1280]{2,1,0:T(8,128)(2,1)S(1)}, bf16[2,1280,1280]{2,1,0:T(8,128)(2,1)S(1)}) custom-call(s32[6]{0:T(128)S(1)} %copy-done.2, bf16[2,160,1280]{2,1,0:T(8,128)(2,1)} %bitcast.35, bf16[2,160,1280]{2,1,0:T(8,128)(2,1)} %copy-done.9, bf16[2,160,1280]{2,1,0:T(8,128)(2,1)} %collective-permute-done.6.refs_2_, ...), custom_call_target="tpu_custom_call" | custom-call | bytes 16000000 | tf_op jit(solution)/shard_map/exchange_context/load_mixer/pallas_call | solution.py:104
  94.0 2.7 %collective-permute-done.11.refs_1_ = bf16[2,160,512]{2,1,0:T(8,128)(2,1)S(1)} collective-permute-done((bf16[2,160,512]{2,1,0:T(8,128)(2,1)}, bf16[2,160,512]{2,1,0:T(8,128)(2,1)S(1)}, u32[]{:S(2)}, u32[]{:S(2)}) %collective-permute-start.11) | collective-permute-done | bytes 327712 | tf_op jit(solution)/shard_map/exchange_context/ppermute | solution.py:24
  96.7 0.5 collective-permute-start.15
  97.2 0.0 collective-permute-start.12
  97.2 0.5 collective-permute-start.13
  97.7 0.0 collective-permute-done.14.refs_4_
  97.7 0.0 collective-permute-start.16
  97.7 7.5 %collective-permute-done.15.refs_5_ = bf16[2,160,512]{2,1,0:T(8,128)(2,1)S(1)} collective-permute-done((bf16[2,160,512]{2,1,0:T(8,128)(2,1)S(1)}, bf16[2,160,512]{2,1,0:T(8,128)(2,1)S(1)}, u32[]{:S(2)}, u32[]{:S(2)}) %collective-permute-start.15) | collective-permute-done | bytes 327712 | tf_op jit(solution)/shard_map/exchange_context/ppermute | solution.py:24
  105.3 1.6 collective-permute-done.17.refs_7_
  106.9 3.8 %mixer.3 = (bf16[128,1280]{1,0:T(8,128)(2,1)S(1)}, f32[128,1280]{1,0:T(8,128)S(1)}) custom-call(s32[6]{0:T(128)S(1)} %copy-done.2, bf16[2,160,512]{2,1,0:T(8,128)(2,1)S(1)} %copy-done.1, bf16[2,160,512]{2,1,0:T(8,128)(2,1)S(1)} %collective-permute-done.11.refs_1_, bf16[2,160,512]{2,1,0:T(8,128)(2,1)S(1)} %collective-permute-done.12.refs_2_, ...), custom_call_target="tpu_custom_call" | custom-call | flops 5000000000 | bytes 20000000 | tf_op jit(solution)/shard_map/mixer/mixer/pallas_call | solution.py:420
  110.7 0.2 collective-permute-start.18
  110.9 0.5 collective-permute-start.20
  111.4 6.4 %mixer.5 = (bf16[256,1280]{1,0:T(8,128)(2,1)S(1)}, f32[256,1280]{1,0:T(8,128)S(1)}) custom-call(s32[6]{0:T(128)S(1)} %copy-done.2, bf16[2,160,512]{2,1,0:T(8,128)(2,1)S(1)} %copy-done.1, bf16[2,160,512]{2,1,0:T(8,128)(2,1)S(1)} %collective-permute-done.11.refs_1_, bf16[2,160,512]{2,1,0:T(8,128)(2,1)S(1)} %collective-permute-done.12.refs_2_, ...), custom_call_target="tpu_custom_call" | custom-call | flops 5000000000 | bytes 20000000 | tf_op jit(solution)/shard_map/mixer/mixer/pallas_call | solution.py:420
  117.8 1.6 collective-permute-start.19
  119.4 4.0 %mixer.4 = (bf16[128,1280]{1,0:T(8,128)(2,1)S(1)}, f32[128,1280]{1,0:T(8,128)S(1)}) custom-call(s32[6]{0:T(128)S(1)} %copy-done.2, bf16[2,160,512]{2,1,0:T(8,128)(2,1)S(1)} %copy-done.1, bf16[2,160,512]{2,1,0:T(8,128)(2,1)S(1)} %collective-permute-done.11.refs_1_, bf16[2,160,512]{2,1,0:T(8,128)(2,1)S(1)} %collective-permute-done.12.refs_2_, ...), custom_call_target="tpu_custom_call" | custom-call | flops 5000000000 | bytes 20000000 | tf_op jit(solution)/shard_map/mixer/mixer/pallas_call | solution.py:420
  123.4 0.0 copy-start.4
  123.4 0.6 collective-permute-start.21
  124.0 2.9 %load_merge.1.weights = bf16[640,5120]{1,0:T(8,128)(2,1)S(1)} custom-call(bf16[320,5120]{1,0:T(8,128)(2,1)} %bitcast.30, bf16[320,5120]{1,0:T(8,128)(2,1)} %collective-permute-done.18.other), custom_call_target="tpu_custom_call" | custom-call | bytes 8000000 | tf_op jit(solution)/shard_map/merge/load_merge/pallas_call | solution.py:129
  127.0 1.6 gather.2.refs_0_
  128.6 6.9 %collective-permute-done.19.received = bf16[256,1280]{1,0:T(8,128)(2,1)S(1)} collective-permute-done((bf16[256,1280]{1,0:T(8,128)(2,1)S(1)}, bf16[256,1280]{1,0:T(8,128)(2,1)S(1)}, u32[]{:S(2)}, u32[]{:S(2)}) %collective-permute-start.19) | collective-permute-done | bytes 655392 | tf_op jit(solution)/shard_map/mixer/ppermute | solution.py:24
  135.5 1.8 %gather.3.earlier = bf16[4,256,1280]{2,1,0:T(8,128)(2,1)S(1)} custom-call(s32[6]{0:T(128)S(1)} %copy-done.2, s32[4,256]{1,0:T(4,128)S(1)} %subtract_bitcast_fusion.index_ref, f32[256,1280]{1,0:T(8,128)S(1)} %get-tuple-element.108.kept, bf16[256,1280]{1,0:T(8,128)(2,1)S(1)} %collective-permute-done.19.received, bf16[1280]{0:T(1024)(128)(2,1)S(1)} %copy-done.4, ...), custom_call_target="tpu_custom_call" | custom-call | flops 1000000000 | bytes 5000000 | tf_op jit(solution)/shard_map/merge/gather/pallas_call | solution.py:461
  137.3 4.7 %collective-permute-done.21.received = bf16[128,1280]{1,0:T(8,128)(2,1)S(1)} collective-permute-done((bf16[128,1280]{1,0:T(8,128)(2,1)S(1)}, bf16[128,1280]{1,0:T(8,128)(2,1)S(1)}, u32[]{:S(2)}, u32[]{:S(2)}) %collective-permute-start.21) | collective-permute-done | bytes 327712 | tf_op jit(solution)/shard_map/mixer/ppermute | solution.py:24
  141.9 3.8 %merge.1 = (f32[256,320]{1,0:T(8,128)S(1)}, f32[256,320]{1,0:T(8,128)S(1)}) custom-call(s32[6]{0:T(128)S(1)} %copy-done.2, s32[4,256]{1,0:T(4,128)S(1)} %subtract_bitcast_fusion.index_ref, f32[128,1280]{1,0:T(8,128)S(1)} %get-tuple-element.113.kept, bf16[128,1280]{1,0:T(8,128)(2,1)S(1)} %collective-permute-done.21.received, bf16[1280]{0:T(1024)(128)(2,1)S(1)} %copy-done.4, ...), custom_call_target="tpu_custom_call" | custom-call | flops 3000000000 | bytes 12000000 | tf_op jit(solution)/shard_map/merge/merge/pallas_call | solution.py:492
  145.8 0.1 collective-permute-start.22
  145.8 1.7 %collective-permute-done.22.received = f32[256,320]{1,0:T(8,128)S(1)} collective-permute-done((f32[256,320]{1,0:T(8,128)S(1)}, f32[256,320]{1,0:T(8,128)S(1)}, u32[]{:S(2)}, u32[]{:S(2)}) %collective-permute-start.22) | collective-permute-done | bytes 327712 | tf_op jit(solution)/shard_map/merge/ppermute | solution.py:24
  147.5 0.3 place.1
  147.8 15.0 %all_to_all.5 = bf16[8,64,320]{2,1,0:T(8,128)(2,1)S(1)} all-to-all(bf16[8,64,320]{2,1,0:T(8,128)(2,1)S(1)} %bitcast.26), channel_id=1, replica_groups=mesh['req'=8,'tp'=4] {'req'}, dimensions={0} | all-to-all | bytes 655360 | tf_op jit(solution)/shard_map/place/all_to_all | solution.py:643
  162.9 0.7 copy.14
  (39 shorter events, 0.1 us)
Async XLA Ops:
  0.0 10.1 %collective-permute-start.1 = (bf16[1280,1280]{1,0:T(8,128)(2,1)}, bf16[1280,1280]{1,0:T(8,128)(2,1)S(1)}, u32[]{:S(2)}, u32[]{:S(2)}) collective-permute-start(bf16[1280,1280]{1,0:T(8,128)(2,1)} %refs_4_.1), channel_id=1, source_target_pairs={{0,1},{1,0},{2,3},{3,2},{4,5},{5,4},{6,7},{7,6},{8,9},{9,8},{10,11... | collective-permute-start | bytes 9830408 | tf_op jit(solution)/shard_map/weights/ppermute | solution.py:24
  0.5 9.6 %collective-permute-start.2 = (bf16[2,160,1280]{2,1,0:T(8,128)(2,1)}, bf16[2,160,1280]{2,1,0:T(8,128)(2,1)S(1)}, u32[]{:S(2)}, u32[]{:S(2)}) collective-permute-start(bf16[2,160,1280]{2,1,0:T(8,128)(2,1)} %bitcast.33), channel_id=1, source_target_pairs={{0,1},{1,0},{2,3},{3,2},{4,5},{5,4},{6,7},{7,6},{8,9},{9,8},{10,11... | collective-permute-start | bytes 2457608 | tf_op jit(solution)/shard_map/weights/ppermute | solution.py:24
  0.5 31.3 %collective-permute-start.6 = (bf16[2,160,1280]{2,1,0:T(8,128)(2,1)}, bf16[2,160,1280]{2,1,0:T(8,128)(2,1)}, u32[]{:S(2)}, u32[]{:S(2)}) collective-permute-start(bf16[2,160,1280]{2,1,0:T(8,128)(2,1)} %bitcast.34), channel_id=1, source_target_pairs={{0,2},{1,3},{2,0},{3,1},{4,6},{5,7},{6,4},{7,5},{8,10},{9,11},{10,... | collective-permute-start | bytes 2457608 | tf_op jit(solution)/shard_map/exchange_keys/ppermute | solution.py:24
  10.1 77.5 %copy-start.9 = (bf16[2,160,1280]{2,1,0:T(8,128)(2,1)}, bf16[2,160,1280]{2,1,0:T(8,128)(2,1)S(1)}, u32[]{:S(2)}) copy-start(bf16[2,160,1280]{2,1,0:T(8,128)(2,1)S(1)} %collective-permute-done.2.refs_1_) | copy-start | bytes 2457604
  10.1 1.7 %copy-start.7 = (bf16[1280,1280]{1,0:T(8,128)(2,1)}, bf16[1280,1280]{1,0:T(8,128)(2,1)S(1)}, u32[]{:S(2)}) copy-start(bf16[1280,1280]{1,0:T(8,128)(2,1)S(1)} %collective-permute-done.1.refs_5_) | copy-start | bytes 9830404
  11.8 20.0 %collective-permute-start.5 = (bf16[336,1024]{1,0:T(8,128)(2,1)}, bf16[336,1024]{1,0:T(8,128)(2,1)S(1)}, u32[]{:S(2)}, u32[]{:S(2)}) collective-permute-start(bf16[336,1024]{1,0:T(8,128)(2,1)} %get-tuple-element.68), channel_id=1, source_target_pairs={{0,4},{4,0},{8,12},{12,8},{16,20},{20,16},{24,28},{28,24},{1,5},{5... | collective-permute-start | bytes 2064392 | tf_op jit(solution)/shard_map/exchange_keys/ppermute | solution.py:24
  13.3 18.5 %collective-permute-start.4 = (bf16[336,1024]{1,0:T(8,128)(2,1)}, bf16[336,1024]{1,0:T(8,128)(2,1)S(1)}, u32[]{:S(2)}, u32[]{:S(2)}) collective-permute-start(bf16[336,1024]{1,0:T(8,128)(2,1)} %get-tuple-element.67.refs_1_.refs_2_.refs_3_.refs_4_), channel_id=1, source_target_pairs={{0,8},{1,9},{2,10},{3,11},{4,12},{5,13},{6,14},{7,15},{8,0},{9,1},... | collective-permute-start | bytes 2064392 | tf_op jit(solution)/shard_map/exchange_keys/ppermute | solution.py:39
  14.9 17.0 %collective-permute-start.3 = (bf16[336,1024]{1,0:T(8,128)(2,1)}, bf16[336,1024]{1,0:T(8,128)(2,1)S(1)}, u32[]{:S(2)}, u32[]{:S(2)}) collective-permute-start(bf16[336,1024]{1,0:T(8,128)(2,1)} %get-tuple-element.67.refs_1_.refs_2_.refs_3_.refs_4_), channel_id=1, source_target_pairs={{0,1},{1,0},{2,3},{3,2},{4,5},{5,4},{6,7},{7,6},{8,16},{9,17},{10,... | collective-permute-start | bytes 2064392 | tf_op jit(solution)/shard_map/exchange_keys/ppermute | solution.py:39
  14.9 22.2 %copy-start.14 = (s32[256,1]{0,1:T(1,128)S(1)}, s32[256,1]{0,1:T(1,128)}, u32[]{:S(2)}) copy-start(s32[256,1]{0,1:T(1,128)} %param.23) | copy-start | bytes 3076
  14.9 23.2 %copy-start.15 = (s32[256,4]{0,1:T(4,128)S(1)}, s32[256,4]{0,1:T(4,128)}, u32[]{:S(2)}) copy-start(s32[256,4]{0,1:T(4,128)} %param.22) | copy-start | bytes 12292
  31.8 11.5 %copy-start.5 = (bf16[336,1024]{1,0:T(8,128)(2,1)}, bf16[336,1024]{1,0:T(8,128)(2,1)S(1)}, u32[]{:S(2)}) copy-start(bf16[336,1024]{1,0:T(8,128)(2,1)S(1)} %collective-permute-done.5.refs_2_.refs_5_) | copy-start | bytes 2064388
  31.8 0.9 copy-start.12
  31.8 1.1 copy-start.13
  31.9 47.4 %collective-permute-start.9 = (bf16[1280,1280]{1,0:T(8,128)(2,1)}, bf16[1280,1280]{1,0:T(8,128)(2,1)}, u32[]{:S(2)}, u32[]{:S(2)}) collective-permute-start(bf16[1280,1280]{1,0:T(8,128)(2,1)} %refs_6_.1), channel_id=1, source_target_pairs={{0,1},{1,0},{2,3},{3,2},{4,5},{5,4},{6,7},{7,6},{8,9},{9,8},{10,11... | collective-permute-start | bytes 9830408 | tf_op jit(solution)/shard_map/exchange_keys/ppermute | solution.py:24
  32.9 10.3 %collective-permute-start = (bf16[160,1024]{1,0:T(8,128)(2,1)}, bf16[160,1024]{1,0:T(8,128)(2,1)S(1)}, u32[]{:S(2)}, u32[]{:S(2)}) collective-permute-start(bf16[160,1024]{1,0:T(8,128)(2,1)} %get-tuple-element.62), channel_id=1, source_target_pairs={{0,4},{4,0},{8,12},{12,8},{16,20},{20,16},{24,28},{28,24},{1,5},{5... | collective-permute-start | bytes 983048 | tf_op jit(solution)/shard_map/exchange_keys/ppermute | solution.py:24
  33.5 45.8 %collective-permute-start.8 = (bf16[336,1024]{1,0:T(8,128)(2,1)S(1)}, bf16[336,1024]{1,0:T(8,128)(2,1)S(1)}, u32[]{:S(2)}, u32[]{:S(2)}) collective-permute-start(bf16[336,1024]{1,0:T(8,128)(2,1)S(1)} %collective-permute-done.5.refs_2_.refs_5_), channel_id=1, source_target_pairs={{0,1},{1,0},{2,3},{3,2},{4,5},{5,4},{6,7},{7,6},{8,16},{9,17},{10,... | collective-permute-start | bytes 2064392 | tf_op jit(solution)/shard_map/exchange_keys/ppermute | solution.py:39
  33.7 45.6 %collective-permute-start.7 = (bf16[336,1024]{1,0:T(8,128)(2,1)S(1)}, bf16[336,1024]{1,0:T(8,128)(2,1)}, u32[]{:S(2)}, u32[]{:S(2)}) collective-permute-start(bf16[336,1024]{1,0:T(8,128)(2,1)S(1)} %collective-permute-done.5.refs_2_.refs_5_), channel_id=1, source_target_pairs={{0,8},{1,9},{2,10},{3,11},{4,12},{5,13},{6,14},{7,15},{8,0},{9,1},... | collective-permute-start | bytes 2064392 | tf_op jit(solution)/shard_map/exchange_keys/ppermute | solution.py:39
  36.6 42.6 %collective-permute-start.10 = (bf16[2,160,1280]{2,1,0:T(8,128)(2,1)S(1)}, bf16[2,160,1280]{2,1,0:T(8,128)(2,1)S(1)}, u32[]{:S(2)}, u32[]{:S(2)}) collective-permute-start(bf16[2,160,1280]{2,1,0:T(8,128)(2,1)S(1)} %collective-permute-done.2.refs_1_), channel_id=1, source_target_pairs={{0,2},{1,3},{2,0},{3,1},{4,6},{5,7},{6,4},{7,5},{8,10},{9,11},{10,... | collective-permute-start | bytes 2457608 | tf_op jit(solution)/shard_map/exchange_keys/ppermute | solution.py:24
  43.3 0.7 copy-start.8
  79.2 8.4 %copy-start.2 = (s32[6]{0:T(128)S(1)}, s32[6]{0:T(128)}, u32[]{:S(2)}) copy-start(s32[6]{0:T(128)} %stack.23.place) | copy-start | bytes 76
  79.2 0.9 copy-start.11
  79.3 8.3 %copy-start.10 = (bf16[2,160,1280]{2,1,0:T(8,128)(2,1)}, bf16[2,160,1280]{2,1,0:T(8,128)(2,1)S(1)}, u32[]{:S(2)}) copy-start(bf16[2,160,1280]{2,1,0:T(8,128)(2,1)S(1)} %collective-permute-done.10.refs_3_) | copy-start | bytes 2457604
  86.9 10.3 %copy-start.1 = (bf16[2,160,512]{2,1,0:T(8,128)(2,1)S(1)}, bf16[2,160,512]{2,1,0:T(8,128)(2,1)}, u32[]{:S(2)}) copy-start(bf16[2,160,512]{2,1,0:T(8,128)(2,1)} %get-tuple-element.87.refs_0_) | copy-start | bytes 983044
  86.9 20.0 %copy-start = (bf16[1024,1280]{1,0:T(8,128)(2,1)S(1)}, bf16[1024,1280]{1,0:T(8,128)(2,1)}, u32[]{:S(2)}) copy-start(bf16[1024,1280]{1,0:T(8,128)(2,1)} %refs_8_.5) | copy-start | bytes 7864324
  87.0 19.9 %copy-start.3 = (bf16[1280]{0:T(1024)(128)(2,1)S(1)}, bf16[1280]{0:T(1024)(128)(2,1)}, u32[]{:S(2)}) copy-start(bf16[1280]{0:T(1024)(128)(2,1)} %refs_9_.5) | copy-start | bytes 7684
  87.0 9.7 %collective-permute-start.11 = (bf16[2,160,512]{2,1,0:T(8,128)(2,1)}, bf16[2,160,512]{2,1,0:T(8,128)(2,1)S(1)}, u32[]{:S(2)}, u32[]{:S(2)}) collective-permute-start(bf16[2,160,512]{2,1,0:T(8,128)(2,1)} %get-tuple-element.88), channel_id=1, source_target_pairs={{0,4},{4,0},{8,12},{12,8},{16,20},{20,16},{24,28},{28,24},{1,5},{5... | collective-permute-start | bytes 983048 | tf_op jit(solution)/shard_map/exchange_context/ppermute | solution.py:24
  87.0 10.7 %collective-permute-start.14 = (bf16[2,160,512]{2,1,0:T(8,128)(2,1)}, bf16[2,160,512]{2,1,0:T(8,128)(2,1)S(1)}, u32[]{:S(2)}, u32[]{:S(2)}) collective-permute-start(bf16[2,160,512]{2,1,0:T(8,128)(2,1)} %get-tuple-element.87.refs_0_), channel_id=1, source_target_pairs={{0,2},{1,3},{2,0},{3,1},{4,6},{5,7},{6,4},{7,5},{8,10},{9,11},{10,... | collective-permute-start | bytes 983048 | tf_op jit(solution)/shard_map/exchange_context/ppermute | solution.py:24
  96.7 14.0 %copy-start.6 = (bf16[5120,320]{0,1:T(8,128)(2,1)S(1)}, bf16[5120,320]{0,1:T(8,128)(2,1)}, u32[]{:S(2)}) copy-start(bf16[5120,320]{0,1:T(8,128)(2,1)} %param.21) | copy-start | bytes 9830404
  96.7 8.6 %collective-permute-start.15 = (bf16[2,160,512]{2,1,0:T(8,128)(2,1)S(1)}, bf16[2,160,512]{2,1,0:T(8,128)(2,1)S(1)}, u32[]{:S(2)}, u32[]{:S(2)}) collective-permute-start(bf16[2,160,512]{2,1,0:T(8,128)(2,1)S(1)} %collective-permute-done.11.refs_1_), channel_id=1, source_target_pairs={{0,2},{1,3},{2,0},{3,1},{4,6},{5,7},{6,4},{7,5},{8,10},{9,11},{10,... | collective-permute-start | bytes 983048 | tf_op jit(solution)/shard_map/exchange_context/ppermute | solution.py:24
  97.2 8.1 %collective-permute-start.12 = (bf16[2,160,512]{2,1,0:T(8,128)(2,1)S(1)}, bf16[2,160,512]{2,1,0:T(8,128)(2,1)S(1)}, u32[]{:S(2)}, u32[]{:S(2)}) collective-permute-start(bf16[2,160,512]{2,1,0:T(8,128)(2,1)S(1)} %copy-done.1), channel_id=1, source_target_pairs={{0,1},{1,0},{2,3},{3,2},{4,5},{5,4},{6,7},{7,6},{8,9},{9,8},{10,11... | collective-permute-start | bytes 983048 | tf_op jit(solution)/shard_map/exchange_context/ppermute | solution.py:24
  97.2 8.1 %collective-permute-start.13 = (bf16[2,160,512]{2,1,0:T(8,128)(2,1)S(1)}, bf16[2,160,512]{2,1,0:T(8,128)(2,1)S(1)}, u32[]{:S(2)}, u32[]{:S(2)}) collective-permute-start(bf16[2,160,512]{2,1,0:T(8,128)(2,1)S(1)} %collective-permute-done.11.refs_1_), channel_id=1, source_target_pairs={{0,1},{1,0},{2,3},{3,2},{4,5},{5,4},{6,7},{7,6},{8,9},{9,8},{10,11... | collective-permute-start | bytes 983048 | tf_op jit(solution)/shard_map/exchange_context/ppermute | solution.py:24
  97.7 7.6 %collective-permute-start.16 = (bf16[2,160,512]{2,1,0:T(8,128)(2,1)S(1)}, bf16[2,160,512]{2,1,0:T(8,128)(2,1)S(1)}, u32[]{:S(2)}, u32[]{:S(2)}) collective-permute-start(bf16[2,160,512]{2,1,0:T(8,128)(2,1)S(1)} %collective-permute-done.14.refs_4_), channel_id=1, source_target_pairs={{0,1},{1,0},{2,3},{3,2},{4,5},{5,4},{6,7},{7,6},{8,9},{9,8},{10,11... | collective-permute-start | bytes 983048 | tf_op jit(solution)/shard_map/exchange_context/ppermute | solution.py:24
  105.3 1.6 collective-permute-start.17
  110.7 13.3 %collective-permute-start.18 = (bf16[320,5120]{1,0:T(8,128)(2,1)S(1)}, bf16[320,5120]{1,0:T(8,128)(2,1)}, u32[]{:S(2)}, u32[]{:S(2)}) collective-permute-start(bf16[320,5120]{1,0:T(8,128)(2,1)S(1)} %bitcast.31), channel_id=1, source_target_pairs={{0,1},{1,0},{2,3},{3,2},{4,5},{5,4},{6,7},{7,6},{8,9},{9,8},{10,11... | collective-permute-start | bytes 9830408 | tf_op jit(solution)/shard_map/mixer/ppermute | solution.py:24
  110.9 16.1 %collective-permute-start.20 = (bf16[128,1280]{1,0:T(8,128)(2,1)S(1)}, bf16[128,1280]{1,0:T(8,128)(2,1)S(1)}, u32[]{:S(2)}, u32[]{:S(2)}) collective-permute-start(bf16[128,1280]{1,0:T(8,128)(2,1)S(1)} %get-tuple-element.101), channel_id=1, source_target_pairs={{0,2},{1,3},{2,0},{3,1},{4,6},{5,7},{6,4},{7,5},{8,10},{9,11},{10,... | collective-permute-start | bytes 983048 | tf_op jit(solution)/shard_map/mixer/ppermute | solution.py:24
  117.8 17.7 %collective-permute-start.19 = (bf16[256,1280]{1,0:T(8,128)(2,1)S(1)}, bf16[256,1280]{1,0:T(8,128)(2,1)S(1)}, u32[]{:S(2)}, u32[]{:S(2)}) collective-permute-start(bf16[256,1280]{1,0:T(8,128)(2,1)S(1)} %get-tuple-element.109), channel_id=1, source_target_pairs={{0,2},{1,3},{2,0},{3,1},{4,6},{5,7},{6,4},{7,5},{8,10},{9,11},{10,... | collective-permute-start | bytes 1966088 | tf_op jit(solution)/shard_map/mixer/ppermute | solution.py:24
  123.4 3.5 %copy-start.4 = (bf16[1280]{0:T(1024)(128)(2,1)S(1)}, bf16[1280]{0:T(1024)(128)(2,1)}, u32[]{:S(2)}) copy-start(bf16[1280]{0:T(1024)(128)(2,1)} %gain_ref.9) | copy-start | bytes 7684
  123.4 18.5 %collective-permute-start.21 = (bf16[128,1280]{1,0:T(8,128)(2,1)S(1)}, bf16[128,1280]{1,0:T(8,128)(2,1)S(1)}, u32[]{:S(2)}, u32[]{:S(2)}) collective-permute-start(bf16[128,1280]{1,0:T(8,128)(2,1)S(1)} %get-tuple-element.105), channel_id=1, source_target_pairs={{0,2},{1,3},{2,0},{3,1},{4,6},{5,7},{6,4},{7,5},{8,10},{9,11},{10,... | collective-permute-start | bytes 983048 | tf_op jit(solution)/shard_map/mixer/ppermute | solution.py:24
  145.8 1.8 %collective-permute-start.22 = (f32[256,320]{1,0:T(8,128)S(1)}, f32[256,320]{1,0:T(8,128)S(1)}, u32[]{:S(2)}, u32[]{:S(2)}) collective-permute-start(f32[256,320]{1,0:T(8,128)S(1)} %get-tuple-element.118), channel_id=1, source_target_pairs={{0,1},{1,0},{2,3},{3,2},{4,5},{5,4},{6,7},{7,6},{8,9},{9,8},{10,11... | collective-permute-start | bytes 983048 | tf_op jit(solution)/shard_map/merge/ppermute | solution.py:24

commit v3 on v2

--- a/solution.py
+++ b/solution.py
@@ -192,199 +192,163 @@
     return jnp.max(jnp.maximum(squares[0], squares[1]))
 
 
-def attend_kernel(groups, blocks, flags, resumed, skip, last, place, *refs):
+def attend_kernel(blocks, flags, resumed, skips, last, place, *refs):
+    groups = len(resumed)
     q_refs, number_refs, refs = refs[:groups], refs[groups : 2 * groups], refs[2 * groups :]
     kv_refs, refs = refs[:blocks], refs[blocks:]
-    if resumed:
-        acc_in, peak_in, refs = refs[0], refs[1], refs[2:]
-    if last:
-        ctx_out, refs = refs[:groups], refs[groups:]
-    else:
-        acc_out, peak_out, refs = refs[0], refs[1], refs[2:]
+    state_refs = []
+    for old in resumed:
+        state_refs.append(refs[:2] if old else None)
+        refs = refs[2:] if old else refs
+    outs, refs = refs[: groups * (1 if last else 2)], refs[groups * (1 if last else 2) :]
     keys, values, columns, acc, peak, bounds, plain = refs
     tiles_of = kv_refs[0].shape[1] // TILE
     tiles = blocks * tiles_of
     tall = kv_refs[0].shape[0] - SEGMENT_ROWS
-    steps_of = kv_refs[0].shape[1] // TILE
-    j = pl.program_id(0)
-    fresh = steps_of * groups - resumed
-
-    @pl.when(j == 0)
-    def _():
-        for b in range(blocks):
-            for t in range(tiles_of):
-                n = b * tiles_of + t
-                at = slice(t * TILE, (t + 1) * TILE)
-                for h in range(2):
-                    block = kv_refs[b][h * HD : (h + 1) * HD, at].astype(jnp.float32)
-                    keys[n, h] = jnp.transpose(block).astype(jnp.bfloat16)
-                    values[n, h, :HD] = kv_refs[b][(2 + h) * HD : (3 + h) * HD, at]
-                    values[n, h, HD:] = jnp.ones((VROWS - HD, TILE), jnp.bfloat16)
-                number = numbers_of(kv_refs[b].at[tall:], at)
-                low, high = jnp.min(number), jnp.max(number)
-                if b in flags:
-                    low = jnp.where(place[flags[b]] == 1, -1.0, low)
-                    high = jnp.where(place[flags[b]] == 1, -1.0, high)
-                bounds[3 * n] = low
-                bounds[3 * n + 1] = high
-                bounds[3 * n + 2] = largest_norm(kv_refs[b][:HD, at], kv_refs[b][HD : 2 * HD, at])
-                columns[n] = jnp.transpose(jnp.broadcast_to(number, (128, TILE)))
-
-    def go_on():
-        acc[...] = acc_in[0]
-        peak[...] = peak_in[0]
-        plain[0] = (jnp.max(jnp.abs(peak_in[0])) == 0.0).astype(jnp.int32)
-
-    def start():
-        acc[...] = jnp.zeros_like(acc)
-        peak[...] = jnp.zeros_like(peak)
-        plain[0] = 1
-
-    if fresh:
-        pl.when(j < fresh)(start)
-    if resumed:
-        pl.when(j >= fresh)(go_on)
-
-    q_row = numbers_of(number_refs[0], slice(0, TILE))
-    queries = q_refs[0][...]
-    if groups > 1:
-        q_row = jnp.where(j < steps_of, q_row, numbers_of(number_refs[1], slice(0, TILE)))
-        queries = jnp.where(j < steps_of, queries, q_refs[1][...])
-    q_low, q_high = jnp.min(q_row), jnp.max(q_row)
-    q_norm = largest_norm(queries[:HD], queries[HD:])
-
-    def scores_of(t, h, at, matches):
-        scores = dot(keys[t, h], queries[h * HD : (h + 1) * HD, at], NN)
-        return scores if matches is None else jnp.where(matches, scores, MASKED)
-
-    def matches_of(t, at):
-        column = columns[t]
-        return jnp.concatenate([column] * (LANES // 128), axis=1) == q_row[:, at]
+
+    for b in range(blocks):
+        for t in range(tiles_of):
+            n = b * tiles_of + t
+            at = slice(t * TILE, (t + 1) * TILE)
+            for h in range(2):
+                block = kv_refs[b][h * HD : (h + 1) * HD, at].astype(jnp.float32)
+                keys[n, h] = jnp.transpose(block).astype(jnp.bfloat16)
+                values[n, h, :HD] = kv_refs[b][(2 + h) * HD : (3 + h) * HD, at]
+                values[n, h, HD:] = jnp.ones((VROWS - HD, TILE), jnp.bfloat16)
+            number = numbers_of(kv_refs[b].at[tall:], at)
+            low, high = jnp.min(number), jnp.max(number)
+            if b in flags:
+                low = jnp.where(place[flags[b]] == 1, -1.0, low)
+                high = jnp.where(place[flags[b]] == 1, -1.0, high)
+            bounds[3 * n] = low
+            bounds[3 * n + 1] = high
+            bounds[3 * n + 2] = largest_norm(kv_refs[b][:HD, at], kv_refs[b][HD : 2 * HD, at])
+            columns[n] = jnp.transpose(jnp.broadcast_to(number, (128, TILE)))
 
     units = [(slice(c, c + LANES), h) for c in range(0, TILE, LANES) for h in range(2)]
 
-    def unshifted(t, masked):
-        scores, probs, matches = {}, {}, None
-        for i in range(len(units) + AHEAD + 1):
-            if i < len(units):
-                at, h = units[i]
-                if masked and h == 0:
-                    matches = matches_of(t, at)
-                scores[i] = scores_of(t, h, at, matches)
-            if 0 <= i - AHEAD < len(units):
-                probs[i - AHEAD] = jnp.exp(scores.pop(i - AHEAD) * FACTOR).astype(jnp.bfloat16)
-            if 0 <= i - AHEAD - 1 < len(units):
-                at, h = units[i - AHEAD - 1]
-                acc[h, :, at] += dot(values[t, h], probs.pop(i - AHEAD - 1), NN)
-
-    def shifted_by_peak(t):
-        for at, h in units:
-            scores = scores_of(t, h, at, matches_of(t, at))
-            old = jnp.where(acc[h, HD : HD + 1, at] > 0.0, peak[h : h + 1, at], START)
-            new = jnp.maximum(old, jnp.max(scores, axis=0, keepdims=True))
-            probs = jnp.exp((scores - new) * FACTOR).astype(jnp.bfloat16)
-            shrink = jnp.exp((old - new) * FACTOR)
-            peak[h : h + 1, at] = new
-            acc[h, :, at] = acc[h, :, at] * shrink + dot(values[t, h], probs, NN)
-        plain[0] = 0
-
-    def visit(t, carry):
-        k_low, k_high = bounds[3 * t], bounds[3 * t + 1]
-        touches = (k_high >= q_low) & (k_low <= q_high)
-        whole = (k_low == k_high) & (q_low == q_high)
-        small = (plain[0] == 1) & (q_norm * bounds[3 * t + 2] <= SMALL * SMALL * HD)
-
-        @pl.when(touches & small & whole)
-        def _():
-            unshifted(t, False)
-
-        @pl.when(touches & small & jnp.logical_not(whole))
-        def _():
-            unshifted(t, True)
-
-        @pl.when(touches & jnp.logical_not(small))
-        def _():
-            shifted_by_peak(t)
-
-        return carry
-
-    lax.fori_loop(jnp.where(j >= fresh, skip, 0), tiles, visit, 0)
-    if last:
-
-        def finish(out):
+    def attend_tile(g, j):
+        if resumed[g]:
+            acc[...] = state_refs[g][0][j]
+            peak[...] = state_refs[g][1][j]
+            plain[0] = (jnp.max(jnp.abs(state_refs[g][1][j])) == 0.0).astype(jnp.int32)
+        else:
+            acc[...] = jnp.zeros_like(acc)
+            peak[...] = jnp.zeros_like(peak)
+            plain[0] = 1
+        mine = pl.ds(pl.multiple_of((j ^ place[1]) * TILE, TILE), TILE)
+        q_row = numbers_of(number_refs[g].at[tall:], mine)
+        queries = q_refs[g][:, mine]
+        q_low, q_high = jnp.min(q_row), jnp.max(q_row)
+        q_norm = largest_norm(queries[:HD], queries[HD:])
+
+        def scores_of(t, h, at, matches):
+            scores = dot(keys[t, h], queries[h * HD : (h + 1) * HD, at], NN)
+            return scores if matches is None else jnp.where(matches, scores, MASKED)
+
+        def matches_of(t, at):
+            column = columns[t]
+            return jnp.concatenate([column] * (LANES // 128), axis=1) == q_row[:, at]
+
+        def unshifted(t, masked):
+            scores, probs, matches = {}, {}, None
+            for i in range(len(units) + AHEAD + 1):
+                if i < len(units):
+                    at, h = units[i]
+                    if masked and h == 0:
+                        matches = matches_of(t, at)
+                    scores[i] = scores_of(t, h, at, matches)
+                if 0 <= i - AHEAD < len(units):
+                    probs[i - AHEAD] = jnp.exp(scores.pop(i - AHEAD) * FACTOR).astype(jnp.bfloat16)
+                if 0 <= i - AHEAD - 1 < len(units):
+                    at, h = units[i - AHEAD - 1]
+                    acc[h, :, at] += dot(values[t, h], probs.pop(i - AHEAD - 1), NN)
+
+        def shifted_by_peak(t):
+            for at, h in units:
+                scores = scores_of(t, h, at, matches_of(t, at))
+                old = jnp.where(acc[h, HD : HD + 1, at] > 0.0, peak[h : h + 1, at], START)
+                new = jnp.maximum(old, jnp.max(scores, axis=0, keepdims=True))
+                probs = jnp.exp((scores - new) * FACTOR).astype(jnp.bfloat16)
+                shrink = jnp.exp((old - new) * FACTOR)
+                peak[h : h + 1, at] = new
+                acc[h, :, at] = acc[h, :, at] * shrink + dot(values[t, h], probs, NN)
+            plain[0] = 0
+
+        def visit(t, carry):
+            k_low, k_high = bounds[3 * t], bounds[3 * t + 1]
+            touches = (k_high >= q_low) & (k_low <= q_high)
+            whole = (k_low == k_high) & (q_low == q_high)
+            small = (plain[0] == 1) & (q_norm * bounds[3 * t + 2] <= SMALL * SMALL * HD)
+
+            @pl.when(touches & small & whole)
+            def _():
+                unshifted(t, False)
+
+            @pl.when(touches & small & jnp.logical_not(whole))
+            def _():
+                unshifted(t, True)
+
+            @pl.when(touches & jnp.logical_not(small))
+            def _():
+                shifted_by_peak(t)
+
+            return carry
+
+        lax.fori_loop(skips[g] * tiles_of, tiles, visit, 0)
+        if last:
             for h in range(2):
                 at = slice(h * HD, (h + 1) * HD)
-                out[0, at, :] = (acc[h, :HD] / acc[h, HD : HD + 1]).astype(jnp.bfloat16)
-
-        for g in range(groups):
-            pl.when(j // steps_of == g)(functools.partial(finish, ctx_out[g]))
-    else:
-        acc_out[0] = acc[...]
-        peak_out[0] = peak[...]
-
-
-def attend(place, queries, numbers, key_values, name, flags={}, state=None, skip=0, last=False):
+                outs[g][j, at, :] = (acc[h, :HD] / acc[h, HD : HD + 1]).astype(jnp.bfloat16)
+        else:
+            outs[2 * g][j] = acc[...]
+            outs[2 * g + 1][j] = peak[...]
+
+    for g in range(groups):
+
+        def step(j, carry, g=g):
+            attend_tile(g, j)
+            return carry
+
+        lax.fori_loop(0, tiles_of, step, 0)
+
+
+def attend(place, queries, numbers, key_values, name, flags, states, skips, last=False):
     half, rows = queries[0].shape
     groups, blocks = len(queries), len(key_values)
-    steps_of = rows // TILE
-    steps = groups * steps_of
-    tiles = blocks * steps_of
-    tall = numbers[0].shape[0] - SEGMENT_ROWS
-    resumed = 0 if state is None else state[0].shape[0]
-    whole = lambda a: pl.BlockSpec(a.shape, lambda j, s: (0,) * a.ndim)
+    tiles_of = rows // TILE
+    tiles = blocks * tiles_of
     acc_shape, peak_shape = (2, VROWS, TILE), (2, TILE)
-    q_spec = pl.BlockSpec((half, TILE), lambda j, s: (0, (j % steps_of) ^ s[1]))
-    number_spec = pl.BlockSpec(
-        (SEGMENT_ROWS, TILE), lambda j, s: (tall // SEGMENT_ROWS, (j % steps_of) ^ s[1])
-    )
-    in_specs = [q_spec] * groups + [number_spec] * groups + [whole(kv) for kv in key_values]
     operands = [*queries, *numbers, *key_values]
-    if state is not None:
-        behind = steps - resumed
-        in_specs += [
-            pl.BlockSpec((1,) + acc_shape, lambda j, s: (jnp.maximum(j - behind, 0), 0, 0, 0)),
-            pl.BlockSpec((1,) + peak_shape, lambda j, s: (jnp.maximum(j - behind, 0), 0, 0)),
-        ]
-        operands += list(state)
+    for state in states:
+        operands += [] if state is None else list(state)
     if last:
-        out_specs = [
-            pl.BlockSpec(
-                (1, half, TILE), lambda j, s, g=g: (jnp.clip(j - g * steps_of, 0, steps_of - 1), 0, 0)
-            )
-            for g in range(groups)
-        ]
-        out_shape = [jax.ShapeDtypeStruct((steps_of, half, TILE), jnp.bfloat16)] * groups
+        out_shape = [pltpu.VMEM((tiles_of, half, TILE), jnp.bfloat16)] * groups
     else:
-        out_specs = [
-            pl.BlockSpec((1,) + acc_shape, lambda j, s: (j, 0, 0, 0)),
-            pl.BlockSpec((1,) + peak_shape, lambda j, s: (j, 0, 0)),
-        ]
         out_shape = [
-            jax.ShapeDtypeStruct((steps,) + acc_shape, jnp.float32),
-            jax.ShapeDtypeStruct((steps,) + peak_shape, jnp.float32),
-        ]
-    return pl.pallas_call(
-        functools.partial(attend_kernel, groups, blocks, flags, resumed, skip, last),
-        grid_spec=pltpu.PrefetchScalarGridSpec(
-            num_scalar_prefetch=1,
-            grid=(steps,),
-            in_specs=in_specs,
-            out_specs=out_specs,
-            scratch_shapes=[
-                pltpu.VMEM((tiles, 2, TILE, HD), jnp.bfloat16),
-                pltpu.VMEM((tiles, 2, VROWS, TILE), jnp.bfloat16),
-                pltpu.VMEM((tiles, TILE, 128), jnp.float32),
-                pltpu.VMEM(acc_shape, jnp.float32),
-                pltpu.VMEM(peak_shape, jnp.float32),
-                pltpu.SMEM((3 * tiles,), jnp.float32),
-                pltpu.SMEM((1,), jnp.int32),
-            ],
-        ),
+            pltpu.VMEM((tiles_of,) + acc_shape, jnp.float32),
+            pltpu.VMEM((tiles_of,) + peak_shape, jnp.float32),
+        ] * groups
+    resumed = [state is not None for state in states]
+    out = pl.pallas_call(
+        functools.partial(attend_kernel, blocks, flags, resumed, skips, last),
+        in_specs=[SCALARS] + [RESIDENT] * len(operands),
+        out_specs=[RESIDENT] * len(out_shape),
         out_shape=out_shape,
-        compiler_params=vmem(),
+        scratch_shapes=[
+            pltpu.VMEM((tiles, 2, TILE, HD), jnp.bfloat16),
+            pltpu.VMEM((tiles, 2, VROWS, TILE), jnp.bfloat16),
+            pltpu.VMEM((tiles, TILE, 128), jnp.float32),
+            pltpu.VMEM(acc_shape, jnp.float32),
+            pltpu.VMEM(peak_shape, jnp.float32),
+            pltpu.SMEM((3 * tiles,), jnp.float32),
+            pltpu.SMEM((1,), jnp.int32),
+        ],
+        compiler_params=vmem(24),
         cost_estimate=pl.CostEstimate(flops=1_000_000, bytes_accessed=1_000_000, transcendentals=0),
         name=name,
-    )(place, *operands)
+    )(place, *[in_vmem(a) for a in operands])
+    return list(out) if last else [out[2 * g : 2 * g + 2] for g in range(groups)]
 
 
 def mixer_kernel(first, which, place, *refs):
@@ -554,7 +518,7 @@
         wo_across = swap(wo_own, "tp", 2)
         q_own, q_send = project(tokens, numbers, attend_gain, weight, (0,), "project_queries")
         q_peer = swap(q_send, "req", 1)
-        state = attend(place, [q_own], [kv_own], [kv_own], "attend_own")
+        (state,) = attend(place, [q_own], [kv_own], [kv_own], "attend_own", {}, [None], [0])
         kv_odd, kv_even, kv_peer, state, wo_across, late_reduce, late_wo = tie(
             (kv_odd, kv_even, kv_peer, state, wo_across, reduce_weight, wo_core)
         )
@@ -576,13 +540,16 @@
     with jax.named_scope("attention"):
         queries, numbers = [q_peer, q_own], [kv_peer, kv_own]
         near = [kv_own, kv_peer, kv_even, kv_odd]
-        state = attend(place, queries, numbers, near, "attend_near", {2: 4, 3: 5}, state, rows // TILE)
-        state, kv_even_peer, kv_odd_peer, reduce_other, wo_both = tie(
-            (state, kv_even_peer, kv_odd_peer, reduce_other, wo_both)
+        states = [None, state]
+        states = attend(
+            place, queries, numbers, near, "attend_near", {2: 4, 3: 5}, states, [0, 1]
+        )
+        states, kv_even_peer, kv_odd_peer, reduce_other, wo_both = tie(
+            (states, kv_even_peer, kv_odd_peer, reduce_other, wo_both)
         )
         far = [kv_even_peer, kv_odd_peer]
         for_peer, context = attend(
-            place, queries, numbers, far, "attend_far", {0: 4, 1: 5}, state, last=True
+            place, queries, numbers, far, "attend_far", {0: 4, 1: 5}, states, [0, 0], True
         )
 
     with jax.named_scope("exchange_context"):

time: 162 us -> 160 us (0.988); the launches traced: 164 us -> 159 us
  Pallas kernels: 95.8 us -> 85.5 us
  blocking collectives: 15 us -> 22.4 us
  waiting for transfers between devices: 30.3 us -> 28.2 us
    pallas_call x3, Pallas kernels: 52.7 us -> 42 us  [attend(): pl.pallas_call(functools.partial(attend_kernel, blocks, flags, resumed, s...]
    all_to_all x1, blocking collectives: 15 us -> 22.4 us  [body(): lax.all_to_all(outgoing, 'req', split_axis=0, concat_axis=0, tiled=True)]
    ppermute x19, waiting for transfers between devices: 30.3 us -> 27.9 us  [swap(): lax.ppermute(block, axis, [(i, i ^ flip) for i in range(lax.axis_size(axi...]
    unnamed x33 -> x25, local copies, waits for them, and re-layouts: 4.57 us -> 4.7 us
  transfers between devices with their start and end apart: 23 -> 23, of which waited for: 7 -> 8; matrix products, arithmetic and copies ran while one was open for 1% -> 1% of each run, Pallas kernels for 50% -> 46%
where the time goes in v3:
time: 160 us; the launch traced here: 159 us
  Pallas kernels  85.5 us (53%)
  waiting for transfers between devices  28.2 us (18%)
  blocking collectives  22.4 us (14%)
  starting transfers between devices  17 us (11%)
  local copies, waits for them, and re-layouts  5 us (3%)
    pallas_call x3, Pallas kernels, attend(): pl.pallas_call(functools.partial(attend_kernel, blocks, flags, resumed, s...  42 us
    ppermute x19, waiting for transfers between devices, swap(): lax.ppermute(block, axis, [(i, i ^ flip) for i in range(lax.axis_size(axi...  27.9 us
    all_to_all x1, blocking collectives, body(): lax.all_to_all(outgoing, 'req', split_axis=0, concat_axis=0, tiled=True)  22.4 us
    pallas_call x3, Pallas kernels, mixer(): pl.pallas_call(functools.partial(mixer_kernel, first, [which for _, which...  14.5 us
    pallas_call x2, Pallas kernels, project(): pl.pallas_call(functools.partial(project_kernel, len(parts)), grid=(rows...  12.2 us
    ppermute x19, starting transfers between devices, swap(): lax.ppermute(block, axis, [(i, i ^ flip) for i in range(lax.axis_size(axi...  11.9 us
    pallas_call x1, Pallas kernels, load_mixer(): pl.pallas_call(load_mixer_kernel, in_specs=[SCALARS] + [ANYWHERE] * 8, ou...  6.4 us
    ppermute x4, starting transfers between devices, swap_pairs(): return lax.ppermute(block, ('req', 'tp'), route)  5.06 us
  transfers between devices with their start and end apart: 23, of which 8 were waited for; matrix products, arithmetic and copies ran while one was open for 1% of the time, Pallas kernels for 46%

profile of v3, /device:TPU:0, one launch (start us, length us, event | category | flops | bytes accessed | tf_op | source)
XLA Modules:
  0.0 159.1 jit_solution(14413646416491400455)
XLA Ops:
  0.0 0.5 collective-permute-start.1
  0.5 0.1 collective-permute-start.2
  0.5 3.0 %collective-permute-start.6 = (bf16[2,160,1280]{2,1,0:T(8,128)(2,1)}, bf16[2,160,1280]{2,1,0:T(8,128)(2,1)}, u32[]{:S(2)}, u32[]{:S(2)}) collective-permute-start(bf16[2,160,1280]{2,1,0:T(8,128)(2,1)} %bitcast.34), channel_id=1, source_target_pairs={{0,2},{1,3},{2,0},{3,1},{4,6},{5,7},{6,4},{7,5},{8,10},{9,11},{10,... | collective-permute-start | bytes 2457608 | tf_op jit(solution)/shard_map/exchange_keys/ppermute | solution.py:24
  3.5 6.6 %project_keys.1 = (bf16[336,1024]{1,0:T(8,128)(2,1)}, bf16[336,1024]{1,0:T(8,128)(2,1)}) custom-call(bf16[1024,1280]{1,0:T(8,128)(2,1)} %refs_8_.5, s32[1,1024]{1,0:T(1,128)} %bitcast.36, bf16[1280]{0:T(1024)(128)(2,1)} %gain_ref.6, bf16[960,1280]{1,0:T(8,128)(2,1)} %bitcast.27, bf16[960,1280]{1,0:T(8,128)(2,1)} %bitcast.28), custom_call_target="tpu_custom_call" | custom-call | tf_op jit(solution)/shard_map/project/project_keys/pallas_call | solution.py:166
  10.1 0.0 collective-permute-done.1.refs_5_
  10.1 1.6 collective-permute-start.5
  11.6 1.6 collective-permute-start.4
  13.2 5.6 %project_queries.1 = (bf16[160,1024]{1,0:T(8,128)(2,1)}, bf16[160,1024]{1,0:T(8,128)(2,1)}) custom-call(bf16[1024,1280]{1,0:T(8,128)(2,1)} %refs_8_.5, s32[1,1024]{1,0:T(1,128)} %bitcast.37, bf16[1280]{0:T(1024)(128)(2,1)} %gain_ref.6, bf16[960,1280]{1,0:T(8,128)(2,1)} %bitcast.29), custom_call_target="tpu_custom_call" | custom-call | tf_op jit(solution)/shard_map/exchange_keys/project_queries/pallas_call | solution.py:166
  18.8 0.1 stack.23.place
  18.9 1.0 copy-done.2
  19.9 8.4 %attend_own.1 = (f32[2,2,96,512]{3,2,1,0:T(8,128)S(1)}, f32[2,2,512]{2,1,0:T(2,128)S(1)}) custom-call(s32[6]{0:T(128)S(1)} %stack.23.place, bf16[160,1024]{1,0:T(8,128)(2,1)S(1)} %copy-done.2, bf16[336,1024]{1,0:T(8,128)(2,1)S(1)} %copy-done.1, bf16[336,1024]{1,0:T(8,128)(2,1)S(1)} %copy-done.1), custom_call_target="tpu_custom_call" | custom-call | flops 1000000 | bytes 1000000 | tf_op jit(solution)/shard_map/exchange_keys/attend_own/pallas_call | solution.py:333
  28.3 0.0 collective-permute-done.6.refs_2_
  28.3 0.0 collective-permute-done.5.refs_2_.refs_5_
  28.3 0.3 collective-permute-done.4.refs_6_
  28.6 0.9 copy-done.5
  29.5 0.2 collective-permute-start.9
  29.7 0.5 collective-permute-start
  30.3 0.0 collective-permute-start.8
  30.3 3.5 %collective-permute-start.7 = (bf16[336,1024]{1,0:T(8,128)(2,1)S(1)}, bf16[336,1024]{1,0:T(8,128)(2,1)}, u32[]{:S(2)}, u32[]{:S(2)}) collective-permute-start(bf16[336,1024]{1,0:T(8,128)(2,1)S(1)} %collective-permute-done.5.refs_2_.refs_5_), channel_id=1, source_target_pairs={{0,8},{1,9},{2,10},{3,11},{4,12},{5,13},{6,14},{7,15},{8,0},{9,1},... | collective-permute-start | bytes 2064392 | tf_op jit(solution)/shard_map/exchange_keys/ppermute | solution.py:39
  33.7 0.6 collective-permute-start.10
  34.3 0.6 reduce-window.6
  34.9 0.2 slice_reduce_fusion
  35.2 0.1 fusion
  35.3 4.6 %collective-permute-done.refs_0_ = bf16[160,1024]{1,0:T(8,128)(2,1)S(1)} collective-permute-done((bf16[160,1024]{1,0:T(8,128)(2,1)}, bf16[160,1024]{1,0:T(8,128)(2,1)S(1)}, u32[]{:S(2)}, u32[]{:S(2)}) %collective-permute-start) | collective-permute-done | bytes 327712 | tf_op jit(solution)/shard_map/exchange_keys/ppermute | solution.py:24
  39.9 1.0 copy-done.3
  40.8 1.1 copy-done.6
  41.9 28.6 %attend_near.1 = (f32[2,2,96,512]{3,2,1,0:T(8,128)S(1)}, f32[2,2,512]{2,1,0:T(2,128)S(1)}, f32[2,2,96,512]{3,2,1,0:T(8,128)S(1)}, f32[2,2,512]{2,1,0:T(2,128)S(1)}) custom-call(s32[6]{0:T(128)S(1)} %stack.23.place, bf16[160,1024]{1,0:T(8,128)(2,1)S(1)} %collective-permute-done.refs_0_, bf16[160,1024]{1,0:T(8,128)(2,1)S(1)} %copy-done.3, ...), custom_call_target="tpu_custom_call" | custom-call | flops 1000000 | bytes 1000000 | tf_op jit(solution)/shard_map/attention/attend_near/pallas_call | solution.py:333
  70.5 0.0 collective-permute-done.7.refs_4_
  70.5 0.0 collective-permute-done.10.refs_3_
  70.5 5.0 %attend_far.1 = (bf16[2,160,512]{2,1,0:T(8,128)(2,1)S(1)}, bf16[2,160,512]{2,1,0:T(8,128)(2,1)S(1)}) custom-call(s32[6]{0:T(128)S(1)} %stack.23.place, bf16[160,1024]{1,0:T(8,128)(2,1)S(1)} %collective-permute-done.refs_0_, bf16[160,1024]{1,0:T(8,128)(2,1)S(1)} %copy-done.4, bf16[336,1024]{1,0:T(8,128)(2,1)S(1)} %collective-permute-done.5.refs_2_.refs_5_, ...), custom_call_target="tpu_custom_call" | custom-call | flops 1000000 | bytes 1000000 | tf_op jit(solution)/shard_map/attention/attend_far/pallas_call | solution.py:333
  75.6 0.0 copy-start
  75.6 0.0 copy-start.7
  75.6 0.6 collective-permute-start.11
  76.2 0.6 collective-permute-start.14
  76.8 6.4 %load_mixer.1 = (bf16[1280,1280]{1,0:T(8,128)(2,1)S(1)}, bf16[2,1280,1280]{2,1,0:T(8,128)(2,1)S(1)}, bf16[2,1280,1280]{2,1,0:T(8,128)(2,1)S(1)}) custom-call(s32[6]{0:T(128)S(1)} %stack.23.place, bf16[2,160,1280]{2,1,0:T(8,128)(2,1)} %bitcast.35, bf16[2,160,1280]{2,1,0:T(8,128)(2,1)} %collective-permute-done.2.refs_1_, ...), custom_call_target="tpu_custom_call" | custom-call | bytes 16000000 | tf_op jit(solution)/shard_map/exchange_context/load_mixer/pallas_call | solution.py:104
  83.2 1.7 %collective-permute-done.11.refs_1_ = bf16[2,160,512]{2,1,0:T(8,128)(2,1)S(1)} collective-permute-done((bf16[2,160,512]{2,1,0:T(8,128)(2,1)S(1)}, bf16[2,160,512]{2,1,0:T(8,128)(2,1)S(1)}, u32[]{:S(2)}, u32[]{:S(2)}) %collective-permute-start.11) | collective-permute-done | bytes 327712 | tf_op jit(solution)/shard_map/exchange_context/ppermute | solution.py:24
  84.9 0.7 collective-permute-start.15
  85.5 0.0 collective-permute-start.12
  85.5 0.5 collective-permute-start.13
  86.0 0.0 collective-permute-done.14.refs_4_
  86.0 0.0 collective-permute-start.16
  86.0 7.1 %collective-permute-done.15.refs_5_ = bf16[2,160,512]{2,1,0:T(8,128)(2,1)S(1)} collective-permute-done((bf16[2,160,512]{2,1,0:T(8,128)(2,1)S(1)}, bf16[2,160,512]{2,1,0:T(8,128)(2,1)S(1)}, u32[]{:S(2)}, u32[]{:S(2)}) %collective-permute-start.15) | collective-permute-done | bytes 327712 | tf_op jit(solution)/shard_map/exchange_context/ppermute | solution.py:24
  93.2 0.0 collective-permute-start.17
  93.2 1.6 %collective-permute-done.17.refs_7_ = bf16[2,160,512]{2,1,0:T(8,128)(2,1)S(1)} collective-permute-done((bf16[2,160,512]{2,1,0:T(8,128)(2,1)S(1)}, bf16[2,160,512]{2,1,0:T(8,128)(2,1)S(1)}, u32[]{:S(2)}, u32[]{:S(2)}) %collective-permute-start.17) | collective-permute-done | bytes 327712 | tf_op jit(solution)/shard_map/exchange_context/ppermute | solution.py:24
  94.8 3.8 %mixer.3 = (bf16[128,1280]{1,0:T(8,128)(2,1)S(1)}, f32[128,1280]{1,0:T(8,128)S(1)}) custom-call(s32[6]{0:T(128)S(1)} %stack.23.place, bf16[2,160,512]{2,1,0:T(8,128)(2,1)S(1)} %get-tuple-element.95.refs_0_, bf16[2,160,512]{2,1,0:T(8,128)(2,1)S(1)} %collective-permute-done.11.refs_1_, bf16[2,160,512]{2,1,0:T(8,128)(2,1)S(1)} %collective-permute-done.12.refs_2_, ...), custom_call_target="tpu_custom_call" | custom-call | flops 5000000000 | bytes 20000000 | tf_op jit(solution)/shard_map/mixer/mixer/pallas_call | solution.py:384
  98.7 0.2 collective-permute-start.18
  98.9 0.8 collective-permute-start.20
  99.6 6.6 %mixer.5 = (bf16[256,1280]{1,0:T(8,128)(2,1)S(1)}, f32[256,1280]{1,0:T(8,128)S(1)}) custom-call(s32[6]{0:T(128)S(1)} %stack.23.place, bf16[2,160,512]{2,1,0:T(8,128)(2,1)S(1)} %get-tuple-element.95.refs_0_, bf16[2,160,512]{2,1,0:T(8,128)(2,1)S(1)} %collective-permute-done.11.refs_1_, bf16[2,160,512]{2,1,0:T(8,128)(2,1)S(1)} %collective-permute-done.12.refs_2_, ...), custom_call_target="tpu_custom_call" | custom-call | flops 5000000000 | bytes 20000000 | tf_op jit(solution)/shard_map/mixer/mixer/pallas_call | solution.py:384
  106.2 1.4 collective-permute-start.19
  107.6 4.1 %mixer.4 = (bf16[128,1280]{1,0:T(8,128)(2,1)S(1)}, f32[128,1280]{1,0:T(8,128)S(1)}) custom-call(s32[6]{0:T(128)S(1)} %stack.23.place, bf16[2,160,512]{2,1,0:T(8,128)(2,1)S(1)} %get-tuple-element.95.refs_0_, bf16[2,160,512]{2,1,0:T(8,128)(2,1)S(1)} %collective-permute-done.11.refs_1_, bf16[2,160,512]{2,1,0:T(8,128)(2,1)S(1)} %collective-permute-done.12.refs_2_, ...), custom_call_target="tpu_custom_call" | custom-call | flops 5000000000 | bytes 20000000 | tf_op jit(solution)/shard_map/mixer/mixer/pallas_call | solution.py:384
  111.7 0.0 copy-start.8
  111.7 0.8 collective-permute-start.21
  112.5 0.0 collective-permute-done.18.other
  112.5 2.9 %load_merge.1.weights = bf16[640,5120]{1,0:T(8,128)(2,1)S(1)} custom-call(bf16[320,5120]{1,0:T(8,128)(2,1)} %bitcast.30, bf16[320,5120]{1,0:T(8,128)(2,1)} %collective-permute-done.18.other), custom_call_target="tpu_custom_call" | custom-call | bytes 8000000 | tf_op jit(solution)/shard_map/merge/load_merge/pallas_call | solution.py:129
  115.4 1.6 %gather.2.refs_0_ = bf16[4,256,1280]{2,1,0:T(8,128)(2,1)S(1)} custom-call(s32[6]{0:T(128)S(1)} %stack.23.place, s32[4,256]{1,0:T(4,128)S(1)} %subtract_bitcast_fusion.index_ref, f32[128,1280]{1,0:T(8,128)S(1)} %get-tuple-element.118.kept, bf16[128,1280]{1,0:T(8,128)(2,1)S(1)} %collective-permute-done.20.received, bf16[1280]{0:T(1024)(128)(2,1)S(1)} %copy-done.8), custom_call_target="tpu_custom_call" | custom-call | flops 1000000000 | bytes 5000000 | tf_op jit(solution)/shard_map/merge/gather/pallas_call | solution.py:425
  117.1 6.8 %collective-permute-done.19.received = bf16[256,1280]{1,0:T(8,128)(2,1)S(1)} collective-permute-done((bf16[256,1280]{1,0:T(8,128)(2,1)S(1)}, bf16[256,1280]{1,0:T(8,128)(2,1)S(1)}, u32[]{:S(2)}, u32[]{:S(2)}) %collective-permute-start.19) | collective-permute-done | bytes 655392 | tf_op jit(solution)/shard_map/mixer/ppermute | solution.py:24
  123.9 1.8 %gather.3.earlier = bf16[4,256,1280]{2,1,0:T(8,128)(2,1)S(1)} custom-call(s32[6]{0:T(128)S(1)} %stack.23.place, s32[4,256]{1,0:T(4,128)S(1)} %subtract_bitcast_fusion.index_ref, f32[256,1280]{1,0:T(8,128)S(1)} %get-tuple-element.116.kept, bf16[256,1280]{1,0:T(8,128)(2,1)S(1)} %collective-permute-done.19.received, bf16[1280]{0:T(1024)(128)(2,1)S(1)} %copy-done.8, ...), custom_call_target="tpu_custom_call" | custom-call | flops 1000000000 | bytes 5000000 | tf_op jit(solution)/shard_map/merge/gather/pallas_call | solution.py:425
  125.7 4.4 %collective-permute-done.21.received = bf16[128,1280]{1,0:T(8,128)(2,1)S(1)} collective-permute-done((bf16[128,1280]{1,0:T(8,128)(2,1)S(1)}, bf16[128,1280]{1,0:T(8,128)(2,1)S(1)}, u32[]{:S(2)}, u32[]{:S(2)}) %collective-permute-start.21) | collective-permute-done | bytes 327712 | tf_op jit(solution)/shard_map/mixer/ppermute | solution.py:24
  130.0 3.8 %merge.1 = (f32[256,320]{1,0:T(8,128)S(1)}, f32[256,320]{1,0:T(8,128)S(1)}) custom-call(s32[6]{0:T(128)S(1)} %stack.23.place, s32[4,256]{1,0:T(4,128)S(1)} %subtract_bitcast_fusion.index_ref, f32[128,1280]{1,0:T(8,128)S(1)} %get-tuple-element.121.kept, bf16[128,1280]{1,0:T(8,128)(2,1)S(1)} %collective-permute-done.21.received, ...), custom_call_target="tpu_custom_call" | custom-call | flops 3000000000 | bytes 12000000 | tf_op jit(solution)/shard_map/merge/merge/pallas_call | solution.py:456
  133.9 0.1 collective-permute-start.22
  134.0 1.7 %collective-permute-done.22.received = f32[256,320]{1,0:T(8,128)S(1)} collective-permute-done((f32[256,320]{1,0:T(8,128)S(1)}, f32[256,320]{1,0:T(8,128)S(1)}, u32[]{:S(2)}, u32[]{:S(2)}) %collective-permute-start.22) | collective-permute-done | bytes 327712 | tf_op jit(solution)/shard_map/merge/ppermute | solution.py:24
  135.7 0.3 place.1
  136.0 22.4 %all_to_all.5 = bf16[8,64,320]{2,1,0:T(8,128)(2,1)S(1)} all-to-all(bf16[8,64,320]{2,1,0:T(8,128)(2,1)S(1)} %bitcast.26), channel_id=1, replica_groups=mesh['req'=8,'tp'=4] {'req'}, dimensions={0} | all-to-all | bytes 655360 | tf_op jit(solution)/shard_map/place/all_to_all | solution.py:610
  158.4 0.7 copy.14
  (31 shorter events, 0.1 us)
Async XLA Ops:
  0.0 10.1 %collective-permute-start.1 = (bf16[1280,1280]{1,0:T(8,128)(2,1)}, bf16[1280,1280]{1,0:T(8,128)(2,1)}, u32[]{:S(2)}, u32[]{:S(2)}) collective-permute-start(bf16[1280,1280]{1,0:T(8,128)(2,1)} %refs_4_.1), channel_id=1, source_target_pairs={{0,1},{1,0},{2,3},{3,2},{4,5},{5,4},{6,7},{7,6},{8,9},{9,8},{10,11... | collective-permute-start | bytes 9830408 | tf_op jit(solution)/shard_map/weights/ppermute | solution.py:24
  0.5 9.6 %collective-permute-start.2 = (bf16[2,160,1280]{2,1,0:T(8,128)(2,1)}, bf16[2,160,1280]{2,1,0:T(8,128)(2,1)}, u32[]{:S(2)}, u32[]{:S(2)}) collective-permute-start(bf16[2,160,1280]{2,1,0:T(8,128)(2,1)} %bitcast.33), channel_id=1, source_target_pairs={{0,1},{1,0},{2,3},{3,2},{4,5},{5,4},{6,7},{7,6},{8,9},{9,8},{10,11... | collective-permute-start | bytes 2457608 | tf_op jit(solution)/shard_map/weights/ppermute | solution.py:24
  0.5 27.8 %collective-permute-start.6 = (bf16[2,160,1280]{2,1,0:T(8,128)(2,1)}, bf16[2,160,1280]{2,1,0:T(8,128)(2,1)}, u32[]{:S(2)}, u32[]{:S(2)}) collective-permute-start(bf16[2,160,1280]{2,1,0:T(8,128)(2,1)} %bitcast.34), channel_id=1, source_target_pairs={{0,2},{1,3},{2,0},{3,1},{4,6},{5,7},{6,4},{7,5},{8,10},{9,11},{10,... | collective-permute-start | bytes 2457608 | tf_op jit(solution)/shard_map/exchange_keys/ppermute | solution.py:24
  10.1 8.8 %copy-start.1 = (bf16[336,1024]{1,0:T(8,128)(2,1)S(1)}, bf16[336,1024]{1,0:T(8,128)(2,1)}, u32[]{:S(2)}) copy-start(bf16[336,1024]{1,0:T(8,128)(2,1)} %get-tuple-element.71.refs_1_.refs_2_.refs_3_.refs_4_) | copy-start | bytes 2064388
  10.1 18.2 %collective-permute-start.5 = (bf16[336,1024]{1,0:T(8,128)(2,1)}, bf16[336,1024]{1,0:T(8,128)(2,1)S(1)}, u32[]{:S(2)}, u32[]{:S(2)}) collective-permute-start(bf16[336,1024]{1,0:T(8,128)(2,1)} %get-tuple-element.72), channel_id=1, source_target_pairs={{0,4},{4,0},{8,12},{12,8},{16,20},{20,16},{24,28},{28,24},{1,5},{5... | collective-permute-start | bytes 2064392 | tf_op jit(solution)/shard_map/exchange_keys/ppermute | solution.py:24
  11.6 17.0 %collective-permute-start.4 = (bf16[336,1024]{1,0:T(8,128)(2,1)}, bf16[336,1024]{1,0:T(8,128)(2,1)S(1)}, u32[]{:S(2)}, u32[]{:S(2)}) collective-permute-start(bf16[336,1024]{1,0:T(8,128)(2,1)} %get-tuple-element.71.refs_1_.refs_2_.refs_3_.refs_4_), channel_id=1, source_target_pairs={{0,8},{1,9},{2,10},{3,11},{4,12},{5,13},{6,14},{7,15},{8,0},{9,1},... | collective-permute-start | bytes 2064392 | tf_op jit(solution)/shard_map/exchange_keys/ppermute | solution.py:39
  13.2 16.3 %collective-permute-start.3 = (bf16[336,1024]{1,0:T(8,128)(2,1)}, bf16[336,1024]{1,0:T(8,128)(2,1)}, u32[]{:S(2)}, u32[]{:S(2)}) collective-permute-start(bf16[336,1024]{1,0:T(8,128)(2,1)} %get-tuple-element.71.refs_1_.refs_2_.refs_3_.refs_4_), channel_id=1, source_target_pairs={{0,1},{1,0},{2,3},{3,2},{4,5},{5,4},{6,7},{7,6},{8,16},{9,17},{10,... | collective-permute-start | bytes 2064392 | tf_op jit(solution)/shard_map/exchange_keys/ppermute | solution.py:39
  13.2 21.1 %copy-start.10 = (s32[256,1]{0,1:T(1,128)S(1)}, s32[256,1]{0,1:T(1,128)}, u32[]{:S(2)}) copy-start(s32[256,1]{0,1:T(1,128)} %param.23) | copy-start | bytes 3076
  13.2 22.0 %copy-start.11 = (s32[256,4]{0,1:T(4,128)S(1)}, s32[256,4]{0,1:T(4,128)}, u32[]{:S(2)}) copy-start(s32[256,4]{0,1:T(4,128)} %param.22) | copy-start | bytes 12292
  18.9 1.0 copy-start.2
  19.9 50.7 %copy-start.4 = (bf16[160,1024]{1,0:T(8,128)(2,1)S(1)}, bf16[160,1024]{1,0:T(8,128)(2,1)}, u32[]{:S(2)}) copy-start(bf16[160,1024]{1,0:T(8,128)(2,1)} %get-tuple-element.68.refs_0_.refs_1_) | copy-start | bytes 983044
  28.6 0.9 copy-start.5
  29.5 41.0 %collective-permute-start.9 = (bf16[1280,1280]{1,0:T(8,128)(2,1)}, bf16[1280,1280]{1,0:T(8,128)(2,1)}, u32[]{:S(2)}, u32[]{:S(2)}) collective-permute-start(bf16[1280,1280]{1,0:T(8,128)(2,1)} %refs_6_.1), channel_id=1, source_target_pairs={{0,1},{1,0},{2,3},{3,2},{4,5},{5,4},{6,7},{7,6},{8,9},{9,8},{10,11... | collective-permute-start | bytes 9830408 | tf_op jit(solution)/shard_map/exchange_keys/ppermute | solution.py:24
  29.7 10.1 %collective-permute-start = (bf16[160,1024]{1,0:T(8,128)(2,1)}, bf16[160,1024]{1,0:T(8,128)(2,1)S(1)}, u32[]{:S(2)}, u32[]{:S(2)}) collective-permute-start(bf16[160,1024]{1,0:T(8,128)(2,1)} %get-tuple-element.66), channel_id=1, source_target_pairs={{0,4},{4,0},{8,12},{12,8},{16,20},{20,16},{24,28},{28,24},{1,5},{5... | collective-permute-start | bytes 983048 | tf_op jit(solution)/shard_map/exchange_keys/ppermute | solution.py:24
  30.3 40.2 %collective-permute-start.8 = (bf16[336,1024]{1,0:T(8,128)(2,1)S(1)}, bf16[336,1024]{1,0:T(8,128)(2,1)S(1)}, u32[]{:S(2)}, u32[]{:S(2)}) collective-permute-start(bf16[336,1024]{1,0:T(8,128)(2,1)S(1)} %collective-permute-done.5.refs_2_.refs_5_), channel_id=1, source_target_pairs={{0,1},{1,0},{2,3},{3,2},{4,5},{5,4},{6,7},{7,6},{8,16},{9,17},{10,... | collective-permute-start | bytes 2064392 | tf_op jit(solution)/shard_map/exchange_keys/ppermute | solution.py:39
  30.3 40.2 %collective-permute-start.7 = (bf16[336,1024]{1,0:T(8,128)(2,1)S(1)}, bf16[336,1024]{1,0:T(8,128)(2,1)}, u32[]{:S(2)}, u32[]{:S(2)}) collective-permute-start(bf16[336,1024]{1,0:T(8,128)(2,1)S(1)} %collective-permute-done.5.refs_2_.refs_5_), channel_id=1, source_target_pairs={{0,8},{1,9},{2,10},{3,11},{4,12},{5,13},{6,14},{7,15},{8,0},{9,1},... | collective-permute-start | bytes 2064392 | tf_op jit(solution)/shard_map/exchange_keys/ppermute | solution.py:39
  33.7 36.8 %collective-permute-start.10 = (bf16[2,160,1280]{2,1,0:T(8,128)(2,1)}, bf16[2,160,1280]{2,1,0:T(8,128)(2,1)}, u32[]{:S(2)}, u32[]{:S(2)}) collective-permute-start(bf16[2,160,1280]{2,1,0:T(8,128)(2,1)} %collective-permute-done.2.refs_1_), channel_id=1, source_target_pairs={{0,2},{1,3},{2,0},{3,1},{4,6},{5,7},{6,4},{7,5},{8,10},{9,11},{10,... | collective-permute-start | bytes 2457608 | tf_op jit(solution)/shard_map/exchange_keys/ppermute | solution.py:24
  39.9 1.0 copy-start.3
  40.8 1.1 copy-start.6
  75.6 19.2 %copy-start = (bf16[1024,1280]{1,0:T(8,128)(2,1)S(1)}, bf16[1024,1280]{1,0:T(8,128)(2,1)}, u32[]{:S(2)}) copy-start(bf16[1024,1280]{1,0:T(8,128)(2,1)} %refs_8_.5) | copy-start | bytes 7864324
  75.6 19.2 %copy-start.7 = (bf16[1280]{0:T(1024)(128)(2,1)S(1)}, bf16[1280]{0:T(1024)(128)(2,1)}, u32[]{:S(2)}) copy-start(bf16[1280]{0:T(1024)(128)(2,1)} %refs_9_.5) | copy-start | bytes 7684
  75.6 9.3 %collective-permute-start.11 = (bf16[2,160,512]{2,1,0:T(8,128)(2,1)S(1)}, bf16[2,160,512]{2,1,0:T(8,128)(2,1)S(1)}, u32[]{:S(2)}, u32[]{:S(2)}) collective-permute-start(bf16[2,160,512]{2,1,0:T(8,128)(2,1)S(1)} %get-tuple-element.96), channel_id=1, source_target_pairs={{0,4},{4,0},{8,12},{12,8},{16,20},{20,16},{24,28},{28,24},{1,5},{5... | collective-permute-start | bytes 983048 | tf_op jit(solution)/shard_map/exchange_context/ppermute | solution.py:24
  76.2 9.8 %collective-permute-start.14 = (bf16[2,160,512]{2,1,0:T(8,128)(2,1)S(1)}, bf16[2,160,512]{2,1,0:T(8,128)(2,1)S(1)}, u32[]{:S(2)}, u32[]{:S(2)}) collective-permute-start(bf16[2,160,512]{2,1,0:T(8,128)(2,1)S(1)} %get-tuple-element.95.refs_0_), channel_id=1, source_target_pairs={{0,2},{1,3},{2,0},{3,1},{4,6},{5,7},{6,4},{7,5},{8,10},{9,11},{10,... | collective-permute-start | bytes 983048 | tf_op jit(solution)/shard_map/exchange_context/ppermute | solution.py:24
  84.9 13.8 %copy-start.9 = (bf16[5120,320]{0,1:T(8,128)(2,1)S(1)}, bf16[5120,320]{0,1:T(8,128)(2,1)}, u32[]{:S(2)}) copy-start(bf16[5120,320]{0,1:T(8,128)(2,1)} %param.21) | copy-start | bytes 9830404
  84.9 8.3 %collective-permute-start.15 = (bf16[2,160,512]{2,1,0:T(8,128)(2,1)S(1)}, bf16[2,160,512]{2,1,0:T(8,128)(2,1)S(1)}, u32[]{:S(2)}, u32[]{:S(2)}) collective-permute-start(bf16[2,160,512]{2,1,0:T(8,128)(2,1)S(1)} %collective-permute-done.11.refs_1_), channel_id=1, source_target_pairs={{0,2},{1,3},{2,0},{3,1},{4,6},{5,7},{6,4},{7,5},{8,10},{9,11},{10,... | collective-permute-start | bytes 983048 | tf_op jit(solution)/shard_map/exchange_context/ppermute | solution.py:24
  85.5 7.6 %collective-permute-start.12 = (bf16[2,160,512]{2,1,0:T(8,128)(2,1)S(1)}, bf16[2,160,512]{2,1,0:T(8,128)(2,1)S(1)}, u32[]{:S(2)}, u32[]{:S(2)}) collective-permute-start(bf16[2,160,512]{2,1,0:T(8,128)(2,1)S(1)} %get-tuple-element.95.refs_0_), channel_id=1, source_target_pairs={{0,1},{1,0},{2,3},{3,2},{4,5},{5,4},{6,7},{7,6},{8,9},{9,8},{10,11... | collective-permute-start | bytes 983048 | tf_op jit(solution)/shard_map/exchange_context/ppermute | solution.py:24
  85.5 7.7 %collective-permute-start.13 = (bf16[2,160,512]{2,1,0:T(8,128)(2,1)S(1)}, bf16[2,160,512]{2,1,0:T(8,128)(2,1)S(1)}, u32[]{:S(2)}, u32[]{:S(2)}) collective-permute-start(bf16[2,160,512]{2,1,0:T(8,128)(2,1)S(1)} %collective-permute-done.11.refs_1_), channel_id=1, source_target_pairs={{0,1},{1,0},{2,3},{3,2},{4,5},{5,4},{6,7},{7,6},{8,9},{9,8},{10,11... | collective-permute-start | bytes 983048 | tf_op jit(solution)/shard_map/exchange_context/ppermute | solution.py:24
  86.0 7.1 %collective-permute-start.16 = (bf16[2,160,512]{2,1,0:T(8,128)(2,1)S(1)}, bf16[2,160,512]{2,1,0:T(8,128)(2,1)S(1)}, u32[]{:S(2)}, u32[]{:S(2)}) collective-permute-start(bf16[2,160,512]{2,1,0:T(8,128)(2,1)S(1)} %collective-permute-done.14.refs_4_), channel_id=1, source_target_pairs={{0,1},{1,0},{2,3},{3,2},{4,5},{5,4},{6,7},{7,6},{8,9},{9,8},{10,11... | collective-permute-start | bytes 983048 | tf_op jit(solution)/shard_map/exchange_context/ppermute | solution.py:24
  93.2 1.6 %collective-permute-start.17 = (bf16[2,160,512]{2,1,0:T(8,128)(2,1)S(1)}, bf16[2,160,512]{2,1,0:T(8,128)(2,1)S(1)}, u32[]{:S(2)}, u32[]{:S(2)}) collective-permute-start(bf16[2,160,512]{2,1,0:T(8,128)(2,1)S(1)} %collective-permute-done.15.refs_5_), channel_id=1, source_target_pairs={{0,1},{1,0},{2,3},{3,2},{4,5},{5,4},{6,7},{7,6},{8,9},{9,8},{10,11... | collective-permute-start | bytes 983048 | tf_op jit(solution)/shard_map/exchange_context/ppermute | solution.py:24
  98.7 13.8 %collective-permute-start.18 = (bf16[320,5120]{1,0:T(8,128)(2,1)S(1)}, bf16[320,5120]{1,0:T(8,128)(2,1)}, u32[]{:S(2)}, u32[]{:S(2)}) collective-permute-start(bf16[320,5120]{1,0:T(8,128)(2,1)S(1)} %bitcast.31), channel_id=1, source_target_pairs={{0,1},{1,0},{2,3},{3,2},{4,5},{5,4},{6,7},{7,6},{8,9},{9,8},{10,11... | collective-permute-start | bytes 9830408 | tf_op jit(solution)/shard_map/mixer/ppermute | solution.py:24
  98.9 16.6 %collective-permute-start.20 = (bf16[128,1280]{1,0:T(8,128)(2,1)S(1)}, bf16[128,1280]{1,0:T(8,128)(2,1)S(1)}, u32[]{:S(2)}, u32[]{:S(2)}) collective-permute-start(bf16[128,1280]{1,0:T(8,128)(2,1)S(1)} %get-tuple-element.109), channel_id=1, source_target_pairs={{0,2},{1,3},{2,0},{3,1},{4,6},{5,7},{6,4},{7,5},{8,10},{9,11},{10,... | collective-permute-start | bytes 983048 | tf_op jit(solution)/shard_map/mixer/ppermute | solution.py:24
  106.2 17.7 %collective-permute-start.19 = (bf16[256,1280]{1,0:T(8,128)(2,1)S(1)}, bf16[256,1280]{1,0:T(8,128)(2,1)S(1)}, u32[]{:S(2)}, u32[]{:S(2)}) collective-permute-start(bf16[256,1280]{1,0:T(8,128)(2,1)S(1)} %get-tuple-element.117), channel_id=1, source_target_pairs={{0,2},{1,3},{2,0},{3,1},{4,6},{5,7},{6,4},{7,5},{8,10},{9,11},{10,... | collective-permute-start | bytes 1966088 | tf_op jit(solution)/shard_map/mixer/ppermute | solution.py:24
  111.7 3.8 %copy-start.8 = (bf16[1280]{0:T(1024)(128)(2,1)S(1)}, bf16[1280]{0:T(1024)(128)(2,1)}, u32[]{:S(2)}) copy-start(bf16[1280]{0:T(1024)(128)(2,1)} %gain_ref.9) | copy-start | bytes 7684
  111.7 18.4 %collective-permute-start.21 = (bf16[128,1280]{1,0:T(8,128)(2,1)S(1)}, bf16[128,1280]{1,0:T(8,128)(2,1)S(1)}, u32[]{:S(2)}, u32[]{:S(2)}) collective-permute-start(bf16[128,1280]{1,0:T(8,128)(2,1)S(1)} %get-tuple-element.113), channel_id=1, source_target_pairs={{0,2},{1,3},{2,0},{3,1},{4,6},{5,7},{6,4},{7,5},{8,10},{9,11},{10,... | collective-permute-start | bytes 983048 | tf_op jit(solution)/shard_map/mixer/ppermute | solution.py:24
  133.9 1.8 %collective-permute-start.22 = (f32[256,320]{1,0:T(8,128)S(1)}, f32[256,320]{1,0:T(8,128)S(1)}, u32[]{:S(2)}, u32[]{:S(2)}) collective-permute-start(f32[256,320]{1,0:T(8,128)S(1)} %get-tuple-element.126), channel_id=1, source_target_pairs={{0,1},{1,0},{2,3},{3,2},{4,5},{5,4},{6,7},{7,6},{8,9},{9,8},{10,11... | collective-permute-start | bytes 983048 | tf_op jit(solution)/shard_map/merge/ppermute | solution.py:24

commit v4 on v3

--- a/solution.py
+++ b/solution.py
@@ -511,6 +511,14 @@
         kv_own, kv_send = project(tokens, numbers, attend_gain, weight, (1, 2), "project_keys")
         kv_own, kv_send, expand_other, wo_core = tie((kv_own, kv_send, expand_other, wo_core))
 
+    with jax.named_scope("slots"):
+        capacity = 2 * merge_index.shape[0] // peers
+        target = owners[:, 0]
+        choose = (target[:, None] == jnp.arange(peers, dtype=jnp.int32)[None, :]).astype(jnp.int32)
+        slot = jnp.sum((jnp.cumsum(choose, axis=0) - 1) * choose, axis=1)
+        position = (target * capacity + slot)[None, :]
+        index = jnp.transpose(merge_index) - req * rows
+
     with jax.named_scope("exchange_keys"):
         kv_peer = swap(kv_send, "req", 1)
         kv_even = swap_pairs(kv_own, 0)
@@ -519,23 +527,14 @@
         q_own, q_send = project(tokens, numbers, attend_gain, weight, (0,), "project_queries")
         q_peer = swap(q_send, "req", 1)
         (state,) = attend(place, [q_own], [kv_own], [kv_own], "attend_own", {}, [None], [0])
-        kv_odd, kv_even, kv_peer, state, wo_across, late_reduce, late_wo = tie(
-            (kv_odd, kv_even, kv_peer, state, wo_across, reduce_weight, wo_core)
+        kv_odd, kv_even, kv_peer, state, wo_across, late_reduce, late_wo, position, index = tie(
+            (kv_odd, kv_even, kv_peer, state, wo_across, reduce_weight, wo_core, position, index)
         )
         kv_even_peer = swap_pairs(kv_peer, 0)
         kv_odd_peer = swap_pairs(kv_peer, 1)
         reduce_other = swap(late_reduce, "tp", 1)
         wo_both = swap(late_wo, "tp", 2)
 
-    with jax.named_scope("slots"):
-        capacity = 2 * merge_index.shape[0] // peers
-        target = owners[:, 0]
-        choose = (target[:, None] == jnp.arange(peers, dtype=jnp.int32)[None, :]).astype(jnp.int32)
-        slot = jnp.sum((jnp.cumsum(choose, axis=0) - 1) * choose, axis=1)
-        position = (target * capacity + slot)[None, :]
-        index = jnp.transpose(merge_index) - req * rows
-
-        q_peer, position, index = tie((q_peer, position, index))
 
     with jax.named_scope("attention"):
         queries, numbers = [q_peer, q_own], [kv_peer, kv_own]

time: 160 us -> 155 us (0.969); the launches traced: 159 us -> 156 us
  Pallas kernels: 85.5 us -> 79.2 us
  local copies, waits for them, and re-layouts: 5 us -> 3.01 us
  blocking collectives: 22.4 us -> 24.2 us
  starting transfers between devices: 17 us -> 18.8 us
  waiting for transfers between devices: 28.2 us -> 29.8 us
    pallas_call x3, Pallas kernels: 42 us -> 35.6 us  [attend(): pl.pallas_call(functools.partial(attend_kernel, blocks, flags, resumed, s...]
    ppermute x19, starting transfers between devices: 11.9 us -> 14.4 us  [swap(): lax.ppermute(block, axis, [(i, i ^ flip) for i in range(lax.axis_size(axi...]
    unnamed x25 -> x23, local copies, waits for them, and re-layouts: 4.7 us -> 2.71 us
    ppermute x19, waiting for transfers between devices: 27.9 us -> 29.8 us  [swap(): lax.ppermute(block, axis, [(i, i ^ flip) for i in range(lax.axis_size(axi...]
    all_to_all x1, blocking collectives: 22.4 us -> 24.2 us  [body(): lax.all_to_all(outgoing, 'req', split_axis=0, concat_axis=0, tiled=True)]
  transfers between devices with their start and end apart: 23 -> 23, of which waited for: 8 -> 8; matrix products, arithmetic and copies ran while one was open for 1% -> 1% of each run, Pallas kernels for 46% -> 44%
where the time goes in v4:
time: 155 us; the launch traced here: 156 us
  Pallas kernels  79.2 us (51%)
  waiting for transfers between devices  29.8 us (19%)
  blocking collectives  24.2 us (16%)
  starting transfers between devices  18.8 us (12%)
  local copies, waits for them, and re-layouts  3.01 us (2%)
    pallas_call x3, Pallas kernels, attend(): pl.pallas_call(functools.partial(attend_kernel, blocks, flags, resumed, s...  35.6 us
    ppermute x19, waiting for transfers between devices, swap(): lax.ppermute(block, axis, [(i, i ^ flip) for i in range(lax.axis_size(axi...  29.8 us
    all_to_all x1, blocking collectives, body(): lax.all_to_all(outgoing, 'req', split_axis=0, concat_axis=0, tiled=True)  24.2 us
    pallas_call x3, Pallas kernels, mixer(): pl.pallas_call(functools.partial(mixer_kernel, first, [which for _, which...  14.6 us
    ppermute x19, starting transfers between devices, swap(): lax.ppermute(block, axis, [(i, i ^ flip) for i in range(lax.axis_size(axi...  14.4 us
    pallas_call x2, Pallas kernels, project(): pl.pallas_call(functools.partial(project_kernel, len(parts)), grid=(rows...  12.2 us
    pallas_call x1, Pallas kernels, load_mixer(): pl.pallas_call(load_mixer_kernel, in_specs=[SCALARS] + [ANYWHERE] * 8, ou...  6.4 us
    ppermute x4, starting transfers between devices, swap_pairs(): return lax.ppermute(block, ('req', 'tp'), route)  4.31 us
  transfers between devices with their start and end apart: 23, of which 8 were waited for; matrix products, arithmetic and copies ran while one was open for 1% of the time, Pallas kernels for 44%

profile of v4, /device:TPU:0, one launch (start us, length us, event | category | flops | bytes accessed | tf_op | source)
XLA Modules:
  0.0 156.0 jit_solution(14274772050430778393)
XLA Ops:
  0.0 0.5 collective-permute-start.1
  0.5 0.1 collective-permute-start.2
  0.5 3.0 %collective-permute-start.6 = (bf16[2,160,1280]{2,1,0:T(8,128)(2,1)}, bf16[2,160,1280]{2,1,0:T(8,128)(2,1)}, u32[]{:S(2)}, u32[]{:S(2)}) collective-permute-start(bf16[2,160,1280]{2,1,0:T(8,128)(2,1)} %bitcast.34), channel_id=1, source_target_pairs={{0,2},{1,3},{2,0},{3,1},{4,6},{5,7},{6,4},{7,5},{8,10},{9,11},{10,... | collective-permute-start | bytes 2457608 | tf_op jit(solution)/shard_map/exchange_keys/ppermute | solution.py:24
  3.5 6.6 %project_keys.1 = (bf16[336,1024]{1,0:T(8,128)(2,1)}, bf16[336,1024]{1,0:T(8,128)(2,1)}) custom-call(bf16[1024,1280]{1,0:T(8,128)(2,1)} %refs_8_.5, s32[1,1024]{1,0:T(1,128)} %bitcast.36, bf16[1280]{0:T(1024)(128)(2,1)} %gain_ref.6, bf16[960,1280]{1,0:T(8,128)(2,1)} %bitcast.27, bf16[960,1280]{1,0:T(8,128)(2,1)} %bitcast.28), custom_call_target="tpu_custom_call" | custom-call | tf_op jit(solution)/shard_map/project/project_keys/pallas_call | solution.py:166
  10.1 0.0 collective-permute-done.2.refs_1_
  10.1 0.0 collective-permute-done.1.refs_5_
  10.1 0.9 copy-done.7
  11.1 1.6 %collective-permute-start.4 = (bf16[336,1024]{1,0:T(8,128)(2,1)}, bf16[336,1024]{1,0:T(8,128)(2,1)S(1)}, u32[]{:S(2)}, u32[]{:S(2)}) collective-permute-start(bf16[336,1024]{1,0:T(8,128)(2,1)} %get-tuple-element.69.refs_1_.refs_2_.refs_3_.refs_4_), channel_id=1, source_target_pairs={{0,8},{1,9},{2,10},{3,11},{4,12},{5,13},{6,14},{7,15},{8,0},{9,1},... | collective-permute-start | bytes 2064392 | tf_op jit(solution)/shard_map/exchange_keys/ppermute | solution.py:39
  12.7 0.0 collective-permute-start.3
  12.7 1.5 collective-permute-start.5
  14.2 5.6 %project_queries.1 = (bf16[160,1024]{1,0:T(8,128)(2,1)}, bf16[160,1024]{1,0:T(8,128)(2,1)}) custom-call(bf16[1024,1280]{1,0:T(8,128)(2,1)} %refs_8_.5, s32[1,1024]{1,0:T(1,128)} %bitcast.37, bf16[1280]{0:T(1024)(128)(2,1)} %gain_ref.6, bf16[960,1280]{1,0:T(8,128)(2,1)} %bitcast.29), custom_call_target="tpu_custom_call" | custom-call | tf_op jit(solution)/shard_map/exchange_keys/project_queries/pallas_call | solution.py:166
  19.7 0.6 reduce-window.6
  20.3 0.2 slice_reduce_fusion
  20.6 0.1 stack.23.place
  20.7 0.1 fusion
  20.8 0.0 copy-start.2
  20.8 1.0 copy-done.2
  21.8 8.4 %attend_own.1 = (f32[2,2,96,512]{3,2,1,0:T(8,128)S(1)}, f32[2,2,512]{2,1,0:T(2,128)S(1)}) custom-call(s32[6]{0:T(128)S(1)} %stack.23.place, bf16[160,1024]{1,0:T(8,128)(2,1)S(1)} %copy-done.2, bf16[336,1024]{1,0:T(8,128)(2,1)S(1)} %copy-done.1, bf16[336,1024]{1,0:T(8,128)(2,1)S(1)} %copy-done.1), custom_call_target="tpu_custom_call" | custom-call | flops 1000000 | bytes 1000000 | tf_op jit(solution)/shard_map/exchange_keys/attend_own/pallas_call | solution.py:333
  30.2 0.5 collective-permute-done.5.refs_2_.refs_5_
  30.7 0.0 collective-permute-done.4.refs_6_
  30.7 0.0 collective-permute-done.3.refs_7_
  30.7 0.0 collective-permute-start.9
  30.7 0.6 collective-permute-start.10
  31.3 0.2 collective-permute-start.8
  31.5 2.6 %collective-permute-start.7 = (bf16[336,1024]{1,0:T(8,128)(2,1)S(1)}, bf16[336,1024]{1,0:T(8,128)(2,1)S(1)}, u32[]{:S(2)}, u32[]{:S(2)}) collective-permute-start(bf16[336,1024]{1,0:T(8,128)(2,1)S(1)} %collective-permute-done.5.refs_2_.refs_5_), channel_id=1, source_target_pairs={{0,8},{1,9},{2,10},{3,11},{4,12},{5,13},{6,14},{7,15},{8,0},{9,1},... | collective-permute-start | bytes 2064392 | tf_op jit(solution)/shard_map/exchange_keys/ppermute | solution.py:39
  34.0 0.8 collective-permute-start
  34.9 8.9 %collective-permute-done.refs_0_ = bf16[160,1024]{1,0:T(8,128)(2,1)S(1)} collective-permute-done((bf16[160,1024]{1,0:T(8,128)(2,1)}, bf16[160,1024]{1,0:T(8,128)(2,1)S(1)}, u32[]{:S(2)}, u32[]{:S(2)}) %collective-permute-start) | collective-permute-done | bytes 327712 | tf_op jit(solution)/shard_map/exchange_keys/ppermute | solution.py:24
  43.7 24.5 %attend_near.1 = (f32[2,2,96,512]{3,2,1,0:T(8,128)S(1)}, f32[2,2,512]{2,1,0:T(2,128)S(1)}, f32[2,2,96,512]{3,2,1,0:T(8,128)S(1)}, f32[2,2,512]{2,1,0:T(2,128)S(1)}) custom-call(s32[6]{0:T(128)S(1)} %stack.23.place, bf16[160,1024]{1,0:T(8,128)(2,1)S(1)} %collective-permute-done.refs_0_, bf16[160,1024]{1,0:T(8,128)(2,1)S(1)} %copy-done.2, ...), custom_call_target="tpu_custom_call" | custom-call | flops 1000000 | bytes 1000000 | tf_op jit(solution)/shard_map/attention/attend_near/pallas_call | solution.py:333
  68.2 0.0 collective-permute-done.8.refs_5_
  68.3 0.0 collective-permute-done.7.refs_4_
  68.3 0.0 collective-permute-done.9.refs_7_
  68.3 2.7 %attend_far.1 = (bf16[2,160,512]{2,1,0:T(8,128)(2,1)S(1)}, bf16[2,160,512]{2,1,0:T(8,128)(2,1)S(1)}) custom-call(s32[6]{0:T(128)S(1)} %stack.23.place, bf16[160,1024]{1,0:T(8,128)(2,1)S(1)} %collective-permute-done.refs_0_, bf16[160,1024]{1,0:T(8,128)(2,1)S(1)} %copy-done.2, bf16[336,1024]{1,0:T(8,128)(2,1)S(1)} %collective-permute-done.5.refs_2_.refs_5_, ...), custom_call_target="tpu_custom_call" | custom-call | flops 1000000 | bytes 1000000 | tf_op jit(solution)/shard_map/attention/attend_far/pallas_call | solution.py:333
  71.0 0.0 copy-start
  71.0 0.0 copy-start.3
  71.0 0.7 collective-permute-start.11
  71.7 1.5 collective-permute-start.14
  73.2 6.4 %load_mixer.1 = (bf16[1280,1280]{1,0:T(8,128)(2,1)S(1)}, bf16[2,1280,1280]{2,1,0:T(8,128)(2,1)S(1)}, bf16[2,1280,1280]{2,1,0:T(8,128)(2,1)S(1)}) custom-call(s32[6]{0:T(128)S(1)} %stack.23.place, bf16[2,160,1280]{2,1,0:T(8,128)(2,1)} %bitcast.35, bf16[2,160,1280]{2,1,0:T(8,128)(2,1)} %copy-done.7, bf16[2,160,1280]{2,1,0:T(8,128)(2,1)} %collective-permute-done.6.refs_2_, ...), custom_call_target="tpu_custom_call" | custom-call | bytes 16000000 | tf_op jit(solution)/shard_map/exchange_context/load_mixer/pallas_call | solution.py:104
  79.6 0.1 collective-permute-done.11.refs_1_
  79.7 1.5 collective-permute-start.15
  81.2 0.0 collective-permute-start.12
  81.2 0.5 collective-permute-start.13
  81.8 0.0 collective-permute-start.16
  81.8 5.8 %collective-permute-done.15.refs_5_ = bf16[2,160,512]{2,1,0:T(8,128)(2,1)S(1)} collective-permute-done((bf16[2,160,512]{2,1,0:T(8,128)(2,1)S(1)}, bf16[2,160,512]{2,1,0:T(8,128)(2,1)S(1)}, u32[]{:S(2)}, u32[]{:S(2)}) %collective-permute-start.15) | collective-permute-done | bytes 327712 | tf_op jit(solution)/shard_map/exchange_context/ppermute | solution.py:24
  87.5 0.0 collective-permute-start.17
  87.6 1.6 %collective-permute-done.17.refs_7_ = bf16[2,160,512]{2,1,0:T(8,128)(2,1)S(1)} collective-permute-done((bf16[2,160,512]{2,1,0:T(8,128)(2,1)S(1)}, bf16[2,160,512]{2,1,0:T(8,128)(2,1)S(1)}, u32[]{:S(2)}, u32[]{:S(2)}) %collective-permute-start.17) | collective-permute-done | bytes 327712 | tf_op jit(solution)/shard_map/exchange_context/ppermute | solution.py:24
  89.2 3.9 %mixer.3 = (bf16[128,1280]{1,0:T(8,128)(2,1)S(1)}, f32[128,1280]{1,0:T(8,128)S(1)}) custom-call(s32[6]{0:T(128)S(1)} %stack.23.place, bf16[2,160,512]{2,1,0:T(8,128)(2,1)S(1)} %get-tuple-element.93.refs_0_, bf16[2,160,512]{2,1,0:T(8,128)(2,1)S(1)} %collective-permute-done.11.refs_1_, bf16[2,160,512]{2,1,0:T(8,128)(2,1)S(1)} %collective-permute-done.12.refs_2_, ...), custom_call_target="tpu_custom_call" | custom-call | flops 5000000000 | bytes 20000000 | tf_op jit(solution)/shard_map/mixer/mixer/pallas_call | solution.py:384
  93.1 0.2 collective-permute-start.18
  93.3 1.4 collective-permute-start.20
  94.7 6.7 %mixer.5 = (bf16[256,1280]{1,0:T(8,128)(2,1)S(1)}, f32[256,1280]{1,0:T(8,128)S(1)}) custom-call(s32[6]{0:T(128)S(1)} %stack.23.place, bf16[2,160,512]{2,1,0:T(8,128)(2,1)S(1)} %get-tuple-element.93.refs_0_, bf16[2,160,512]{2,1,0:T(8,128)(2,1)S(1)} %collective-permute-done.11.refs_1_, bf16[2,160,512]{2,1,0:T(8,128)(2,1)S(1)} %collective-permute-done.12.refs_2_, ...), custom_call_target="tpu_custom_call" | custom-call | flops 5000000000 | bytes 20000000 | tf_op jit(solution)/shard_map/mixer/mixer/pallas_call | solution.py:384
  101.3 0.7 collective-permute-start.19
  102.0 4.1 %mixer.4 = (bf16[128,1280]{1,0:T(8,128)(2,1)S(1)}, f32[128,1280]{1,0:T(8,128)S(1)}) custom-call(s32[6]{0:T(128)S(1)} %stack.23.place, bf16[2,160,512]{2,1,0:T(8,128)(2,1)S(1)} %get-tuple-element.93.refs_0_, bf16[2,160,512]{2,1,0:T(8,128)(2,1)S(1)} %collective-permute-done.11.refs_1_, bf16[2,160,512]{2,1,0:T(8,128)(2,1)S(1)} %collective-permute-done.12.refs_2_, ...), custom_call_target="tpu_custom_call" | custom-call | flops 5000000000 | bytes 20000000 | tf_op jit(solution)/shard_map/mixer/mixer/pallas_call | solution.py:384
  106.1 0.0 copy-start.4
  106.1 1.5 collective-permute-start.21
  107.6 2.9 %load_merge.1.weights = bf16[640,5120]{1,0:T(8,128)(2,1)S(1)} custom-call(bf16[320,5120]{1,0:T(8,128)(2,1)} %bitcast.30, bf16[320,5120]{1,0:T(8,128)(2,1)} %collective-permute-done.18.other), custom_call_target="tpu_custom_call" | custom-call | bytes 8000000 | tf_op jit(solution)/shard_map/merge/load_merge/pallas_call | solution.py:129
  110.6 1.6 %gather.2.refs_0_ = bf16[4,256,1280]{2,1,0:T(8,128)(2,1)S(1)} custom-call(s32[6]{0:T(128)S(1)} %stack.23.place, s32[4,256]{1,0:T(4,128)S(1)} %subtract_bitcast_fusion.index_ref, f32[128,1280]{1,0:T(8,128)S(1)} %get-tuple-element.116.kept, bf16[128,1280]{1,0:T(8,128)(2,1)S(1)} %collective-permute-done.20.received, bf16[1280]{0:T(1024)(128)(2,1)S(1)} %copy-done.4), custom_call_target="tpu_custom_call" | custom-call | flops 1000000000 | bytes 5000000 | tf_op jit(solution)/shard_map/merge/gather/pallas_call | solution.py:425
  112.2 6.8 %collective-permute-done.19.received = bf16[256,1280]{1,0:T(8,128)(2,1)S(1)} collective-permute-done((bf16[256,1280]{1,0:T(8,128)(2,1)S(1)}, bf16[256,1280]{1,0:T(8,128)(2,1)S(1)}, u32[]{:S(2)}, u32[]{:S(2)}) %collective-permute-start.19) | collective-permute-done | bytes 655392 | tf_op jit(solution)/shard_map/mixer/ppermute | solution.py:24
  119.0 1.8 %gather.3.earlier = bf16[4,256,1280]{2,1,0:T(8,128)(2,1)S(1)} custom-call(s32[6]{0:T(128)S(1)} %stack.23.place, s32[4,256]{1,0:T(4,128)S(1)} %subtract_bitcast_fusion.index_ref, f32[256,1280]{1,0:T(8,128)S(1)} %get-tuple-element.114.kept, bf16[256,1280]{1,0:T(8,128)(2,1)S(1)} %collective-permute-done.19.received, bf16[1280]{0:T(1024)(128)(2,1)S(1)} %copy-done.4, ...), custom_call_target="tpu_custom_call" | custom-call | flops 1000000000 | bytes 5000000 | tf_op jit(solution)/shard_map/merge/gather/pallas_call | solution.py:425
  120.8 4.4 %collective-permute-done.21.received = bf16[128,1280]{1,0:T(8,128)(2,1)S(1)} collective-permute-done((bf16[128,1280]{1,0:T(8,128)(2,1)S(1)}, bf16[128,1280]{1,0:T(8,128)(2,1)S(1)}, u32[]{:S(2)}, u32[]{:S(2)}) %collective-permute-start.21) | collective-permute-done | bytes 327712 | tf_op jit(solution)/shard_map/mixer/ppermute | solution.py:24
  125.1 3.8 %merge.1 = (f32[256,320]{1,0:T(8,128)S(1)}, f32[256,320]{1,0:T(8,128)S(1)}) custom-call(s32[6]{0:T(128)S(1)} %stack.23.place, s32[4,256]{1,0:T(4,128)S(1)} %subtract_bitcast_fusion.index_ref, f32[128,1280]{1,0:T(8,128)S(1)} %get-tuple-element.119.kept, bf16[128,1280]{1,0:T(8,128)(2,1)S(1)} %collective-permute-done.21.received, ...), custom_call_target="tpu_custom_call" | custom-call | flops 3000000000 | bytes 12000000 | tf_op jit(solution)/shard_map/merge/merge/pallas_call | solution.py:456
  129.0 0.1 collective-permute-start.22
  129.0 1.7 %collective-permute-done.22.received = f32[256,320]{1,0:T(8,128)S(1)} collective-permute-done((f32[256,320]{1,0:T(8,128)S(1)}, f32[256,320]{1,0:T(8,128)S(1)}, u32[]{:S(2)}, u32[]{:S(2)}) %collective-permute-start.22) | collective-permute-done | bytes 327712 | tf_op jit(solution)/shard_map/merge/ppermute | solution.py:24
  130.8 0.3 place.1
  131.1 24.2 %all_to_all.5 = bf16[8,64,320]{2,1,0:T(8,128)(2,1)S(1)} all-to-all(bf16[8,64,320]{2,1,0:T(8,128)(2,1)S(1)} %bitcast.26), channel_id=1, replica_groups=mesh['req'=8,'tp'=4] {'req'}, dimensions={0} | all-to-all | bytes 655360 | tf_op jit(solution)/shard_map/place/all_to_all | solution.py:609
  155.2 0.7 copy.14
  (29 shorter events, 0.1 us)
Async XLA Ops:
  0.0 10.1 %collective-permute-start.1 = (bf16[1280,1280]{1,0:T(8,128)(2,1)}, bf16[1280,1280]{1,0:T(8,128)(2,1)}, u32[]{:S(2)}, u32[]{:S(2)}) collective-permute-start(bf16[1280,1280]{1,0:T(8,128)(2,1)} %refs_4_.1), channel_id=1, source_target_pairs={{0,1},{1,0},{2,3},{3,2},{4,5},{5,4},{6,7},{7,6},{8,9},{9,8},{10,11... | collective-permute-start | bytes 9830408 | tf_op jit(solution)/shard_map/weights/ppermute | solution.py:24
  0.5 9.6 %collective-permute-start.2 = (bf16[2,160,1280]{2,1,0:T(8,128)(2,1)}, bf16[2,160,1280]{2,1,0:T(8,128)(2,1)S(1)}, u32[]{:S(2)}, u32[]{:S(2)}) collective-permute-start(bf16[2,160,1280]{2,1,0:T(8,128)(2,1)} %bitcast.33), channel_id=1, source_target_pairs={{0,1},{1,0},{2,3},{3,2},{4,5},{5,4},{6,7},{7,6},{8,9},{9,8},{10,11... | collective-permute-start | bytes 2457608 | tf_op jit(solution)/shard_map/weights/ppermute | solution.py:24
  0.5 29.7 %collective-permute-start.6 = (bf16[2,160,1280]{2,1,0:T(8,128)(2,1)}, bf16[2,160,1280]{2,1,0:T(8,128)(2,1)}, u32[]{:S(2)}, u32[]{:S(2)}) collective-permute-start(bf16[2,160,1280]{2,1,0:T(8,128)(2,1)} %bitcast.34), channel_id=1, source_target_pairs={{0,2},{1,3},{2,0},{3,1},{4,6},{5,7},{6,4},{7,5},{8,10},{9,11},{10,... | collective-permute-start | bytes 2457608 | tf_op jit(solution)/shard_map/exchange_keys/ppermute | solution.py:24
  3.5 10.7 %copy-start.9 = (s32[256,1]{0,1:T(1,128)S(1)}, s32[256,1]{0,1:T(1,128)}, u32[]{:S(2)}) copy-start(s32[256,1]{0,1:T(1,128)} %param.23) | copy-start | bytes 3076
  10.1 10.7 %copy-start.10 = (s32[256,4]{0,1:T(4,128)S(1)}, s32[256,4]{0,1:T(4,128)}, u32[]{:S(2)}) copy-start(s32[256,4]{0,1:T(4,128)} %param.22) | copy-start | bytes 12292
  10.1 10.7 %copy-start.1 = (bf16[336,1024]{1,0:T(8,128)(2,1)S(1)}, bf16[336,1024]{1,0:T(8,128)(2,1)}, u32[]{:S(2)}) copy-start(bf16[336,1024]{1,0:T(8,128)(2,1)} %get-tuple-element.69.refs_1_.refs_2_.refs_3_.refs_4_) | copy-start | bytes 2064388
  10.1 1.0 copy-start.7
  11.1 19.6 %collective-permute-start.4 = (bf16[336,1024]{1,0:T(8,128)(2,1)}, bf16[336,1024]{1,0:T(8,128)(2,1)S(1)}, u32[]{:S(2)}, u32[]{:S(2)}) collective-permute-start(bf16[336,1024]{1,0:T(8,128)(2,1)} %get-tuple-element.69.refs_1_.refs_2_.refs_3_.refs_4_), channel_id=1, source_target_pairs={{0,8},{1,9},{2,10},{3,11},{4,12},{5,13},{6,14},{7,15},{8,0},{9,1},... | collective-permute-start | bytes 2064392 | tf_op jit(solution)/shard_map/exchange_keys/ppermute | solution.py:39
  12.7 18.1 %collective-permute-start.3 = (bf16[336,1024]{1,0:T(8,128)(2,1)}, bf16[336,1024]{1,0:T(8,128)(2,1)S(1)}, u32[]{:S(2)}, u32[]{:S(2)}) collective-permute-start(bf16[336,1024]{1,0:T(8,128)(2,1)} %get-tuple-element.69.refs_1_.refs_2_.refs_3_.refs_4_), channel_id=1, source_target_pairs={{0,1},{1,0},{2,3},{3,2},{4,5},{5,4},{6,7},{7,6},{8,16},{9,17},{10,... | collective-permute-start | bytes 2064392 | tf_op jit(solution)/shard_map/exchange_keys/ppermute | solution.py:39
  12.7 18.1 %collective-permute-start.5 = (bf16[336,1024]{1,0:T(8,128)(2,1)}, bf16[336,1024]{1,0:T(8,128)(2,1)S(1)}, u32[]{:S(2)}, u32[]{:S(2)}) collective-permute-start(bf16[336,1024]{1,0:T(8,128)(2,1)} %get-tuple-element.70), channel_id=1, source_target_pairs={{0,4},{4,0},{8,12},{12,8},{16,20},{20,16},{24,28},{28,24},{1,5},{5... | collective-permute-start | bytes 2064392 | tf_op jit(solution)/shard_map/exchange_keys/ppermute | solution.py:24
  20.8 1.0 copy-start.2
  30.7 37.6 %collective-permute-start.9 = (bf16[1280,1280]{1,0:T(8,128)(2,1)}, bf16[1280,1280]{1,0:T(8,128)(2,1)S(1)}, u32[]{:S(2)}, u32[]{:S(2)}) collective-permute-start(bf16[1280,1280]{1,0:T(8,128)(2,1)} %refs_6_.1), channel_id=1, source_target_pairs={{0,1},{1,0},{2,3},{3,2},{4,5},{5,4},{6,7},{7,6},{8,9},{9,8},{10,11... | collective-permute-start | bytes 9830408 | tf_op jit(solution)/shard_map/exchange_keys/ppermute | solution.py:24
  30.7 37.5 %collective-permute-start.10 = (bf16[2,160,1280]{2,1,0:T(8,128)(2,1)}, bf16[2,160,1280]{2,1,0:T(8,128)(2,1)S(1)}, u32[]{:S(2)}, u32[]{:S(2)}) collective-permute-start(bf16[2,160,1280]{2,1,0:T(8,128)(2,1)} %copy-done.7), channel_id=1, source_target_pairs={{0,2},{1,3},{2,0},{3,1},{4,6},{5,7},{6,4},{7,5},{8,10},{9,11},{10,... | collective-permute-start | bytes 2457608 | tf_op jit(solution)/shard_map/exchange_keys/ppermute | solution.py:24
  31.3 36.9 %collective-permute-start.8 = (bf16[336,1024]{1,0:T(8,128)(2,1)S(1)}, bf16[336,1024]{1,0:T(8,128)(2,1)S(1)}, u32[]{:S(2)}, u32[]{:S(2)}) collective-permute-start(bf16[336,1024]{1,0:T(8,128)(2,1)S(1)} %collective-permute-done.5.refs_2_.refs_5_), channel_id=1, source_target_pairs={{0,1},{1,0},{2,3},{3,2},{4,5},{5,4},{6,7},{7,6},{8,16},{9,17},{10,... | collective-permute-start | bytes 2064392 | tf_op jit(solution)/shard_map/exchange_keys/ppermute | solution.py:39
  31.5 36.8 %collective-permute-start.7 = (bf16[336,1024]{1,0:T(8,128)(2,1)S(1)}, bf16[336,1024]{1,0:T(8,128)(2,1)S(1)}, u32[]{:S(2)}, u32[]{:S(2)}) collective-permute-start(bf16[336,1024]{1,0:T(8,128)(2,1)S(1)} %collective-permute-done.5.refs_2_.refs_5_), channel_id=1, source_target_pairs={{0,8},{1,9},{2,10},{3,11},{4,12},{5,13},{6,14},{7,15},{8,0},{9,1},... | collective-permute-start | bytes 2064392 | tf_op jit(solution)/shard_map/exchange_keys/ppermute | solution.py:39
  34.0 9.7 %collective-permute-start = (bf16[160,1024]{1,0:T(8,128)(2,1)}, bf16[160,1024]{1,0:T(8,128)(2,1)S(1)}, u32[]{:S(2)}, u32[]{:S(2)}) collective-permute-start(bf16[160,1024]{1,0:T(8,128)(2,1)} %get-tuple-element.65), channel_id=1, source_target_pairs={{0,4},{4,0},{8,12},{12,8},{16,20},{20,16},{24,28},{28,24},{1,5},{5... | collective-permute-start | bytes 983048 | tf_op jit(solution)/shard_map/exchange_keys/ppermute | solution.py:24
  68.3 4.9 %copy-start.8 = (bf16[2,160,1280]{2,1,0:T(8,128)(2,1)}, bf16[2,160,1280]{2,1,0:T(8,128)(2,1)S(1)}, u32[]{:S(2)}) copy-start(bf16[2,160,1280]{2,1,0:T(8,128)(2,1)S(1)} %collective-permute-done.10.refs_3_) | copy-start | bytes 2457604
  68.3 4.9 %copy-start.6 = (bf16[1280,1280]{1,0:T(8,128)(2,1)}, bf16[1280,1280]{1,0:T(8,128)(2,1)S(1)}, u32[]{:S(2)}) copy-start(bf16[1280,1280]{1,0:T(8,128)(2,1)S(1)} %collective-permute-done.9.refs_7_) | copy-start | bytes 9830404
  71.0 18.2 %copy-start = (bf16[1024,1280]{1,0:T(8,128)(2,1)S(1)}, bf16[1024,1280]{1,0:T(8,128)(2,1)}, u32[]{:S(2)}) copy-start(bf16[1024,1280]{1,0:T(8,128)(2,1)} %refs_8_.5) | copy-start | bytes 7864324
  71.0 18.2 %copy-start.3 = (bf16[1280]{0:T(1024)(128)(2,1)S(1)}, bf16[1280]{0:T(1024)(128)(2,1)}, u32[]{:S(2)}) copy-start(bf16[1280]{0:T(1024)(128)(2,1)} %refs_9_.5) | copy-start | bytes 7684
  71.0 8.7 %collective-permute-start.11 = (bf16[2,160,512]{2,1,0:T(8,128)(2,1)S(1)}, bf16[2,160,512]{2,1,0:T(8,128)(2,1)S(1)}, u32[]{:S(2)}, u32[]{:S(2)}) collective-permute-start(bf16[2,160,512]{2,1,0:T(8,128)(2,1)S(1)} %get-tuple-element.94), channel_id=1, source_target_pairs={{0,4},{4,0},{8,12},{12,8},{16,20},{20,16},{24,28},{28,24},{1,5},{5... | collective-permute-start | bytes 983048 | tf_op jit(solution)/shard_map/exchange_context/ppermute | solution.py:24
  71.7 10.1 %collective-permute-start.14 = (bf16[2,160,512]{2,1,0:T(8,128)(2,1)S(1)}, bf16[2,160,512]{2,1,0:T(8,128)(2,1)S(1)}, u32[]{:S(2)}, u32[]{:S(2)}) collective-permute-start(bf16[2,160,512]{2,1,0:T(8,128)(2,1)S(1)} %get-tuple-element.93.refs_0_), channel_id=1, source_target_pairs={{0,2},{1,3},{2,0},{3,1},{4,6},{5,7},{6,4},{7,5},{8,10},{9,11},{10,... | collective-permute-start | bytes 983048 | tf_op jit(solution)/shard_map/exchange_context/ppermute | solution.py:24
  79.7 13.3 %copy-start.5 = (bf16[5120,320]{0,1:T(8,128)(2,1)S(1)}, bf16[5120,320]{0,1:T(8,128)(2,1)}, u32[]{:S(2)}) copy-start(bf16[5120,320]{0,1:T(8,128)(2,1)} %param.21) | copy-start | bytes 9830404
  79.7 7.8 %collective-permute-start.15 = (bf16[2,160,512]{2,1,0:T(8,128)(2,1)S(1)}, bf16[2,160,512]{2,1,0:T(8,128)(2,1)S(1)}, u32[]{:S(2)}, u32[]{:S(2)}) collective-permute-start(bf16[2,160,512]{2,1,0:T(8,128)(2,1)S(1)} %collective-permute-done.11.refs_1_), channel_id=1, source_target_pairs={{0,2},{1,3},{2,0},{3,1},{4,6},{5,7},{6,4},{7,5},{8,10},{9,11},{10,... | collective-permute-start | bytes 983048 | tf_op jit(solution)/shard_map/exchange_context/ppermute | solution.py:24
  81.2 6.3 %collective-permute-start.12 = (bf16[2,160,512]{2,1,0:T(8,128)(2,1)S(1)}, bf16[2,160,512]{2,1,0:T(8,128)(2,1)S(1)}, u32[]{:S(2)}, u32[]{:S(2)}) collective-permute-start(bf16[2,160,512]{2,1,0:T(8,128)(2,1)S(1)} %get-tuple-element.93.refs_0_), channel_id=1, source_target_pairs={{0,1},{1,0},{2,3},{3,2},{4,5},{5,4},{6,7},{7,6},{8,9},{9,8},{10,11... | collective-permute-start | bytes 983048 | tf_op jit(solution)/shard_map/exchange_context/ppermute | solution.py:24
  81.2 6.3 %collective-permute-start.13 = (bf16[2,160,512]{2,1,0:T(8,128)(2,1)S(1)}, bf16[2,160,512]{2,1,0:T(8,128)(2,1)S(1)}, u32[]{:S(2)}, u32[]{:S(2)}) collective-permute-start(bf16[2,160,512]{2,1,0:T(8,128)(2,1)S(1)} %collective-permute-done.11.refs_1_), channel_id=1, source_target_pairs={{0,1},{1,0},{2,3},{3,2},{4,5},{5,4},{6,7},{7,6},{8,9},{9,8},{10,11... | collective-permute-start | bytes 983048 | tf_op jit(solution)/shard_map/exchange_context/ppermute | solution.py:24
  81.8 5.8 %collective-permute-start.16 = (bf16[2,160,512]{2,1,0:T(8,128)(2,1)S(1)}, bf16[2,160,512]{2,1,0:T(8,128)(2,1)S(1)}, u32[]{:S(2)}, u32[]{:S(2)}) collective-permute-start(bf16[2,160,512]{2,1,0:T(8,128)(2,1)S(1)} %collective-permute-done.14.refs_4_), channel_id=1, source_target_pairs={{0,1},{1,0},{2,3},{3,2},{4,5},{5,4},{6,7},{7,6},{8,9},{9,8},{10,11... | collective-permute-start | bytes 983048 | tf_op jit(solution)/shard_map/exchange_context/ppermute | solution.py:24
  87.5 1.6 %collective-permute-start.17 = (bf16[2,160,512]{2,1,0:T(8,128)(2,1)S(1)}, bf16[2,160,512]{2,1,0:T(8,128)(2,1)S(1)}, u32[]{:S(2)}, u32[]{:S(2)}) collective-permute-start(bf16[2,160,512]{2,1,0:T(8,128)(2,1)S(1)} %collective-permute-done.15.refs_5_), channel_id=1, source_target_pairs={{0,1},{1,0},{2,3},{3,2},{4,5},{5,4},{6,7},{7,6},{8,9},{9,8},{10,11... | collective-permute-start | bytes 983048 | tf_op jit(solution)/shard_map/exchange_context/ppermute | solution.py:24
  93.1 14.6 %collective-permute-start.18 = (bf16[320,5120]{1,0:T(8,128)(2,1)S(1)}, bf16[320,5120]{1,0:T(8,128)(2,1)}, u32[]{:S(2)}, u32[]{:S(2)}) collective-permute-start(bf16[320,5120]{1,0:T(8,128)(2,1)S(1)} %bitcast.31), channel_id=1, source_target_pairs={{0,1},{1,0},{2,3},{3,2},{4,5},{5,4},{6,7},{7,6},{8,9},{9,8},{10,11... | collective-permute-start | bytes 9830408 | tf_op jit(solution)/shard_map/mixer/ppermute | solution.py:24
  93.3 17.3 %collective-permute-start.20 = (bf16[128,1280]{1,0:T(8,128)(2,1)S(1)}, bf16[128,1280]{1,0:T(8,128)(2,1)S(1)}, u32[]{:S(2)}, u32[]{:S(2)}) collective-permute-start(bf16[128,1280]{1,0:T(8,128)(2,1)S(1)} %get-tuple-element.107), channel_id=1, source_target_pairs={{0,2},{1,3},{2,0},{3,1},{4,6},{5,7},{6,4},{7,5},{8,10},{9,11},{10,... | collective-permute-start | bytes 983048 | tf_op jit(solution)/shard_map/mixer/ppermute | solution.py:24
  101.3 17.7 %collective-permute-start.19 = (bf16[256,1280]{1,0:T(8,128)(2,1)S(1)}, bf16[256,1280]{1,0:T(8,128)(2,1)S(1)}, u32[]{:S(2)}, u32[]{:S(2)}) collective-permute-start(bf16[256,1280]{1,0:T(8,128)(2,1)S(1)} %get-tuple-element.115), channel_id=1, source_target_pairs={{0,2},{1,3},{2,0},{3,1},{4,6},{5,7},{6,4},{7,5},{8,10},{9,11},{10,... | collective-permute-start | bytes 1966088 | tf_op jit(solution)/shard_map/mixer/ppermute | solution.py:24
  106.1 4.5 %copy-start.4 = (bf16[1280]{0:T(1024)(128)(2,1)S(1)}, bf16[1280]{0:T(1024)(128)(2,1)}, u32[]{:S(2)}) copy-start(bf16[1280]{0:T(1024)(128)(2,1)} %gain_ref.9) | copy-start | bytes 7684
  106.1 19.0 %collective-permute-start.21 = (bf16[128,1280]{1,0:T(8,128)(2,1)S(1)}, bf16[128,1280]{1,0:T(8,128)(2,1)S(1)}, u32[]{:S(2)}, u32[]{:S(2)}) collective-permute-start(bf16[128,1280]{1,0:T(8,128)(2,1)S(1)} %get-tuple-element.111), channel_id=1, source_target_pairs={{0,2},{1,3},{2,0},{3,1},{4,6},{5,7},{6,4},{7,5},{8,10},{9,11},{10,... | collective-permute-start | bytes 983048 | tf_op jit(solution)/shard_map/mixer/ppermute | solution.py:24
  129.0 1.8 %collective-permute-start.22 = (f32[256,320]{1,0:T(8,128)S(1)}, f32[256,320]{1,0:T(8,128)S(1)}, u32[]{:S(2)}, u32[]{:S(2)}) collective-permute-start(f32[256,320]{1,0:T(8,128)S(1)} %get-tuple-element.124), channel_id=1, source_target_pairs={{0,1},{1,0},{2,3},{3,2},{4,5},{5,4},{6,7},{7,6},{8,9},{9,8},{10,11... | collective-permute-start | bytes 983048 | tf_op jit(solution)/shard_map/merge/ppermute | solution.py:24

commit v5 on v4

--- a/solution.py
+++ b/solution.py
@@ -497,7 +497,7 @@
     core = lax.axis_index("tp") % 2
 
     per_core = rows // 2
-    chunks = [(0, 128), (128, per_core - 256), (per_core - 128, 128)]
+    chunks = [(first, 128) for first in range(0, per_core, 128)]
     place = jnp.stack([par, core, core * per_core, req, alone(0), alone(1)])
     tie = lax.optimization_barrier
     with jax.named_scope("weights"):

time: 155 us -> 156 us (level)
  Pallas kernels: 79.2 us -> 88.6 us
  waiting for transfers between devices: 29.8 us -> 25.9 us
  blocking collectives: 24.2 us -> 20.4 us
    pallas_call x3, Pallas kernels: 35.6 us -> 42.6 us  [attend(): pl.pallas_call(functools.partial(attend_kernel, blocks, flags, resumed, s...]
    ppermute x19 -> x20, waiting for transfers between devices: 29.8 us -> 25.9 us  [swap(): lax.ppermute(block, axis, [(i, i ^ flip) for i in range(lax.axis_size(axi...]
    all_to_all x1, blocking collectives: 24.2 us -> 20.4 us  [body(): lax.all_to_all(outgoing, 'req', split_axis=0, concat_axis=0, tiled=True)]
    pallas_call x2 -> x3, Pallas kernels: 3.39 us -> 4.84 us  [gather(): pl.pallas_call(functools.partial(gather_kernel, first), in_specs=[SCALARS...]
    pallas_call x3 -> x4, Pallas kernels: 14.6 us -> 15.5 us  [mixer(): pl.pallas_call(functools.partial(mixer_kernel, first, [which for _, which...]
    ppermute x19 -> x20, starting transfers between devices: 14.4 us -> 15.1 us  [swap(): lax.ppermute(block, axis, [(i, i ^ flip) for i in range(lax.axis_size(axi...]
  transfers between devices with their start and end apart: 23 -> 24, of which waited for: 8 -> 8; matrix products, arithmetic and copies ran while one was open for 1% -> 1% of each run, Pallas kernels for 44% -> 47%
where the time goes in v5:
time: 156 us; the launch traced here: 158 us
  Pallas kernels  88.6 us (57%)
  waiting for transfers between devices  25.9 us (17%)
  blocking collectives  20.4 us (13%)
  starting transfers between devices  19.4 us (12%)
  local copies, waits for them, and re-layouts  3.02 us (2%)
    pallas_call x3, Pallas kernels, attend(): pl.pallas_call(functools.partial(attend_kernel, blocks, flags, resumed, s...  42.6 us
    ppermute x20, waiting for transfers between devices, swap(): lax.ppermute(block, axis, [(i, i ^ flip) for i in range(lax.axis_size(axi...  25.9 us
    all_to_all x1, blocking collectives, body(): lax.all_to_all(outgoing, 'req', split_axis=0, concat_axis=0, tiled=True)  20.4 us
    pallas_call x4, Pallas kernels, mixer(): pl.pallas_call(functools.partial(mixer_kernel, first, [which for _, which...  15.5 us
    ppermute x20, starting transfers between devices, swap(): lax.ppermute(block, axis, [(i, i ^ flip) for i in range(lax.axis_size(axi...  15.1 us
    pallas_call x2, Pallas kernels, project(): pl.pallas_call(functools.partial(project_kernel, len(parts)), grid=(rows...  12.2 us
    pallas_call x1, Pallas kernels, load_mixer(): pl.pallas_call(load_mixer_kernel, in_specs=[SCALARS] + [ANYWHERE] * 8, ou...  6.4 us
    pallas_call x3, Pallas kernels, gather(): pl.pallas_call(functools.partial(gather_kernel, first), in_specs=[SCALARS...  4.84 us
  transfers between devices with their start and end apart: 24, of which 8 were waited for; matrix products, arithmetic and copies ran while one was open for 1% of the time, Pallas kernels for 47%

profile of v5, /device:TPU:0, one launch (start us, length us, event | category | flops | bytes accessed | tf_op | source)
XLA Modules:
  0.0 158.3 jit_solution(13047441211540524231)
XLA Ops:
  0.0 0.5 collective-permute-start.1
  0.5 0.1 collective-permute-start.2
  0.5 3.0 %collective-permute-start.6 = (bf16[2,160,1280]{2,1,0:T(8,128)(2,1)}, bf16[2,160,1280]{2,1,0:T(8,128)(2,1)}, u32[]{:S(2)}, u32[]{:S(2)}) collective-permute-start(bf16[2,160,1280]{2,1,0:T(8,128)(2,1)} %bitcast.34), channel_id=1, source_target_pairs={{0,2},{1,3},{2,0},{3,1},{4,6},{5,7},{6,4},{7,5},{8,10},{9,11},{10,... | collective-permute-start | bytes 2457608 | tf_op jit(solution)/shard_map/exchange_keys/ppermute | solution.py:24
  3.5 6.6 %project_keys.1 = (bf16[336,1024]{1,0:T(8,128)(2,1)}, bf16[336,1024]{1,0:T(8,128)(2,1)}) custom-call(bf16[1024,1280]{1,0:T(8,128)(2,1)} %refs_8_.7, s32[1,1024]{1,0:T(1,128)} %bitcast.36, bf16[1280]{0:T(1024)(128)(2,1)} %gain_ref.7, bf16[960,1280]{1,0:T(8,128)(2,1)} %bitcast.27, bf16[960,1280]{1,0:T(8,128)(2,1)} %bitcast.28), custom_call_target="tpu_custom_call" | custom-call | tf_op jit(solution)/shard_map/project/project_keys/pallas_call | solution.py:166
  10.1 0.0 collective-permute-done.1.refs_5_
  10.1 1.0 copy-done.7
  11.1 1.6 collective-permute-start.4
  12.7 0.0 collective-permute-start.3
  12.7 1.5 collective-permute-start.5
  14.2 5.6 %project_queries.1 = (bf16[160,1024]{1,0:T(8,128)(2,1)}, bf16[160,1024]{1,0:T(8,128)(2,1)}) custom-call(bf16[1024,1280]{1,0:T(8,128)(2,1)} %refs_8_.7, s32[1,1024]{1,0:T(1,128)} %bitcast.37, bf16[1280]{0:T(1024)(128)(2,1)} %gain_ref.7, bf16[960,1280]{1,0:T(8,128)(2,1)} %bitcast.29), custom_call_target="tpu_custom_call" | custom-call | tf_op jit(solution)/shard_map/exchange_keys/project_queries/pallas_call | solution.py:166
  19.7 0.6 reduce-window.6
  20.3 0.2 slice_reduce_fusion
  20.6 0.1 stack.23.place
  20.7 0.1 fusion
  20.8 0.0 copy-start.2
  20.8 1.0 copy-done.2
  21.8 8.4 %attend_own.1 = (f32[2,2,96,512]{3,2,1,0:T(8,128)S(1)}, f32[2,2,512]{2,1,0:T(2,128)S(1)}) custom-call(s32[6]{0:T(128)S(1)} %stack.23.place, bf16[160,1024]{1,0:T(8,128)(2,1)S(1)} %copy-done.2, bf16[336,1024]{1,0:T(8,128)(2,1)S(1)} %copy-done.1, bf16[336,1024]{1,0:T(8,128)(2,1)S(1)} %copy-done.1), custom_call_target="tpu_custom_call" | custom-call | flops 1000000 | bytes 1000000 | tf_op jit(solution)/shard_map/exchange_keys/attend_own/pallas_call | solution.py:333
  30.2 0.5 collective-permute-done.5.refs_2_.refs_5_
  30.7 0.0 collective-permute-done.4.refs_6_
  30.7 0.0 collective-permute-start.9
  30.7 0.6 collective-permute-start.10
  31.3 0.2 collective-permute-start.8
  31.5 2.6 %collective-permute-start.7 = (bf16[336,1024]{1,0:T(8,128)(2,1)S(1)}, bf16[336,1024]{1,0:T(8,128)(2,1)S(1)}, u32[]{:S(2)}, u32[]{:S(2)}) collective-permute-start(bf16[336,1024]{1,0:T(8,128)(2,1)S(1)} %collective-permute-done.5.refs_2_.refs_5_), channel_id=1, source_target_pairs={{0,8},{1,9},{2,10},{3,11},{4,12},{5,13},{6,14},{7,15},{8,0},{9,1},... | collective-permute-start | bytes 2064392 | tf_op jit(solution)/shard_map/exchange_keys/ppermute | solution.py:39
  34.0 0.9 collective-permute-start
  34.9 8.9 %collective-permute-done.refs_0_ = bf16[160,1024]{1,0:T(8,128)(2,1)S(1)} collective-permute-done((bf16[160,1024]{1,0:T(8,128)(2,1)}, bf16[160,1024]{1,0:T(8,128)(2,1)S(1)}, u32[]{:S(2)}, u32[]{:S(2)}) %collective-permute-start) | collective-permute-done | bytes 327712 | tf_op jit(solution)/shard_map/exchange_keys/ppermute | solution.py:24
  43.8 28.0 %attend_near.1 = (f32[2,2,96,512]{3,2,1,0:T(8,128)S(1)}, f32[2,2,512]{2,1,0:T(2,128)S(1)}, f32[2,2,96,512]{3,2,1,0:T(8,128)S(1)}, f32[2,2,512]{2,1,0:T(2,128)S(1)}) custom-call(s32[6]{0:T(128)S(1)} %stack.23.place, bf16[160,1024]{1,0:T(8,128)(2,1)S(1)} %collective-permute-done.refs_0_, bf16[160,1024]{1,0:T(8,128)(2,1)S(1)} %copy-done.2, ...), custom_call_target="tpu_custom_call" | custom-call | flops 1000000 | bytes 1000000 | tf_op jit(solution)/shard_map/attention/attend_near/pallas_call | solution.py:333
  71.7 0.0 collective-permute-done.8.refs_5_
  71.8 0.0 collective-permute-done.9.refs_7_
  71.8 6.2 %attend_far.1 = (bf16[2,160,512]{2,1,0:T(8,128)(2,1)S(1)}, bf16[2,160,512]{2,1,0:T(8,128)(2,1)S(1)}) custom-call(s32[6]{0:T(128)S(1)} %stack.23.place, bf16[160,1024]{1,0:T(8,128)(2,1)S(1)} %collective-permute-done.refs_0_, bf16[160,1024]{1,0:T(8,128)(2,1)S(1)} %copy-done.2, bf16[336,1024]{1,0:T(8,128)(2,1)S(1)} %collective-permute-done.5.refs_2_.refs_5_, ...), custom_call_target="tpu_custom_call" | custom-call | flops 1000000 | bytes 1000000 | tf_op jit(solution)/shard_map/attention/attend_far/pallas_call | solution.py:333
  78.0 0.0 copy-start
  78.0 0.0 copy-start.3
  78.0 0.7 collective-permute-start.11
  78.7 1.5 collective-permute-start.14
  80.2 6.4 %load_mixer.1 = (bf16[1280,1280]{1,0:T(8,128)(2,1)S(1)}, bf16[2,1280,1280]{2,1,0:T(8,128)(2,1)S(1)}, bf16[2,1280,1280]{2,1,0:T(8,128)(2,1)S(1)}) custom-call(s32[6]{0:T(128)S(1)} %stack.23.place, bf16[2,160,1280]{2,1,0:T(8,128)(2,1)} %bitcast.35, bf16[2,160,1280]{2,1,0:T(8,128)(2,1)} %copy-done.7, bf16[2,160,1280]{2,1,0:T(8,128)(2,1)} %collective-permute-done.6.refs_2_, ...), custom_call_target="tpu_custom_call" | custom-call | bytes 16000000 | tf_op jit(solution)/shard_map/exchange_context/load_mixer/pallas_call | solution.py:104
  86.6 0.1 collective-permute-done.11.refs_1_
  86.7 1.5 collective-permute-start.15
  88.3 0.5 collective-permute-start.13
  88.8 0.0 collective-permute-done.14.refs_4_
  88.8 0.0 collective-permute-start.16
  88.8 5.8 %collective-permute-done.15.refs_5_ = bf16[2,160,512]{2,1,0:T(8,128)(2,1)S(1)} collective-permute-done((bf16[2,160,512]{2,1,0:T(8,128)(2,1)S(1)}, bf16[2,160,512]{2,1,0:T(8,128)(2,1)S(1)}, u32[]{:S(2)}, u32[]{:S(2)}) %collective-permute-start.15) | collective-permute-done | bytes 327712 | tf_op jit(solution)/shard_map/exchange_context/ppermute | solution.py:24
  94.6 0.0 collective-permute-done.16.refs_6_
  94.6 1.6 %collective-permute-done.17.refs_7_ = bf16[2,160,512]{2,1,0:T(8,128)(2,1)S(1)} collective-permute-done((bf16[2,160,512]{2,1,0:T(8,128)(2,1)S(1)}, bf16[2,160,512]{2,1,0:T(8,128)(2,1)S(1)}, u32[]{:S(2)}, u32[]{:S(2)}) %collective-permute-start.17) | collective-permute-done | bytes 327712 | tf_op jit(solution)/shard_map/exchange_context/ppermute | solution.py:24
  96.2 3.8 %mixer.4 = (bf16[128,1280]{1,0:T(8,128)(2,1)S(1)}, f32[128,1280]{1,0:T(8,128)S(1)}) custom-call(s32[6]{0:T(128)S(1)} %stack.23.place, bf16[2,160,512]{2,1,0:T(8,128)(2,1)S(1)} %get-tuple-element.95.refs_0_, bf16[2,160,512]{2,1,0:T(8,128)(2,1)S(1)} %collective-permute-done.11.refs_1_, bf16[2,160,512]{2,1,0:T(8,128)(2,1)S(1)} %collective-permute-done.12.refs_2_, ...), custom_call_target="tpu_custom_call" | custom-call | flops 5000000000 | bytes 20000000 | tf_op jit(solution)/shard_map/mixer/mixer/pallas_call | solution.py:384
  100.0 0.2 collective-permute-start.18
  100.2 1.4 collective-permute-start.21
  101.6 3.8 %mixer.7 = (bf16[128,1280]{1,0:T(8,128)(2,1)S(1)}, f32[128,1280]{1,0:T(8,128)S(1)}) custom-call(s32[6]{0:T(128)S(1)} %stack.23.place, bf16[2,160,512]{2,1,0:T(8,128)(2,1)S(1)} %get-tuple-element.95.refs_0_, bf16[2,160,512]{2,1,0:T(8,128)(2,1)S(1)} %collective-permute-done.11.refs_1_, bf16[2,160,512]{2,1,0:T(8,128)(2,1)S(1)} %collective-permute-done.12.refs_2_, ...), custom_call_target="tpu_custom_call" | custom-call | flops 5000000000 | bytes 20000000 | tf_op jit(solution)/shard_map/mixer/mixer/pallas_call | solution.py:384
  105.5 0.7 collective-permute-start.20
  106.1 4.0 %mixer.6 = (bf16[128,1280]{1,0:T(8,128)(2,1)S(1)}, f32[128,1280]{1,0:T(8,128)S(1)}) custom-call(s32[6]{0:T(128)S(1)} %stack.23.place, bf16[2,160,512]{2,1,0:T(8,128)(2,1)S(1)} %get-tuple-element.95.refs_0_, bf16[2,160,512]{2,1,0:T(8,128)(2,1)S(1)} %collective-permute-done.11.refs_1_, bf16[2,160,512]{2,1,0:T(8,128)(2,1)S(1)} %collective-permute-done.12.refs_2_, ...), custom_call_target="tpu_custom_call" | custom-call | flops 5000000000 | bytes 20000000 | tf_op jit(solution)/shard_map/mixer/mixer/pallas_call | solution.py:384
  110.2 1.5 collective-permute-start.19
  111.7 3.8 %mixer.5 = (bf16[128,1280]{1,0:T(8,128)(2,1)S(1)}, f32[128,1280]{1,0:T(8,128)S(1)}) custom-call(s32[6]{0:T(128)S(1)} %stack.23.place, bf16[2,160,512]{2,1,0:T(8,128)(2,1)S(1)} %get-tuple-element.95.refs_0_, bf16[2,160,512]{2,1,0:T(8,128)(2,1)S(1)} %collective-permute-done.11.refs_1_, bf16[2,160,512]{2,1,0:T(8,128)(2,1)S(1)} %collective-permute-done.12.refs_2_, ...), custom_call_target="tpu_custom_call" | custom-call | flops 5000000000 | bytes 20000000 | tf_op jit(solution)/shard_map/mixer/mixer/pallas_call | solution.py:384
  115.5 0.0 copy-start.4
  115.5 0.7 collective-permute-start.22
  116.2 2.9 %load_merge.1.weights = bf16[640,5120]{1,0:T(8,128)(2,1)S(1)} custom-call(bf16[320,5120]{1,0:T(8,128)(2,1)} %bitcast.30, bf16[320,5120]{1,0:T(8,128)(2,1)} %collective-permute-done.18.other), custom_call_target="tpu_custom_call" | custom-call | bytes 8000000 | tf_op jit(solution)/shard_map/merge/load_merge/pallas_call | solution.py:129
  119.1 1.6 %gather.3.refs_0_ = bf16[4,256,1280]{2,1,0:T(8,128)(2,1)S(1)} custom-call(s32[6]{0:T(128)S(1)} %stack.23.place, s32[4,256]{1,0:T(4,128)S(1)} %subtract_bitcast_fusion.index_ref, f32[128,1280]{1,0:T(8,128)S(1)} %get-tuple-element.120.kept, bf16[128,1280]{1,0:T(8,128)(2,1)S(1)} %collective-permute-done.21.received, bf16[1280]{0:T(1024)(128)(2,1)S(1)} %copy-done.4), custom_call_target="tpu_custom_call" | custom-call | flops 1000000000 | bytes 5000000 | tf_op jit(solution)/shard_map/merge/gather/pallas_call | solution.py:425
  120.8 1.6 %gather.4.refs_0_ = bf16[4,256,1280]{2,1,0:T(8,128)(2,1)S(1)} custom-call(s32[6]{0:T(128)S(1)} %stack.23.place, s32[4,256]{1,0:T(4,128)S(1)} %subtract_bitcast_fusion.index_ref, f32[128,1280]{1,0:T(8,128)S(1)} %get-tuple-element.118.kept, bf16[128,1280]{1,0:T(8,128)(2,1)S(1)} %collective-permute-done.20.received, bf16[1280]{0:T(1024)(128)(2,1)S(1)} %copy-done.4, ...), custom_call_target="tpu_custom_call" | custom-call | flops 1000000000 | bytes 5000000 | tf_op jit(solution)/shard_map/merge/gather/pallas_call | solution.py:425
  122.4 2.4 %collective-permute-done.19.received = bf16[128,1280]{1,0:T(8,128)(2,1)S(1)} collective-permute-done((bf16[128,1280]{1,0:T(8,128)(2,1)S(1)}, bf16[128,1280]{1,0:T(8,128)(2,1)S(1)}, u32[]{:S(2)}, u32[]{:S(2)}) %collective-permute-start.19) | collective-permute-done | bytes 327712 | tf_op jit(solution)/shard_map/mixer/ppermute | solution.py:24
  124.8 1.6 %gather.5.earlier = bf16[4,256,1280]{2,1,0:T(8,128)(2,1)S(1)} custom-call(s32[6]{0:T(128)S(1)} %stack.23.place, s32[4,256]{1,0:T(4,128)S(1)} %subtract_bitcast_fusion.index_ref, f32[128,1280]{1,0:T(8,128)S(1)} %get-tuple-element.116.kept, bf16[128,1280]{1,0:T(8,128)(2,1)S(1)} %collective-permute-done.19.received, bf16[1280]{0:T(1024)(128)(2,1)S(1)} %copy-done.4, ...), custom_call_target="tpu_custom_call" | custom-call | flops 1000000000 | bytes 5000000 | tf_op jit(solution)/shard_map/merge/gather/pallas_call | solution.py:425
  126.4 4.9 %collective-permute-done.22.received = bf16[128,1280]{1,0:T(8,128)(2,1)S(1)} collective-permute-done((bf16[128,1280]{1,0:T(8,128)(2,1)S(1)}, bf16[128,1280]{1,0:T(8,128)(2,1)S(1)}, u32[]{:S(2)}, u32[]{:S(2)}) %collective-permute-start.22) | collective-permute-done | bytes 327712 | tf_op jit(solution)/shard_map/mixer/ppermute | solution.py:24
  131.3 3.8 %merge.1 = (f32[256,320]{1,0:T(8,128)S(1)}, f32[256,320]{1,0:T(8,128)S(1)}) custom-call(s32[6]{0:T(128)S(1)} %stack.23.place, s32[4,256]{1,0:T(4,128)S(1)} %subtract_bitcast_fusion.index_ref, f32[128,1280]{1,0:T(8,128)S(1)} %get-tuple-element.123.kept, bf16[128,1280]{1,0:T(8,128)(2,1)S(1)} %collective-permute-done.22.received, ...), custom_call_target="tpu_custom_call" | custom-call | flops 3000000000 | bytes 12000000 | tf_op jit(solution)/shard_map/merge/merge/pallas_call | solution.py:456
  135.1 0.1 collective-permute-start.23
  135.2 1.7 %collective-permute-done.23.received = f32[256,320]{1,0:T(8,128)S(1)} collective-permute-done((f32[256,320]{1,0:T(8,128)S(1)}, f32[256,320]{1,0:T(8,128)S(1)}, u32[]{:S(2)}, u32[]{:S(2)}) %collective-permute-start.23) | collective-permute-done | bytes 327712 | tf_op jit(solution)/shard_map/merge/ppermute | solution.py:24
  136.9 0.3 place.1
  137.2 20.4 %all_to_all.5 = bf16[8,64,320]{2,1,0:T(8,128)(2,1)S(1)} all-to-all(bf16[8,64,320]{2,1,0:T(8,128)(2,1)S(1)} %bitcast.26), channel_id=1, replica_groups=mesh['req'=8,'tp'=4] {'req'}, dimensions={0} | all-to-all | bytes 655360 | tf_op jit(solution)/shard_map/place/all_to_all | solution.py:609
  157.6 0.7 copy.14
  (33 shorter events, 0.1 us)
Async XLA Ops:
  0.0 10.1 %collective-permute-start.1 = (bf16[1280,1280]{1,0:T(8,128)(2,1)}, bf16[1280,1280]{1,0:T(8,128)(2,1)}, u32[]{:S(2)}, u32[]{:S(2)}) collective-permute-start(bf16[1280,1280]{1,0:T(8,128)(2,1)} %refs_4_.1), channel_id=1, source_target_pairs={{0,1},{1,0},{2,3},{3,2},{4,5},{5,4},{6,7},{7,6},{8,9},{9,8},{10,11... | collective-permute-start | bytes 9830408 | tf_op jit(solution)/shard_map/weights/ppermute | solution.py:24
  0.5 9.6 %collective-permute-start.2 = (bf16[2,160,1280]{2,1,0:T(8,128)(2,1)}, bf16[2,160,1280]{2,1,0:T(8,128)(2,1)S(1)}, u32[]{:S(2)}, u32[]{:S(2)}) collective-permute-start(bf16[2,160,1280]{2,1,0:T(8,128)(2,1)} %bitcast.33), channel_id=1, source_target_pairs={{0,1},{1,0},{2,3},{3,2},{4,5},{5,4},{6,7},{7,6},{8,9},{9,8},{10,11... | collective-permute-start | bytes 2457608 | tf_op jit(solution)/shard_map/weights/ppermute | solution.py:24
  0.5 29.7 %collective-permute-start.6 = (bf16[2,160,1280]{2,1,0:T(8,128)(2,1)}, bf16[2,160,1280]{2,1,0:T(8,128)(2,1)}, u32[]{:S(2)}, u32[]{:S(2)}) collective-permute-start(bf16[2,160,1280]{2,1,0:T(8,128)(2,1)} %bitcast.34), channel_id=1, source_target_pairs={{0,2},{1,3},{2,0},{3,1},{4,6},{5,7},{6,4},{7,5},{8,10},{9,11},{10,... | collective-permute-start | bytes 2457608 | tf_op jit(solution)/shard_map/exchange_keys/ppermute | solution.py:24
  3.5 10.7 %copy-start.9 = (s32[256,1]{0,1:T(1,128)S(1)}, s32[256,1]{0,1:T(1,128)}, u32[]{:S(2)}) copy-start(s32[256,1]{0,1:T(1,128)} %param.23) | copy-start | bytes 3076
  10.1 10.7 %copy-start.10 = (s32[256,4]{0,1:T(4,128)S(1)}, s32[256,4]{0,1:T(4,128)}, u32[]{:S(2)}) copy-start(s32[256,4]{0,1:T(4,128)} %param.22) | copy-start | bytes 12292
  10.1 10.7 %copy-start.1 = (bf16[336,1024]{1,0:T(8,128)(2,1)S(1)}, bf16[336,1024]{1,0:T(8,128)(2,1)}, u32[]{:S(2)}) copy-start(bf16[336,1024]{1,0:T(8,128)(2,1)} %get-tuple-element.71.refs_1_.refs_2_.refs_3_.refs_4_) | copy-start | bytes 2064388
  10.1 1.0 copy-start.7
  11.1 19.6 %collective-permute-start.4 = (bf16[336,1024]{1,0:T(8,128)(2,1)}, bf16[336,1024]{1,0:T(8,128)(2,1)S(1)}, u32[]{:S(2)}, u32[]{:S(2)}) collective-permute-start(bf16[336,1024]{1,0:T(8,128)(2,1)} %get-tuple-element.71.refs_1_.refs_2_.refs_3_.refs_4_), channel_id=1, source_target_pairs={{0,8},{1,9},{2,10},{3,11},{4,12},{5,13},{6,14},{7,15},{8,0},{9,1},... | collective-permute-start | bytes 2064392 | tf_op jit(solution)/shard_map/exchange_keys/ppermute | solution.py:39
  12.7 18.1 %collective-permute-start.3 = (bf16[336,1024]{1,0:T(8,128)(2,1)}, bf16[336,1024]{1,0:T(8,128)(2,1)S(1)}, u32[]{:S(2)}, u32[]{:S(2)}) collective-permute-start(bf16[336,1024]{1,0:T(8,128)(2,1)} %get-tuple-element.71.refs_1_.refs_2_.refs_3_.refs_4_), channel_id=1, source_target_pairs={{0,1},{1,0},{2,3},{3,2},{4,5},{5,4},{6,7},{7,6},{8,16},{9,17},{10,... | collective-permute-start | bytes 2064392 | tf_op jit(solution)/shard_map/exchange_keys/ppermute | solution.py:39
  12.7 18.1 %collective-permute-start.5 = (bf16[336,1024]{1,0:T(8,128)(2,1)}, bf16[336,1024]{1,0:T(8,128)(2,1)S(1)}, u32[]{:S(2)}, u32[]{:S(2)}) collective-permute-start(bf16[336,1024]{1,0:T(8,128)(2,1)} %get-tuple-element.72), channel_id=1, source_target_pairs={{0,4},{4,0},{8,12},{12,8},{16,20},{20,16},{24,28},{28,24},{1,5},{5... | collective-permute-start | bytes 2064392 | tf_op jit(solution)/shard_map/exchange_keys/ppermute | solution.py:24
  20.8 1.0 copy-start.2
  30.7 41.1 %collective-permute-start.9 = (bf16[1280,1280]{1,0:T(8,128)(2,1)}, bf16[1280,1280]{1,0:T(8,128)(2,1)S(1)}, u32[]{:S(2)}, u32[]{:S(2)}) collective-permute-start(bf16[1280,1280]{1,0:T(8,128)(2,1)} %refs_6_.1), channel_id=1, source_target_pairs={{0,1},{1,0},{2,3},{3,2},{4,5},{5,4},{6,7},{7,6},{8,9},{9,8},{10,11... | collective-permute-start | bytes 9830408 | tf_op jit(solution)/shard_map/exchange_keys/ppermute | solution.py:24
  30.7 41.0 %collective-permute-start.10 = (bf16[2,160,1280]{2,1,0:T(8,128)(2,1)}, bf16[2,160,1280]{2,1,0:T(8,128)(2,1)S(1)}, u32[]{:S(2)}, u32[]{:S(2)}) collective-permute-start(bf16[2,160,1280]{2,1,0:T(8,128)(2,1)} %copy-done.7), channel_id=1, source_target_pairs={{0,2},{1,3},{2,0},{3,1},{4,6},{5,7},{6,4},{7,5},{8,10},{9,11},{10,... | collective-permute-start | bytes 2457608 | tf_op jit(solution)/shard_map/exchange_keys/ppermute | solution.py:24
  31.3 40.4 %collective-permute-start.8 = (bf16[336,1024]{1,0:T(8,128)(2,1)S(1)}, bf16[336,1024]{1,0:T(8,128)(2,1)S(1)}, u32[]{:S(2)}, u32[]{:S(2)}) collective-permute-start(bf16[336,1024]{1,0:T(8,128)(2,1)S(1)} %collective-permute-done.5.refs_2_.refs_5_), channel_id=1, source_target_pairs={{0,1},{1,0},{2,3},{3,2},{4,5},{5,4},{6,7},{7,6},{8,16},{9,17},{10,... | collective-permute-start | bytes 2064392 | tf_op jit(solution)/shard_map/exchange_keys/ppermute | solution.py:39
  31.5 40.3 %collective-permute-start.7 = (bf16[336,1024]{1,0:T(8,128)(2,1)S(1)}, bf16[336,1024]{1,0:T(8,128)(2,1)S(1)}, u32[]{:S(2)}, u32[]{:S(2)}) collective-permute-start(bf16[336,1024]{1,0:T(8,128)(2,1)S(1)} %collective-permute-done.5.refs_2_.refs_5_), channel_id=1, source_target_pairs={{0,8},{1,9},{2,10},{3,11},{4,12},{5,13},{6,14},{7,15},{8,0},{9,1},... | collective-permute-start | bytes 2064392 | tf_op jit(solution)/shard_map/exchange_keys/ppermute | solution.py:39
  34.0 9.7 %collective-permute-start = (bf16[160,1024]{1,0:T(8,128)(2,1)}, bf16[160,1024]{1,0:T(8,128)(2,1)S(1)}, u32[]{:S(2)}, u32[]{:S(2)}) collective-permute-start(bf16[160,1024]{1,0:T(8,128)(2,1)} %get-tuple-element.67), channel_id=1, source_target_pairs={{0,4},{4,0},{8,12},{12,8},{16,20},{20,16},{24,28},{28,24},{1,5},{5... | collective-permute-start | bytes 983048 | tf_op jit(solution)/shard_map/exchange_keys/ppermute | solution.py:24
  71.8 8.4 %copy-start.8 = (bf16[2,160,1280]{2,1,0:T(8,128)(2,1)}, bf16[2,160,1280]{2,1,0:T(8,128)(2,1)S(1)}, u32[]{:S(2)}) copy-start(bf16[2,160,1280]{2,1,0:T(8,128)(2,1)S(1)} %collective-permute-done.10.refs_3_) | copy-start | bytes 2457604
  71.8 8.4 %copy-start.6 = (bf16[1280,1280]{1,0:T(8,128)(2,1)}, bf16[1280,1280]{1,0:T(8,128)(2,1)S(1)}, u32[]{:S(2)}) copy-start(bf16[1280,1280]{1,0:T(8,128)(2,1)S(1)} %collective-permute-done.9.refs_7_) | copy-start | bytes 9830404
  78.0 18.2 %copy-start = (bf16[1024,1280]{1,0:T(8,128)(2,1)S(1)}, bf16[1024,1280]{1,0:T(8,128)(2,1)}, u32[]{:S(2)}) copy-start(bf16[1024,1280]{1,0:T(8,128)(2,1)} %refs_8_.7) | copy-start | bytes 7864324
  78.0 18.2 %copy-start.3 = (bf16[1280]{0:T(1024)(128)(2,1)S(1)}, bf16[1280]{0:T(1024)(128)(2,1)}, u32[]{:S(2)}) copy-start(bf16[1280]{0:T(1024)(128)(2,1)} %refs_9_.7) | copy-start | bytes 7684
  78.0 8.7 %collective-permute-start.11 = (bf16[2,160,512]{2,1,0:T(8,128)(2,1)S(1)}, bf16[2,160,512]{2,1,0:T(8,128)(2,1)S(1)}, u32[]{:S(2)}, u32[]{:S(2)}) collective-permute-start(bf16[2,160,512]{2,1,0:T(8,128)(2,1)S(1)} %get-tuple-element.96), channel_id=1, source_target_pairs={{0,4},{4,0},{8,12},{12,8},{16,20},{20,16},{24,28},{28,24},{1,5},{5... | collective-permute-start | bytes 983048 | tf_op jit(solution)/shard_map/exchange_context/ppermute | solution.py:24
  78.7 10.1 %collective-permute-start.14 = (bf16[2,160,512]{2,1,0:T(8,128)(2,1)S(1)}, bf16[2,160,512]{2,1,0:T(8,128)(2,1)S(1)}, u32[]{:S(2)}, u32[]{:S(2)}) collective-permute-start(bf16[2,160,512]{2,1,0:T(8,128)(2,1)S(1)} %get-tuple-element.95.refs_0_), channel_id=1, source_target_pairs={{0,2},{1,3},{2,0},{3,1},{4,6},{5,7},{6,4},{7,5},{8,10},{9,11},{10,... | collective-permute-start | bytes 983048 | tf_op jit(solution)/shard_map/exchange_context/ppermute | solution.py:24
  86.7 13.3 %copy-start.5 = (bf16[5120,320]{0,1:T(8,128)(2,1)S(1)}, bf16[5120,320]{0,1:T(8,128)(2,1)}, u32[]{:S(2)}) copy-start(bf16[5120,320]{0,1:T(8,128)(2,1)} %param.21) | copy-start | bytes 9830404
  86.7 7.8 %collective-permute-start.15 = (bf16[2,160,512]{2,1,0:T(8,128)(2,1)S(1)}, bf16[2,160,512]{2,1,0:T(8,128)(2,1)S(1)}, u32[]{:S(2)}, u32[]{:S(2)}) collective-permute-start(bf16[2,160,512]{2,1,0:T(8,128)(2,1)S(1)} %collective-permute-done.11.refs_1_), channel_id=1, source_target_pairs={{0,2},{1,3},{2,0},{3,1},{4,6},{5,7},{6,4},{7,5},{8,10},{9,11},{10,... | collective-permute-start | bytes 983048 | tf_op jit(solution)/shard_map/exchange_context/ppermute | solution.py:24
  88.3 6.3 %collective-permute-start.12 = (bf16[2,160,512]{2,1,0:T(8,128)(2,1)S(1)}, bf16[2,160,512]{2,1,0:T(8,128)(2,1)S(1)}, u32[]{:S(2)}, u32[]{:S(2)}) collective-permute-start(bf16[2,160,512]{2,1,0:T(8,128)(2,1)S(1)} %get-tuple-element.95.refs_0_), channel_id=1, source_target_pairs={{0,1},{1,0},{2,3},{3,2},{4,5},{5,4},{6,7},{7,6},{8,9},{9,8},{10,11... | collective-permute-start | bytes 983048 | tf_op jit(solution)/shard_map/exchange_context/ppermute | solution.py:24
  88.3 6.3 %collective-permute-start.13 = (bf16[2,160,512]{2,1,0:T(8,128)(2,1)S(1)}, bf16[2,160,512]{2,1,0:T(8,128)(2,1)S(1)}, u32[]{:S(2)}, u32[]{:S(2)}) collective-permute-start(bf16[2,160,512]{2,1,0:T(8,128)(2,1)S(1)} %collective-permute-done.11.refs_1_), channel_id=1, source_target_pairs={{0,1},{1,0},{2,3},{3,2},{4,5},{5,4},{6,7},{7,6},{8,9},{9,8},{10,11... | collective-permute-start | bytes 983048 | tf_op jit(solution)/shard_map/exchange_context/ppermute | solution.py:24
  88.8 5.8 %collective-permute-start.16 = (bf16[2,160,512]{2,1,0:T(8,128)(2,1)S(1)}, bf16[2,160,512]{2,1,0:T(8,128)(2,1)S(1)}, u32[]{:S(2)}, u32[]{:S(2)}) collective-permute-start(bf16[2,160,512]{2,1,0:T(8,128)(2,1)S(1)} %collective-permute-done.14.refs_4_), channel_id=1, source_target_pairs={{0,1},{1,0},{2,3},{3,2},{4,5},{5,4},{6,7},{7,6},{8,9},{9,8},{10,11... | collective-permute-start | bytes 983048 | tf_op jit(solution)/shard_map/exchange_context/ppermute | solution.py:24
  94.5 1.6 %collective-permute-start.17 = (bf16[2,160,512]{2,1,0:T(8,128)(2,1)S(1)}, bf16[2,160,512]{2,1,0:T(8,128)(2,1)S(1)}, u32[]{:S(2)}, u32[]{:S(2)}) collective-permute-start(bf16[2,160,512]{2,1,0:T(8,128)(2,1)S(1)} %collective-permute-done.15.refs_5_), channel_id=1, source_target_pairs={{0,1},{1,0},{2,3},{3,2},{4,5},{5,4},{6,7},{7,6},{8,9},{9,8},{10,11... | collective-permute-start | bytes 983048 | tf_op jit(solution)/shard_map/exchange_context/ppermute | solution.py:24
  100.0 16.2 %collective-permute-start.18 = (bf16[320,5120]{1,0:T(8,128)(2,1)S(1)}, bf16[320,5120]{1,0:T(8,128)(2,1)}, u32[]{:S(2)}, u32[]{:S(2)}) collective-permute-start(bf16[320,5120]{1,0:T(8,128)(2,1)S(1)} %bitcast.31), channel_id=1, source_target_pairs={{0,1},{1,0},{2,3},{3,2},{4,5},{5,4},{6,7},{7,6},{8,9},{9,8},{10,11... | collective-permute-start | bytes 9830408 | tf_op jit(solution)/shard_map/mixer/ppermute | solution.py:24
  100.2 18.9 %collective-permute-start.21 = (bf16[128,1280]{1,0:T(8,128)(2,1)S(1)}, bf16[128,1280]{1,0:T(8,128)(2,1)S(1)}, u32[]{:S(2)}, u32[]{:S(2)}) collective-permute-start(bf16[128,1280]{1,0:T(8,128)(2,1)S(1)} %get-tuple-element.109), channel_id=1, source_target_pairs={{0,2},{1,3},{2,0},{3,1},{4,6},{5,7},{6,4},{7,5},{8,10},{9,11},{10,... | collective-permute-start | bytes 983048 | tf_op jit(solution)/shard_map/mixer/ppermute | solution.py:24
  105.5 15.3 %collective-permute-start.20 = (bf16[128,1280]{1,0:T(8,128)(2,1)S(1)}, bf16[128,1280]{1,0:T(8,128)(2,1)S(1)}, u32[]{:S(2)}, u32[]{:S(2)}) collective-permute-start(bf16[128,1280]{1,0:T(8,128)(2,1)S(1)} %get-tuple-element.119), channel_id=1, source_target_pairs={{0,2},{1,3},{2,0},{3,1},{4,6},{5,7},{6,4},{7,5},{8,10},{9,11},{10,... | collective-permute-start | bytes 983048 | tf_op jit(solution)/shard_map/mixer/ppermute | solution.py:24
  110.2 14.6 %collective-permute-start.19 = (bf16[128,1280]{1,0:T(8,128)(2,1)S(1)}, bf16[128,1280]{1,0:T(8,128)(2,1)S(1)}, u32[]{:S(2)}, u32[]{:S(2)}) collective-permute-start(bf16[128,1280]{1,0:T(8,128)(2,1)S(1)} %get-tuple-element.117), channel_id=1, source_target_pairs={{0,2},{1,3},{2,0},{3,1},{4,6},{5,7},{6,4},{7,5},{8,10},{9,11},{10,... | collective-permute-start | bytes 983048 | tf_op jit(solution)/shard_map/mixer/ppermute | solution.py:24
  115.5 3.7 %copy-start.4 = (bf16[1280]{0:T(1024)(128)(2,1)S(1)}, bf16[1280]{0:T(1024)(128)(2,1)}, u32[]{:S(2)}) copy-start(bf16[1280]{0:T(1024)(128)(2,1)} %gain_ref.11) | copy-start | bytes 7684
  115.5 15.8 %collective-permute-start.22 = (bf16[128,1280]{1,0:T(8,128)(2,1)S(1)}, bf16[128,1280]{1,0:T(8,128)(2,1)S(1)}, u32[]{:S(2)}, u32[]{:S(2)}) collective-permute-start(bf16[128,1280]{1,0:T(8,128)(2,1)S(1)} %get-tuple-element.113), channel_id=1, source_target_pairs={{0,2},{1,3},{2,0},{3,1},{4,6},{5,7},{6,4},{7,5},{8,10},{9,11},{10,... | collective-permute-start | bytes 983048 | tf_op jit(solution)/shard_map/mixer/ppermute | solution.py:24
  135.1 1.8 %collective-permute-start.23 = (f32[256,320]{1,0:T(8,128)S(1)}, f32[256,320]{1,0:T(8,128)S(1)}, u32[]{:S(2)}, u32[]{:S(2)}) collective-permute-start(f32[256,320]{1,0:T(8,128)S(1)} %get-tuple-element.128), channel_id=1, source_target_pairs={{0,1},{1,0},{2,3},{3,2},{4,5},{5,4},{6,7},{7,6},{8,9},{9,8},{10,11... | collective-permute-start | bytes 983048 | tf_op jit(solution)/shard_map/merge/ppermute | solution.py:24
